TPU v7x, 32 devices: a whole 2x2x4 slice. The times are simulated.
32 devices in a mesh: groups: 2 (over y), dp: 4 (over z), mp: 2 (over x), layer: 2 (over core).
Axes of the slice: x: 2, y: 2, z: 4, core: 2. Of those that a mesh axis runs over, the one named last changes fastest.
Arguments:
- acts: bfloat16 [2, 4096, 8192], P('layer', ('groups', 'dp'), 'mp'), parts along dimension 1, may hold values from -6 to 6
- grads: bfloat16 [2, 4096, 28672], P('layer', ('groups', 'dp'), 'mp'), parts along dimension 1, may hold values from -6 to 6
- query_left: bfloat16 [2, 8192, 512], P('layer', ('mp', 'dp'), 'groups'), parts along dimension 2, may hold values from -0.0625 to 0.0625
- query_right: bfloat16 [2, 28672, 512], P('layer', ('mp', 'dp'), 'groups'), parts along dimension 2, may hold values from -0.03125 to 0.03125
- seq_len: int32 [16], P(('groups', 'dp')), parts along dimension 0, may hold values from 1 to 256, 1024 in all
Outputs:
- scores: float32 [2, 16, 32], P('layer', ('groups', 'dp')), parts along dimension 1
There are 2 independent parts, one for each index of `groups`. A program takes and returns all parts, laid end to end along the dimension named above; each array names one. Nothing has to cross between parts.
Inputs may be any that keep to these rules, and one draw needn't show every extreme that they name: `seq_len`: every sequence has at least one live token and some sequence has exactly 256.
All inputs are finite; a program needn't handle non-finite values. No bound on the sum of `seq_len` on one device may be relied on, other than what follows from the above.
Results may differ from a plain program's by a relative error of at most 0.0003.
Values may be sent and summed in bfloat16 or wider, within the bound.
No kernel may reach another device: no remote copies, remote signals or barrier semaphores. Data moves between devices by JAX's collectives and lax.ppermute only.
A program may use at most 64 MiB of HBM per device.

v0:
```python
import math

import jax
import jax.numpy as jnp
from jax import lax
from jax.sharding import PartitionSpec as P

RANK = 8
LEN = 256

TRADE = [(0, 1), (1, 0), (2, 3), (3, 2)]
TO_END = [(1, 0), (2, 3)]
ACROSS = [(1, 2), (2, 1)]
TO_MIDDLE = [(0, 1), (3, 2)]


def live_rows(seq_len, row_count):
    seq_count = seq_len.shape[0]
    seq_span = row_count // seq_count
    positions = lax.broadcasted_iota(jnp.int32, (seq_count, seq_span, 1), 1)
    live = (positions < seq_len[:, None, None]).astype(jnp.float32)
    return live.reshape(row_count, 1)


def column_scores(masked_acts, proj_grads, seq_count):
    product = masked_acts * proj_grads
    return jnp.sum(product.reshape(seq_count, -1, product.shape[1]), axis=1)


def rank_scores(columns):
    seq_count = columns.shape[0]
    return jnp.sum(columns.reshape(seq_count, -1, RANK), axis=2)


def dot(a, b):
    return jnp.dot(a, b, preferred_element_type=jnp.float32)


def on_any(acts, grads, left, right, seq_len):
    seq_count = seq_len.shape[0]
    live = live_rows(seq_len, acts.shape[0])
    proj_acts = dot(acts, lax.all_gather(left, "dp", axis=0, tiled=True))
    proj_grads = dot(grads, lax.all_gather(right, "dp", axis=0, tiled=True))
    masked = lax.psum(proj_acts, "mp") * live
    scores = rank_scores(column_scores(masked, proj_grads, seq_count))
    return lax.psum(scores, "mp") / math.sqrt(RANK * LEN)


def after(value, *arrived):
    return lax.optimization_barrier((value, *arrived))[0]


class Sender:
    def __init__(self, pairs):
        self.pairs = pairs
        self.came = []

    def ready(self, value, *arrived):
        return after(value, *self.came[-2:-1], *arrived)

    def __call__(self, x, pairs=None):
        self.came.append(lax.ppermute(x, "dp", pairs or self.pairs))
        return self.came[-1]


def on_line(acts, grads, left, right, seq_len):
    seq_count = seq_len.shape[0]
    row_count = acts.shape[0]
    place = lax.axis_index("dp")
    is_end = (place == 0) | (place == 3)
    near = place ^ 1
    far_middle = jnp.where(place < 2, 2, 1)
    far_end = jnp.where(place < 2, 3, 0)

    unit = left.shape[0]
    depth = right.shape[0]
    half = unit // 2
    spans = {"B": (0, unit), "C1": (unit, 2 * unit), "C2": (2 * unit, 3 * unit), "C3": (3 * unit, depth)}
    trade = Sender(TRADE)
    across = Sender(ACROSS)

    def columns(array, source, start, stop):
        span = array.shape[1] // 4
        return lax.dynamic_slice_in_dim(array, source * span + start, stop - start, axis=1)

    def own(name, sender):
        start, stop = spans[name]
        return sender.ready(right)[start:stop]

    def guest(index, sender):
        source = sender.ready(grads)
        start = unit + index * half
        middle = start + half // 2
        blocks = [columns(source, near, start, middle), columns(source, near, middle, start + half)]
        return jnp.concatenate(blocks, axis=0)

    def either(at_end, at_middle):
        return jnp.where(is_end, at_end, at_middle)

    x, y = {}, {}
    x["A"] = trade(left)
    y["AM"] = across(left)
    first = right[:unit]
    x["B"] = trade(first)
    y["BM"] = across(first)
    y["AE"] = across(across.ready(x["A"]))
    x["AM"] = trade(either(own("C1", trade), y["AM"]))
    y["C1M"] = across(own("C1", across))
    x["BM"] = trade(either(own("C2", trade), y["BM"]))
    y["C2M"] = across(own("C2", across))
    x["AE"] = trade(either(guest(0, trade), y["AE"]))
    y["C3M"] = across(own("C3", across))
    x["C1M"] = trade(either(guest(1, trade), y["C1M"]))
    y["BE"] = across(across.ready(x["B"]))
    x["C2M"] = trade(either(guest(2, trade), y["C2M"]))
    y["C1E"] = across(across.ready(x["AM"]))
    x["C3M"] = trade(either(own("C3", trade), y["C3M"]))
    y["C2E"] = across(across.ready(x["BM"]))
    x["BE"] = trade(either(guest(3, trade), y["BE"]))
    y["C3E"] = across(across.ready(x["C3M"], x["BE"]))
    x["C1E"] = trade(either(guest(4, trade), y["C1E"]))
    x["C2E"] = trade(trade.ready(y["C2E"]), TO_END)
    x["C3E"] = trade(trade.ready(y["C3E"]), TO_END)

    proj_acts = dot(columns(after(acts, x["A"], y["AM"]), place, 0, unit), left)
    proj_acts += dot(columns(acts, near, 0, unit), x["A"])
    proj_acts += dot(columns(acts, far_middle, 0, unit), either(x["AM"], y["AM"]))
    proj_acts += dot(columns(acts, far_end, 0, unit), either(x["AE"], y["AE"]))
    other_acts = lax.ppermute(proj_acts, "mp", [(0, 1), (1, 0)])
    masked = after((proj_acts + other_acts) * live_rows(seq_len, row_count))
    guest_acts = lax.ppermute(masked, "dp", TO_MIDDLE)

    def near_term(name, got):
        if name != "B":
            got = either(jnp.zeros_like(got), got)
        return dot(columns(grads, near, *spans[name]), got)

    def middle_term(name):
        return dot(columns(grads, far_middle, *spans[name]), either(x[name + "M"], y[name + "M"]))

    def end_term(name):
        return dot(columns(grads, far_end, *spans[name]), either(x[name + "E"], y[name + "E"]))

    def guest_term(index, got):
        start = unit + index * half
        terms = []
        for block in (0, 1):
            rows = got[block * row_count : (block + 1) * row_count]
            begin = start + block * (half // 2)
            terms.append(dot(rows, right[begin : begin + half // 2]))
        return terms[0] + terms[1]

    proj_grads = dot(columns(after(grads, x["B"], y["BM"]), place, 0, depth), right)
    proj_grads += near_term("B", x["B"])
    proj_grads = after(proj_grads)
    proj_grads += near_term("C1", x["AM"])
    proj_grads += middle_term("B")
    proj_grads += near_term("C2", x["BM"])
    proj_grads = after(proj_grads)
    guest_grads = guest_term(0, x["AE"])
    proj_grads += middle_term("C1")
    guest_grads += guest_term(1, x["C1M"])
    proj_grads, guest_grads = lax.optimization_barrier((proj_grads, guest_grads))
    proj_grads += middle_term("C2")
    guest_grads += guest_term(2, x["C2M"])
    proj_grads += middle_term("C3")
    proj_grads += near_term("C3", x["C3M"])
    proj_grads, guest_grads, masked = lax.optimization_barrier((proj_grads, guest_grads, masked))
    proj_grads += end_term("B")
    guest_grads += guest_term(3, x["BE"])
    proj_grads, guest_grads = lax.optimization_barrier((proj_grads, guest_grads))
    proj_grads += end_term("C1")
    guest_grads += guest_term(4, x["C1E"])
    guest_scores = lax.ppermute(column_scores(guest_acts, guest_grads, seq_count), "dp", TO_END)

    proj_grads = after(proj_grads)
    proj_grads = after(proj_grads + end_term("C2"), guest_scores)
    proj_grads += end_term("C3")
    scores = rank_scores(column_scores(masked, proj_grads, seq_count) + guest_scores)
    other_scores = lax.ppermute(scores, "mp", [(0, 1), (1, 0)])
    return (scores + other_scores) / math.sqrt(RANK * LEN)


def suits_line(mesh, acts, left, right):
    unit = left.shape[0]
    fits = right.shape[0] * 2 == unit * 7 and acts.shape[0] * 2 == unit and left.shape[1] * 4 == unit
    return mesh.shape["dp"] == 4 and mesh.shape["mp"] == 2 and fits


def solution(mesh):
    def on_device(acts, grads, query_left, query_right, seq_len):
        body = on_line if suits_line(mesh, acts[0], query_left[0], query_right[0]) else on_any
        return body(acts[0], grads[0], query_left[0], query_right[0], seq_len)[None]

    return jax.shard_map(
        on_device,
        mesh=mesh,
        in_specs=(
            P("layer", ("groups", "dp"), "mp"),
            P("layer", ("groups", "dp"), "mp"),
            P("layer", ("mp", "dp"), "groups"),
            P("layer", ("mp", "dp"), "groups"),
            P(("groups", "dp")),
        ),
        out_specs=P("layer", ("groups", "dp"), None),
        check_vma=False,
    )
```

profile of v0, /device:TPU:0, one launch (start us, length us, event | category | flops | bytes accessed | tf_op | source)
XLA Modules:
  0.0 143.7 jit_solution(2335484898673988629)
XLA Ops:
  0.0 2.0 %slice_bitcast_fusion = bf16[1024,256]{1,0:T(8,128)(2,1)} fusion(bf16[1,3584,256]{2,1,0:T(8,128)(2,1)} %param.8), kind=kLoop, calls=%fused_computation.85 | loop fusion | bytes 1048576 | tf_op jit(solution)/shard_map/slice | solution.py:103
  2.0 0.7 collective-permute-start.1
  2.7 5.9 %collective-permute-start = (bf16[1024,256]{1,0:T(8,128)(2,1)}, bf16[1024,256]{1,0:T(8,128)(2,1)S(1)}, u32[]{:S(2)}, u32[]{:S(2)}) collective-permute-start(bf16[1024,256]{1,0:T(8,128)(2,1)} %slice_bitcast_fusion), channel_id=1, source_target_pairs={{0,4},{4,0},{8,12},{12,8},{1,5},{5,1},{9,13},{13,9},{2,6},{6,2},{1... | collective-permute-start | bytes 1572872 | tf_op jit(solution)/shard_map/ppermute | solution.py:62
  8.7 0.7 collective-permute-start.3
  9.4 0.7 fusion.135
  10.1 1.1 slice.118
  11.2 0.7 collective-permute-start.6
  11.9 9.7 %collective-permute-done = bf16[1024,256]{1,0:T(8,128)(2,1)S(1)} collective-permute-done((bf16[1024,256]{1,0:T(8,128)(2,1)}, bf16[1024,256]{1,0:T(8,128)(2,1)S(1)}, u32[]{:S(2)}, u32[]{:S(2)}) %collective-permute-start) | collective-permute-done | bytes 524320 | tf_op jit(solution)/shard_map/ppermute | solution.py:62
  21.6 1.2 slice_select_fusion
  22.7 5.0 %collective-permute-start.5 = (bf16[1024,256]{1,0:T(8,128)(2,1)S(1)}, bf16[1024,256]{1,0:T(8,128)(2,1)S(1)}, u32[]{:S(2)}, u32[]{:S(2)}) collective-permute-start(bf16[1024,256]{1,0:T(8,128)(2,1)S(1)} %slice_select_fusion), channel_id=1, source_target_pairs={{0,4},{4,0},{8,12},{12,8},{1,5},{5,1},{9,13},{13,9},{2,6},{6,2},{1... | collective-permute-start | bytes 1572872 | tf_op jit(solution)/shard_map/ppermute | solution.py:62
  27.8 5.2 %collective-permute-done.2 = bf16[1024,256]{1,0:T(8,128)(2,1)} collective-permute-done((bf16[1024,256]{1,0:T(8,128)(2,1)}, bf16[1024,256]{1,0:T(8,128)(2,1)}, u32[]{:S(2)}, u32[]{:S(2)}) %collective-permute-start.2) | collective-permute-done | bytes 524320 | tf_op jit(solution)/shard_map/ppermute | solution.py:62
  32.9 1.8 %fusion.30 = f32[512,256]{1,0:T(8,128)S(1)} fusion(bf16[1024,256]{1,0:T(8,128)(2,1)S(1)} %collective-permute-done, bf16[1,512,14336]{2,1,0:T(8,128)(2,1)} %param.6, s32[]{:T(128)S(6)} %select_n.175), kind=kOutput, calls=%fused_computation.39 | convolution fusion | flops 268435456 | bytes 2097156 | tf_op jit(solution)/shard_map/dot_general | solution.py:36
  34.8 3.6 %fusion.10 = f32[512,256]{1,0:T(8,128)S(1)} fusion(f32[512,256]{1,0:T(8,128)S(1)} %fusion.30, bf16[512,14336]{1,0:T(8,128)(2,1)} %bitcast.102, s32[]{:T(128)S(6)} %select_n.174, bf16[1,3584,256]{2,1,0:T(8,128)(2,1)S(1)} %copy-done), kind=kOutput, calls=%fused_computation.21 | convolution fusion | flops 939655168 | bytes 6553604 | tf_op jit(solution)/shard_map/dot_general | solution.py:36
  38.4 2.1 %collective-permute-start.4 = (bf16[1024,256]{1,0:T(8,128)(2,1)S(1)}, bf16[1024,256]{1,0:T(8,128)(2,1)S(1)}, u32[]{:S(2)}, u32[]{:S(2)}) collective-permute-start(bf16[1024,256]{1,0:T(8,128)(2,1)S(1)} %slice_select_fusion.1), channel_id=1, source_target_pairs={{0,4},{4,0},{8,12},{12,8},{1,5},{5,1},{9,13},{13,9},{2,6},{6,2},{1... | collective-permute-start | bytes 1572872 | tf_op jit(solution)/shard_map/ppermute | solution.py:62
  40.5 0.7 collective-permute-start.8
  41.2 1.8 %fusion.20 = f32[512,256]{1,0:T(8,128)S(1)} fusion(bf16[1024,256]{1,0:T(8,128)(2,1)} %collective-permute-done.2, bf16[1,512,4096]{2,1,0:T(8,128)(2,1)} %param.5, s32[]{:T(128)S(6)} %select_n.204), kind=kOutput, calls=%fused_computation.29 | convolution fusion | flops 268435456 | bytes 2097156 | tf_op jit(solution)/shard_map/dot_general | solution.py:36
  43.0 1.7 %convolution_add_fusion.3 = f32[512,256]{1,0:T(8,128)S(1)} fusion(f32[512,256]{1,0:T(8,128)S(1)} %fusion.20, bf16[512,4096]{1,0:T(8,128)(2,1)} %bitcast.108, s32[]{:T(128)S(6)} %select_n.203, bf16[1,1024,256]{2,1,0:T(8,128)(2,1)S(1)} %copy-done.3), kind=kOutput, calls=%fused_computation.5 | convolution fusion | flops 268566528 | bytes 2621444 | tf_op jit(solution)/shard_map/dot_general | solution.py:36
  44.8 0.7 collective-permute-start.12
  45.7 4.7 %collective-permute-start.7 = (bf16[1024,256]{1,0:T(8,128)(2,1)S(1)}, bf16[1024,256]{1,0:T(8,128)(2,1)S(1)}, u32[]{:S(2)}, u32[]{:S(2)}) collective-permute-start(bf16[1024,256]{1,0:T(8,128)(2,1)S(1)} %maximum_select_fusion), channel_id=1, source_target_pairs={{0,4},{4,0},{8,12},{12,8},{1,5},{5,1},{9,13},{13,9},{2,6},{6,2},{1... | collective-permute-start | bytes 1572872 | tf_op jit(solution)/shard_map/ppermute | solution.py:62
  50.4 0.5 fusion.27
  50.9 0.5 fusion.25
  51.3 4.0 %collective-permute-done.4 = bf16[1024,256]{1,0:T(8,128)(2,1)S(1)} collective-permute-done((bf16[1024,256]{1,0:T(8,128)(2,1)S(1)}, bf16[1024,256]{1,0:T(8,128)(2,1)S(1)}, u32[]{:S(2)}, u32[]{:S(2)}) %collective-permute-start.4) | collective-permute-done | bytes 524320 | tf_op jit(solution)/shard_map/ppermute | solution.py:62
  55.3 0.5 fusion.9
  56.0 2.1 %collective-permute-start.9 = (bf16[1024,256]{1,0:T(8,128)(2,1)S(1)}, bf16[1024,256]{1,0:T(8,128)(2,1)S(1)}, u32[]{:S(2)}, u32[]{:S(2)}) collective-permute-start(bf16[1024,256]{1,0:T(8,128)(2,1)S(1)} %maximum_select_fusion.1), channel_id=1, source_target_pairs={{0,4},{4,0},{8,12},{12,8},{1,5},{5,1},{9,13},{13,9},{2,6},{6,2},{1... | collective-permute-start | bytes 1572872 | tf_op jit(solution)/shard_map/ppermute | solution.py:62
  58.1 0.7 collective-permute-start.10
  58.9 0.7 collective-permute-start.17
  59.6 7.0 %collective-permute-done.7 = bf16[1024,256]{1,0:T(8,128)(2,1)S(1)} collective-permute-done((bf16[1024,256]{1,0:T(8,128)(2,1)S(1)}, bf16[1024,256]{1,0:T(8,128)(2,1)S(1)}, u32[]{:S(2)}, u32[]{:S(2)}) %collective-permute-start.7) | collective-permute-done | bytes 524320 | tf_op jit(solution)/shard_map/ppermute | solution.py:62
  66.6 2.1 %collective-permute-start.13 = (bf16[512,256]{1,0:T(8,128)(2,1)S(1)}, bf16[512,256]{1,0:T(8,128)(2,1)S(1)}, u32[]{:S(2)}, u32[]{:S(2)}) collective-permute-start(bf16[512,256]{1,0:T(8,128)(2,1)S(1)} %slice_select_fusion.2), channel_id=1, source_target_pairs={{0,4},{4,0},{8,12},{12,8},{1,5},{5,1},{9,13},{13,9},{2,6},{6,2},{1... | collective-permute-start | bytes 786440 | tf_op jit(solution)/shard_map/ppermute | solution.py:62
  68.7 0.4 fusion.23
  69.4 0.2 convolution_add_fusion.9
  69.7 8.1 %collective-permute-done.9 = bf16[1024,256]{1,0:T(8,128)(2,1)S(1)} collective-permute-done((bf16[1024,256]{1,0:T(8,128)(2,1)S(1)}, bf16[1024,256]{1,0:T(8,128)(2,1)S(1)}, u32[]{:S(2)}, u32[]{:S(2)}) %collective-permute-start.9) | collective-permute-done | bytes 524320 | tf_op jit(solution)/shard_map/ppermute | solution.py:62
  78.0 0.2 fusion.7
  78.5 2.1 %collective-permute-start.11 = (bf16[1024,256]{1,0:T(8,128)(2,1)S(1)}, bf16[1024,256]{1,0:T(8,128)(2,1)S(1)}, u32[]{:S(2)}, u32[]{:S(2)}) collective-permute-start(bf16[1024,256]{1,0:T(8,128)(2,1)S(1)} %maximum_select_fusion.2), channel_id=1, source_target_pairs={{0,4},{4,0},{8,12},{12,8},{1,5},{5,1},{9,13},{13,9},{2,6},{6,2},{1... | collective-permute-start | bytes 1572872 | tf_op jit(solution)/shard_map/ppermute | solution.py:62
  80.6 0.5 fusion.17
  81.1 0.5 fusion.4
  81.5 1.5 %collective-permute-start.14 = (f32[512,256]{1,0:T(8,128)S(1)}, f32[512,256]{1,0:T(8,128)S(1)}, u32[]{:S(2)}, u32[]{:S(2)}) collective-permute-start(f32[512,256]{1,0:T(8,128)S(1)} %fusion.4), channel_id=1, source_target_pairs={{0,2},{2,0},{1,3},{3,1},{4,6},{6,4},{5,7},{7,5},{8,10},{10,8},{9,1... | collective-permute-start | bytes 1572872 | tf_op jit(solution)/shard_map/ppermute | solution.py:129
  83.1 0.7 collective-permute-start.15
  83.8 0.3 fusion.49
  84.1 0.3 fusion.47
  84.6 1.8 %collective-permute-start.18 = (bf16[1024,256]{1,0:T(8,128)(2,1)S(1)}, bf16[1024,256]{1,0:T(8,128)(2,1)S(1)}, u32[]{:S(2)}, u32[]{:S(2)}) collective-permute-start(bf16[1024,256]{1,0:T(8,128)(2,1)S(1)} %maximum_select_fusion.4), channel_id=1, source_target_pairs={{0,4},{4,0},{8,12},{12,8},{1,5},{5,1},{9,13},{13,9},{2,6},{6,2},{1... | collective-permute-start | bytes 1572872 | tf_op jit(solution)/shard_map/ppermute | solution.py:62
  86.4 5.9 %collective-permute-done.14 = f32[512,256]{1,0:T(8,128)S(1)} collective-permute-done((f32[512,256]{1,0:T(8,128)S(1)}, f32[512,256]{1,0:T(8,128)S(1)}, u32[]{:S(2)}, u32[]{:S(2)}) %collective-permute-start.14) | collective-permute-done | bytes 524320 | tf_op jit(solution)/shard_map/ppermute | solution.py:129
  92.5 2.1 %collective-permute-done.11 = bf16[1024,256]{1,0:T(8,128)(2,1)S(1)} collective-permute-done((bf16[1024,256]{1,0:T(8,128)(2,1)S(1)}, bf16[1024,256]{1,0:T(8,128)(2,1)S(1)}, u32[]{:S(2)}, u32[]{:S(2)}) %collective-permute-start.11) | collective-permute-done | bytes 524320 | tf_op jit(solution)/shard_map/ppermute | solution.py:62
  94.8 2.1 %collective-permute-start.16 = (bf16[1024,256]{1,0:T(8,128)(2,1)S(1)}, bf16[1024,256]{1,0:T(8,128)(2,1)S(1)}, u32[]{:S(2)}, u32[]{:S(2)}) collective-permute-start(bf16[1024,256]{1,0:T(8,128)(2,1)S(1)} %maximum_select_fusion.3), channel_id=1, source_target_pairs={{0,4},{4,0},{8,12},{12,8},{1,5},{5,1},{9,13},{13,9},{2,6},{6,2},{1... | collective-permute-start | bytes 1572872 | tf_op jit(solution)/shard_map/ppermute | solution.py:62
  97.0 1.9 %collective-permute-start.21 = (f32[512,256]{1,0:T(8,128)S(1)}, f32[512,256]{1,0:T(8,128)S(1)}, u32[]{:S(2)}, u32[]{:S(2)}) collective-permute-start(f32[512,256]{1,0:T(8,128)S(1)} %add_multiply_fusion.2), channel_id=1, source_target_pairs={{0,4},{12,8},{1,5},{13,9},{2,6},{14,10},{3,7},{15,11},{16,20},{28,... | collective-permute-start | bytes 1572872 | tf_op jit(solution)/shard_map/ppermute | solution.py:131
  98.9 0.5 fusion.8
  99.4 0.2 fusion.80
  99.6 0.2 fusion.6
  99.9 0.7 collective-permute-start.19
  100.6 5.3 %collective-permute-done.18 = bf16[1024,256]{1,0:T(8,128)(2,1)S(1)} collective-permute-done((bf16[1024,256]{1,0:T(8,128)(2,1)S(1)}, bf16[1024,256]{1,0:T(8,128)(2,1)S(1)}, u32[]{:S(2)}, u32[]{:S(2)}) %collective-permute-start.18) | collective-permute-done | bytes 524320 | tf_op jit(solution)/shard_map/ppermute | solution.py:62
  106.3 10.4 %collective-permute-done.16 = bf16[1024,256]{1,0:T(8,128)(2,1)S(1)} collective-permute-done((bf16[1024,256]{1,0:T(8,128)(2,1)S(1)}, bf16[1024,256]{1,0:T(8,128)(2,1)S(1)}, u32[]{:S(2)}, u32[]{:S(2)}) %collective-permute-start.16) | collective-permute-done | bytes 524320 | tf_op jit(solution)/shard_map/ppermute | solution.py:62
  116.7 0.7 collective-permute-start.23
  117.3 0.5 convolution_add_fusion.1
  118.0 0.2 fusion.5
  118.3 1.3 collective-permute-start.20
  119.6 1.3 collective-permute-start.24
  120.9 0.5 convolution_add_fusion
  121.4 5.1 %collective-permute-done.21 = f32[512,256]{1,0:T(8,128)S(1)} collective-permute-done((f32[512,256]{1,0:T(8,128)S(1)}, f32[512,256]{1,0:T(8,128)S(1)}, u32[]{:S(2)}, u32[]{:S(2)}) %collective-permute-start.21) | collective-permute-done | bytes 524320 | tf_op jit(solution)/shard_map/ppermute | solution.py:131
  126.6 1.3 collective-permute-start.22
  127.8 10.5 %collective-permute-done.24 = bf16[512,256]{1,0:T(8,128)(2,1)S(1)} collective-permute-done((bf16[512,256]{1,0:T(8,128)(2,1)S(1)}, bf16[512,256]{1,0:T(8,128)(2,1)S(1)}, u32[]{:S(2)}, u32[]{:S(2)}) %collective-permute-start.24) | collective-permute-done | bytes 262176 | tf_op jit(solution)/shard_map/ppermute | solution.py:62
  138.4 0.3 fusion.45
  138.7 0.5 fusion.13
  139.5 1.5 %collective-permute-start.25 = (f32[2,32]{1,0:T(2,128)S(1)}, f32[2,32]{1,0:T(2,128)S(1)}, u32[]{:S(2)}, u32[]{:S(2)}) collective-permute-start(f32[2,32]{1,0:T(2,128)S(1)} %reduce_sum.29), channel_id=1, source_target_pairs={{0,2},{2,0},{1,3},{3,1},{4,6},{6,4},{5,7},{7,5},{8,10},{10,8},{9,1... | collective-permute-start | bytes 776 | tf_op jit(solution)/shard_map/ppermute | solution.py:180
  141.0 2.1 %collective-permute-done.25 = f32[2,32]{1,0:T(2,128)S(1)} collective-permute-done((f32[2,32]{1,0:T(2,128)S(1)}, f32[2,32]{1,0:T(2,128)S(1)}, u32[]{:S(2)}, u32[]{:S(2)}) %collective-permute-start.25) | collective-permute-done | bytes 288 | tf_op jit(solution)/shard_map/ppermute | solution.py:180
  143.1 0.6 multiply_bitcast_fusion
  (51 shorter events, 3.2 us)
Async XLA Ops:
  0.0 34.8 %copy-start = (bf16[1,3584,256]{2,1,0:T(8,128)(2,1)S(1)}, bf16[1,3584,256]{2,1,0:T(8,128)(2,1)}, u32[]{:S(2)}) copy-start(bf16[1,3584,256]{2,1,0:T(8,128)(2,1)} %param.8) | copy-start | bytes 5505028
  2.0 8.1 %collective-permute-start.1 = (bf16[1024,256]{1,0:T(8,128)(2,1)}, bf16[1024,256]{1,0:T(8,128)(2,1)S(1)}, u32[]{:S(2)}, u32[]{:S(2)}) collective-permute-start(bf16[1024,256]{1,0:T(8,128)(2,1)} %slice_bitcast_fusion), channel_id=1, source_target_pairs={{4,8},{8,4},{5,9},{9,5},{6,10},{10,6},{7,11},{11,7},{20,24},{24,20... | collective-permute-start | bytes 1572872 | tf_op jit(solution)/shard_map/ppermute | solution.py:62
  2.7 18.9 %collective-permute-start = (bf16[1024,256]{1,0:T(8,128)(2,1)}, bf16[1024,256]{1,0:T(8,128)(2,1)S(1)}, u32[]{:S(2)}, u32[]{:S(2)}) collective-permute-start(bf16[1024,256]{1,0:T(8,128)(2,1)} %slice_bitcast_fusion), channel_id=1, source_target_pairs={{0,4},{4,0},{8,12},{12,8},{1,5},{5,1},{9,13},{13,9},{2,6},{6,2},{1... | collective-permute-start | bytes 1572872 | tf_op jit(solution)/shard_map/ppermute | solution.py:62
  8.6 24.3 %collective-permute-start.2 = (bf16[1024,256]{1,0:T(8,128)(2,1)}, bf16[1024,256]{1,0:T(8,128)(2,1)}, u32[]{:S(2)}, u32[]{:S(2)}) collective-permute-start(bf16[1024,256]{1,0:T(8,128)(2,1)} %bitcast.109), channel_id=1, source_target_pairs={{0,4},{4,0},{8,12},{12,8},{1,5},{5,1},{9,13},{13,9},{2,6},{6,2},{1... | collective-permute-start | bytes 1572872 | tf_op jit(solution)/shard_map/ppermute | solution.py:62
  8.7 29.7 %collective-permute-start.3 = (bf16[1024,256]{1,0:T(8,128)(2,1)}, bf16[1024,256]{1,0:T(8,128)(2,1)S(1)}, u32[]{:S(2)}, u32[]{:S(2)}) collective-permute-start(bf16[1024,256]{1,0:T(8,128)(2,1)} %bitcast.110), channel_id=1, source_target_pairs={{4,8},{8,4},{5,9},{9,5},{6,10},{10,6},{7,11},{11,7},{20,24},{24,20... | collective-permute-start | bytes 1572872 | tf_op jit(solution)/shard_map/ppermute | solution.py:62
  11.2 33.5 %collective-permute-start.6 = (bf16[1024,256]{1,0:T(8,128)(2,1)S(1)}, bf16[1024,256]{1,0:T(8,128)(2,1)S(1)}, u32[]{:S(2)}, u32[]{:S(2)}) collective-permute-start(bf16[1024,256]{1,0:T(8,128)(2,1)S(1)} %slice.118), channel_id=1, source_target_pairs={{4,8},{8,4},{5,9},{9,5},{6,10},{10,6},{7,11},{11,7},{20,24},{24,20... | collective-permute-start | bytes 1572872 | tf_op jit(solution)/shard_map/ppermute | solution.py:62
  21.6 21.5 %copy-start.3 = (bf16[1,1024,256]{2,1,0:T(8,128)(2,1)S(1)}, bf16[1,1024,256]{2,1,0:T(8,128)(2,1)}, u32[]{:S(2)}) copy-start(bf16[1,1024,256]{2,1,0:T(8,128)(2,1)} %param.7) | copy-start | bytes 1572868
  22.7 22.7 %collective-permute-start.5 = (bf16[1024,256]{1,0:T(8,128)(2,1)S(1)}, bf16[1024,256]{1,0:T(8,128)(2,1)S(1)}, u32[]{:S(2)}, u32[]{:S(2)}) collective-permute-start(bf16[1024,256]{1,0:T(8,128)(2,1)S(1)} %slice_select_fusion), channel_id=1, source_target_pairs={{0,4},{4,0},{8,12},{12,8},{1,5},{5,1},{9,13},{13,9},{2,6},{6,2},{1... | collective-permute-start | bytes 1572872 | tf_op jit(solution)/shard_map/ppermute | solution.py:62
  32.9 12.6 %copy-start.1 = (bf16[1,512,14336]{2,1,0:T(8,128)(2,1)S(1)}, bf16[1,512,14336]{2,1,0:T(8,128)(2,1)}, u32[]{:S(2)}) copy-start(bf16[1,512,14336]{2,1,0:T(8,128)(2,1)} %param.6) | copy-start | bytes 44040196
  38.4 16.9 %collective-permute-start.4 = (bf16[1024,256]{1,0:T(8,128)(2,1)S(1)}, bf16[1024,256]{1,0:T(8,128)(2,1)S(1)}, u32[]{:S(2)}, u32[]{:S(2)}) collective-permute-start(bf16[1024,256]{1,0:T(8,128)(2,1)S(1)} %slice_select_fusion.1), channel_id=1, source_target_pairs={{0,4},{4,0},{8,12},{12,8},{1,5},{5,1},{9,13},{13,9},{2,6},{6,2},{1... | collective-permute-start | bytes 1572872 | tf_op jit(solution)/shard_map/ppermute | solution.py:62
  40.5 15.3 %collective-permute-start.8 = (bf16[1024,256]{1,0:T(8,128)(2,1)}, bf16[1024,256]{1,0:T(8,128)(2,1)S(1)}, u32[]{:S(2)}, u32[]{:S(2)}) collective-permute-start(bf16[1024,256]{1,0:T(8,128)(2,1)} %collective-permute-done.2), channel_id=1, source_target_pairs={{4,8},{8,4},{5,9},{9,5},{6,10},{10,6},{7,11},{11,7},{20,24},{24,20... | collective-permute-start | bytes 1572872 | tf_op jit(solution)/shard_map/ppermute | solution.py:62
  44.8 14.1 %collective-permute-start.12 = (bf16[512,256]{1,0:T(8,128)(2,1)S(1)}, bf16[512,256]{1,0:T(8,128)(2,1)S(1)}, u32[]{:S(2)}, u32[]{:S(2)}) collective-permute-start(bf16[512,256]{1,0:T(8,128)(2,1)S(1)} %slice.133), channel_id=1, source_target_pairs={{4,8},{8,4},{5,9},{9,5},{6,10},{10,6},{7,11},{11,7},{20,24},{24,20... | collective-permute-start | bytes 786440 | tf_op jit(solution)/shard_map/ppermute | solution.py:62
  45.7 20.8 %collective-permute-start.7 = (bf16[1024,256]{1,0:T(8,128)(2,1)S(1)}, bf16[1024,256]{1,0:T(8,128)(2,1)S(1)}, u32[]{:S(2)}, u32[]{:S(2)}) collective-permute-start(bf16[1024,256]{1,0:T(8,128)(2,1)S(1)} %maximum_select_fusion), channel_id=1, source_target_pairs={{0,4},{4,0},{8,12},{12,8},{1,5},{5,1},{9,13},{13,9},{2,6},{6,2},{1... | collective-permute-start | bytes 1572872 | tf_op jit(solution)/shard_map/ppermute | solution.py:62
  56.0 21.8 %collective-permute-start.9 = (bf16[1024,256]{1,0:T(8,128)(2,1)S(1)}, bf16[1024,256]{1,0:T(8,128)(2,1)S(1)}, u32[]{:S(2)}, u32[]{:S(2)}) collective-permute-start(bf16[1024,256]{1,0:T(8,128)(2,1)S(1)} %maximum_select_fusion.1), channel_id=1, source_target_pairs={{0,4},{4,0},{8,12},{12,8},{1,5},{5,1},{9,13},{13,9},{2,6},{6,2},{1... | collective-permute-start | bytes 1572872 | tf_op jit(solution)/shard_map/ppermute | solution.py:62
  58.1 20.2 %collective-permute-start.10 = (bf16[1024,256]{1,0:T(8,128)(2,1)S(1)}, bf16[1024,256]{1,0:T(8,128)(2,1)S(1)}, u32[]{:S(2)}, u32[]{:S(2)}) collective-permute-start(bf16[1024,256]{1,0:T(8,128)(2,1)S(1)} %slice.131), channel_id=1, source_target_pairs={{4,8},{8,4},{5,9},{9,5},{6,10},{10,6},{7,11},{11,7},{20,24},{24,20... | collective-permute-start | bytes 1572872 | tf_op jit(solution)/shard_map/ppermute | solution.py:62
  58.9 25.6 %collective-permute-start.17 = (bf16[1024,256]{1,0:T(8,128)(2,1)S(1)}, bf16[1024,256]{1,0:T(8,128)(2,1)S(1)}, u32[]{:S(2)}, u32[]{:S(2)}) collective-permute-start(bf16[1024,256]{1,0:T(8,128)(2,1)S(1)} %collective-permute-done.4), channel_id=1, source_target_pairs={{4,8},{8,4},{5,9},{9,5},{6,10},{10,6},{7,11},{11,7},{20,24},{24,20... | collective-permute-start | bytes 1572872 | tf_op jit(solution)/shard_map/ppermute | solution.py:62
  66.6 17.2 %collective-permute-start.13 = (bf16[512,256]{1,0:T(8,128)(2,1)S(1)}, bf16[512,256]{1,0:T(8,128)(2,1)S(1)}, u32[]{:S(2)}, u32[]{:S(2)}) collective-permute-start(bf16[512,256]{1,0:T(8,128)(2,1)S(1)} %slice_select_fusion.2), channel_id=1, source_target_pairs={{0,4},{4,0},{8,12},{12,8},{1,5},{5,1},{9,13},{13,9},{2,6},{6,2},{1... | collective-permute-start | bytes 786440 | tf_op jit(solution)/shard_map/ppermute | solution.py:62
  69.2 11.4 %copy-start.2 = (bf16[1,512,4096]{2,1,0:T(8,128)(2,1)S(1)}, bf16[1,512,4096]{2,1,0:T(8,128)(2,1)}, u32[]{:S(2)}) copy-start(bf16[1,512,4096]{2,1,0:T(8,128)(2,1)} %param.5) | copy-start | bytes 12582916
  78.5 16.1 %collective-permute-start.11 = (bf16[1024,256]{1,0:T(8,128)(2,1)S(1)}, bf16[1024,256]{1,0:T(8,128)(2,1)S(1)}, u32[]{:S(2)}, u32[]{:S(2)}) collective-permute-start(bf16[1024,256]{1,0:T(8,128)(2,1)S(1)} %maximum_select_fusion.2), channel_id=1, source_target_pairs={{0,4},{4,0},{8,12},{12,8},{1,5},{5,1},{9,13},{13,9},{2,6},{6,2},{1... | collective-permute-start | bytes 1572872 | tf_op jit(solution)/shard_map/ppermute | solution.py:62
  81.5 10.8 %collective-permute-start.14 = (f32[512,256]{1,0:T(8,128)S(1)}, f32[512,256]{1,0:T(8,128)S(1)}, u32[]{:S(2)}, u32[]{:S(2)}) collective-permute-start(f32[512,256]{1,0:T(8,128)S(1)} %fusion.4), channel_id=1, source_target_pairs={{0,2},{2,0},{1,3},{3,1},{4,6},{6,4},{5,7},{7,5},{8,10},{10,8},{9,1... | collective-permute-start | bytes 1572872 | tf_op jit(solution)/shard_map/ppermute | solution.py:129
  83.1 11.6 %collective-permute-start.15 = (bf16[1024,256]{1,0:T(8,128)(2,1)S(1)}, bf16[1024,256]{1,0:T(8,128)(2,1)S(1)}, u32[]{:S(2)}, u32[]{:S(2)}) collective-permute-start(bf16[1024,256]{1,0:T(8,128)(2,1)S(1)} %collective-permute-done), channel_id=1, source_target_pairs={{4,8},{8,4},{5,9},{9,5},{6,10},{10,6},{7,11},{11,7},{20,24},{24,20... | collective-permute-start | bytes 1572872 | tf_op jit(solution)/shard_map/ppermute | solution.py:62
  84.6 21.2 %collective-permute-start.18 = (bf16[1024,256]{1,0:T(8,128)(2,1)S(1)}, bf16[1024,256]{1,0:T(8,128)(2,1)S(1)}, u32[]{:S(2)}, u32[]{:S(2)}) collective-permute-start(bf16[1024,256]{1,0:T(8,128)(2,1)S(1)} %maximum_select_fusion.4), channel_id=1, source_target_pairs={{0,4},{4,0},{8,12},{12,8},{1,5},{5,1},{9,13},{13,9},{2,6},{6,2},{1... | collective-permute-start | bytes 1572872 | tf_op jit(solution)/shard_map/ppermute | solution.py:62
  94.8 21.8 %collective-permute-start.16 = (bf16[1024,256]{1,0:T(8,128)(2,1)S(1)}, bf16[1024,256]{1,0:T(8,128)(2,1)S(1)}, u32[]{:S(2)}, u32[]{:S(2)}) collective-permute-start(bf16[1024,256]{1,0:T(8,128)(2,1)S(1)} %maximum_select_fusion.3), channel_id=1, source_target_pairs={{0,4},{4,0},{8,12},{12,8},{1,5},{5,1},{9,13},{13,9},{2,6},{6,2},{1... | collective-permute-start | bytes 1572872 | tf_op jit(solution)/shard_map/ppermute | solution.py:62
  97.0 29.5 %collective-permute-start.21 = (f32[512,256]{1,0:T(8,128)S(1)}, f32[512,256]{1,0:T(8,128)S(1)}, u32[]{:S(2)}, u32[]{:S(2)}) collective-permute-start(f32[512,256]{1,0:T(8,128)S(1)} %add_multiply_fusion.2), channel_id=1, source_target_pairs={{0,4},{12,8},{1,5},{13,9},{2,6},{14,10},{3,7},{15,11},{16,20},{28,... | collective-permute-start | bytes 1572872 | tf_op jit(solution)/shard_map/ppermute | solution.py:131
  99.9 18.4 %collective-permute-start.19 = (bf16[1024,256]{1,0:T(8,128)(2,1)S(1)}, bf16[1024,256]{1,0:T(8,128)(2,1)S(1)}, u32[]{:S(2)}, u32[]{:S(2)}) collective-permute-start(bf16[1024,256]{1,0:T(8,128)(2,1)S(1)} %collective-permute-done.5), channel_id=1, source_target_pairs={{4,8},{8,4},{5,9},{9,5},{6,10},{10,6},{7,11},{11,7},{20,24},{24,20... | collective-permute-start | bytes 1572872 | tf_op jit(solution)/shard_map/ppermute | solution.py:62
  116.7 2.9 %collective-permute-start.23 = (bf16[512,256]{1,0:T(8,128)(2,1)S(1)}, bf16[512,256]{1,0:T(8,128)(2,1)S(1)}, u32[]{:S(2)}, u32[]{:S(2)}) collective-permute-start(bf16[512,256]{1,0:T(8,128)(2,1)S(1)} %collective-permute-done.13), channel_id=1, source_target_pairs={{4,8},{8,4},{5,9},{9,5},{6,10},{10,6},{7,11},{11,7},{20,24},{24,20... | collective-permute-start | bytes 786440 | tf_op jit(solution)/shard_map/ppermute | solution.py:62
  118.3 20.4 %collective-permute-start.20 = (bf16[1024,256]{1,0:T(8,128)(2,1)S(1)}, bf16[1024,256]{1,0:T(8,128)(2,1)S(1)}, u32[]{:S(2)}, u32[]{:S(2)}) collective-permute-start(bf16[1024,256]{1,0:T(8,128)(2,1)S(1)} %collective-permute-done.19), channel_id=1, source_target_pairs={{4,0},{8,12},{5,1},{9,13},{6,2},{10,14},{7,3},{11,15},{20,16},{24,... | collective-permute-start | bytes 1572872 | tf_op jit(solution)/shard_map/ppermute | solution.py:62
  119.6 18.8 %collective-permute-start.24 = (bf16[512,256]{1,0:T(8,128)(2,1)S(1)}, bf16[512,256]{1,0:T(8,128)(2,1)S(1)}, u32[]{:S(2)}, u32[]{:S(2)}) collective-permute-start(bf16[512,256]{1,0:T(8,128)(2,1)S(1)} %collective-permute-done.23), channel_id=1, source_target_pairs={{4,0},{8,12},{5,1},{9,13},{6,2},{10,14},{7,3},{11,15},{20,16},{24,... | collective-permute-start | bytes 786440 | tf_op jit(solution)/shard_map/ppermute | solution.py:62
  126.6 12.7 %collective-permute-start.22 = (f32[2,256]{1,0:T(2,128)S(1)}, f32[2,256]{1,0:T(2,128)S(1)}, u32[]{:S(2)}, u32[]{:S(2)}) collective-permute-start(f32[2,256]{1,0:T(2,128)S(1)} %bitcast_reduce_fusion.1), channel_id=1, source_target_pairs={{4,0},{8,12},{5,1},{9,13},{6,2},{10,14},{7,3},{11,15},{20,16},{24,... | collective-permute-start | bytes 6152 | tf_op jit(solution)/shard_map/ppermute | solution.py:174
  139.5 3.6 %collective-permute-start.25 = (f32[2,32]{1,0:T(2,128)S(1)}, f32[2,32]{1,0:T(2,128)S(1)}, u32[]{:S(2)}, u32[]{:S(2)}) collective-permute-start(f32[2,32]{1,0:T(2,128)S(1)} %reduce_sum.29), channel_id=1, source_target_pairs={{0,2},{2,0},{1,3},{3,1},{4,6},{6,4},{5,7},{7,5},{8,10},{10,8},{9,1... | collective-permute-start | bytes 776 | tf_op jit(solution)/shard_map/ppermute | solution.py:180
where the time goes:
time: 144 us
  waiting for transfers between devices  75.2 us (52%)
  starting transfers between devices  43.8 us (30%)
  matrix products  16.6 us (12%)
  other arithmetic  3.86 us (3%)
  local copies, waits for them, and re-layouts  3.63 us (3%)
    ppermute x22, waiting for transfers between devices, __call__(): self.came.append(lax.ppermute(x, 'dp', pairs or self.pairs))  62.1 us
    ppermute x22, starting transfers between devices, __call__(): self.came.append(lax.ppermute(x, 'dp', pairs or self.pairs))  37.5 us
    dot_general x27, matrix products, dot(): return jnp.dot(a, b, preferred_element_type=jnp.float32)  16.6 us
    ppermute x1, waiting for transfers between devices, on_line(): other_acts = lax.ppermute(proj_acts, 'mp', [(0, 1), (1, 0)])  5.92 us
    ppermute x1, waiting for transfers between devices, on_line(): guest_acts = lax.ppermute(masked, 'dp', TO_MIDDLE)  5.07 us
  transfers between devices with their start and end apart: 26, of which 12 were waited for; matrix products, arithmetic and copies ran while one was open for 15% of the time, Pallas kernels for 0%

commit v1 on v0

--- a/solution.py
+++ b/solution.py
@@ -100,25 +100,24 @@
     x, y = {}, {}
     x["A"] = trade(left)
     y["AM"] = across(left)
-    first = right[:unit]
-    x["B"] = trade(first)
-    y["BM"] = across(first)
-    y["AE"] = across(across.ready(x["A"]))
+    x["B"] = trade(right[:unit])
+    y["AE"] = across(after(x["A"], y["AM"]))
     x["AM"] = trade(either(own("C1", trade), y["AM"]))
+    y["BM"] = across(own("B", across))
+    x["AE"] = trade(either(own("C2", trade), y["AE"]))
     y["C1M"] = across(own("C1", across))
-    x["BM"] = trade(either(own("C2", trade), y["BM"]))
+    x["BM"] = trade(either(guest(0, trade), y["BM"]))
     y["C2M"] = across(own("C2", across))
-    x["AE"] = trade(either(guest(0, trade), y["AE"]))
+    x["C1M"] = trade(either(guest(1, trade), y["C1M"]))
     y["C3M"] = across(own("C3", across))
-    x["C1M"] = trade(either(guest(1, trade), y["C1M"]))
+    x["C2M"] = trade(either(guest(2, trade), y["C2M"]))
     y["BE"] = across(across.ready(x["B"]))
-    x["C2M"] = trade(either(guest(2, trade), y["C2M"]))
+    x["C3M"] = trade(either(own("C3", trade), y["C3M"]))
     y["C1E"] = across(across.ready(x["AM"]))
-    x["C3M"] = trade(either(own("C3", trade), y["C3M"]))
-    y["C2E"] = across(across.ready(x["BM"]))
     x["BE"] = trade(either(guest(3, trade), y["BE"]))
-    y["C3E"] = across(across.ready(x["C3M"], x["BE"]))
+    y["C2E"] = across(across.ready(x["AE"]))
     x["C1E"] = trade(either(guest(4, trade), y["C1E"]))
+    y["C3E"] = across(after(x["C3M"], y["C2E"]))
     x["C2E"] = trade(trade.ready(y["C2E"]), TO_END)
     x["C3E"] = trade(trade.ready(y["C3E"]), TO_END)
 
@@ -150,14 +149,15 @@
             terms.append(dot(rows, right[begin : begin + half // 2]))
         return terms[0] + terms[1]
 
-    proj_grads = dot(columns(after(grads, x["B"], y["BM"]), place, 0, depth), right)
+    proj_grads = dot(columns(after(grads, x["AM"], y["AE"]), place, 0, depth), right)
+    proj_grads = after(proj_grads, x["AE"])
     proj_grads += near_term("B", x["B"])
     proj_grads = after(proj_grads)
     proj_grads += near_term("C1", x["AM"])
+    proj_grads += near_term("C2", x["AE"])
+    proj_grads = after(proj_grads)
     proj_grads += middle_term("B")
-    proj_grads += near_term("C2", x["BM"])
-    proj_grads = after(proj_grads)
-    guest_grads = guest_term(0, x["AE"])
+    guest_grads = guest_term(0, x["BM"])
     proj_grads += middle_term("C1")
     guest_grads += guest_term(1, x["C1M"])
     proj_grads, guest_grads = lax.optimization_barrier((proj_grads, guest_grads))

time: 144 us -> 135 us (0.938)
  waiting for transfers between devices: 75.2 us -> 35.9 us
  starting transfers between devices: 43.8 us -> 76.8 us
  matrix products: 16.6 us -> 14 us
    ppermute x22, starting transfers between devices: 37.5 us -> 67.6 us  [__call__(): self.came.append(lax.ppermute(x, 'dp', pairs or self.pairs))]
    ppermute x22, waiting for transfers between devices: 62.1 us -> 33.6 us  [__call__(): self.came.append(lax.ppermute(x, 'dp', pairs or self.pairs))]
    ppermute x1, waiting for transfers between devices: 5.92 us -> 0.18 us  [on_line(): other_acts = lax.ppermute(proj_acts, 'mp', [(0, 1), (1, 0)])]
    ppermute x1, waiting for transfers between devices: 5.07 us -> 0.01 us  [on_line(): guest_acts = lax.ppermute(masked, 'dp', TO_MIDDLE)]
    ppermute x1, starting transfers between devices: 1.95 us -> 4.92 us  [on_line(): guest_acts = lax.ppermute(masked, 'dp', TO_MIDDLE)]
    dot_general x27, matrix products: 16.6 us -> 14 us  [dot(): return jnp.dot(a, b, preferred_element_type=jnp.float32)]
  transfers between devices with their start and end apart: 26 -> 26, of which waited for: 12 -> 8; matrix products, arithmetic and copies ran while one was open for 15% -> 15% of each run, Pallas kernels for 0% -> 0%
where the time goes in v1:
time: 135 us
  starting transfers between devices  76.8 us (57%)
  waiting for transfers between devices  35.9 us (27%)
  matrix products  14 us (10%)
  other arithmetic  3.97 us (3%)
  local copies, waits for them, and re-layouts  3.47 us (3%)
    ppermute x22, starting transfers between devices, __call__(): self.came.append(lax.ppermute(x, 'dp', pairs or self.pairs))  67.6 us
    ppermute x22, waiting for transfers between devices, __call__(): self.came.append(lax.ppermute(x, 'dp', pairs or self.pairs))  33.6 us
    dot_general x27, matrix products, dot(): return jnp.dot(a, b, preferred_element_type=jnp.float32)  14 us
    ppermute x1, starting transfers between devices, on_line(): guest_acts = lax.ppermute(masked, 'dp', TO_MIDDLE)  4.92 us
  transfers between devices with their start and end apart: 26, of which 8 were waited for; matrix products, arithmetic and copies ran while one was open for 15% of the time, Pallas kernels for 0%

profile of v1, /device:TPU:0, one launch (start us, length us, event | category | flops | bytes accessed | tf_op | source)
XLA Modules:
  0.0 134.7 jit_solution(9279828088426721203)
XLA Ops:
  0.0 3.0 %collective-permute-start = (bf16[1024,256]{1,0:T(8,128)(2,1)}, bf16[1024,256]{1,0:T(8,128)(2,1)S(1)}, u32[]{:S(2)}, u32[]{:S(2)}) collective-permute-start(bf16[1024,256]{1,0:T(8,128)(2,1)} %bitcast.114), channel_id=1, source_target_pairs={{0,4},{4,0},{8,12},{12,8},{1,5},{5,1},{9,13},{13,9},{2,6},{6,2},{1... | collective-permute-start | bytes 1572872 | tf_op jit(solution)/shard_map/ppermute | solution.py:62
  3.0 0.7 collective-permute-start.1
  3.7 1.9 %slice_bitcast_fusion = bf16[1024,256]{1,0:T(8,128)(2,1)} fusion(bf16[1,3584,256]{2,1,0:T(8,128)(2,1)} %param.8), kind=kLoop, calls=%fused_computation.83 | loop fusion | bytes 1048576 | tf_op jit(solution)/shard_map/slice | solution.py:103
  5.6 4.4 %collective-permute-start.4 = (bf16[1024,256]{1,0:T(8,128)(2,1)}, bf16[1024,256]{1,0:T(8,128)(2,1)S(1)}, u32[]{:S(2)}, u32[]{:S(2)}) collective-permute-start(bf16[1024,256]{1,0:T(8,128)(2,1)} %slice_bitcast_fusion), channel_id=1, source_target_pairs={{0,4},{4,0},{8,12},{12,8},{1,5},{5,1},{9,13},{13,9},{2,6},{6,2},{1... | collective-permute-start | bytes 1572872 | tf_op jit(solution)/shard_map/ppermute | solution.py:62
  10.0 0.7 fusion.139
  10.7 5.3 %collective-permute-done = bf16[1024,256]{1,0:T(8,128)(2,1)S(1)} collective-permute-done((bf16[1024,256]{1,0:T(8,128)(2,1)}, bf16[1024,256]{1,0:T(8,128)(2,1)S(1)}, u32[]{:S(2)}, u32[]{:S(2)}) %collective-permute-start) | collective-permute-done | bytes 524320 | tf_op jit(solution)/shard_map/ppermute | solution.py:62
  16.0 0.7 collective-permute-start.3
  16.7 1.3 slice_select_fusion.1
  17.9 6.9 %collective-permute-start.2 = (bf16[1024,256]{1,0:T(8,128)(2,1)S(1)}, bf16[1024,256]{1,0:T(8,128)(2,1)S(1)}, u32[]{:S(2)}, u32[]{:S(2)}) collective-permute-start(bf16[1024,256]{1,0:T(8,128)(2,1)S(1)} %slice_select_fusion.1), channel_id=1, source_target_pairs={{0,4},{4,0},{8,12},{12,8},{1,5},{5,1},{9,13},{13,9},{2,6},{6,2},{1... | collective-permute-start | bytes 1572872 | tf_op jit(solution)/shard_map/ppermute | solution.py:62
  24.9 1.7 %fusion.15 = f32[512,256]{1,0:T(8,128)S(1)} fusion(bf16[1024,256]{1,0:T(8,128)(2,1)S(1)} %collective-permute-done, bf16[1,512,4096]{2,1,0:T(8,128)(2,1)} %param.5, s32[]{:T(128)S(6)} %select_n.204), kind=kOutput, calls=%fused_computation.25 | convolution fusion | flops 268435456 | bytes 2097156 | tf_op jit(solution)/shard_map/dot_general | solution.py:36
  26.6 1.8 %convolution_add_fusion.3 = f32[512,256]{1,0:T(8,128)S(1)} fusion(f32[512,256]{1,0:T(8,128)S(1)} %fusion.15, bf16[512,4096]{1,0:T(8,128)(2,1)} %bitcast.113, s32[]{:T(128)S(6)} %select_n.203, bf16[1,1024,256]{2,1,0:T(8,128)(2,1)} %param.7), kind=kOutput, calls=%fused_computation.5 | convolution fusion | flops 268566528 | bytes 2621444 | tf_op jit(solution)/shard_map/dot_general | solution.py:36
  28.4 0.7 collective-permute-start.6
  29.2 1.7 %fusion.26 = f32[512,256]{1,0:T(8,128)S(1)} fusion(bf16[1024,256]{1,0:T(8,128)(2,1)S(1)} %collective-permute-done.4, bf16[1,512,14336]{2,1,0:T(8,128)(2,1)} %param.6, s32[]{:T(128)S(6)} %select_n.178), kind=kOutput, calls=%fused_computation.36 | convolution fusion | flops 268435456 | bytes 2097156 | tf_op jit(solution)/shard_map/dot_general | solution.py:36
  30.9 0.7 collective-permute-start.8
  31.7 8.8 %collective-permute-start.5 = (bf16[1024,256]{1,0:T(8,128)(2,1)S(1)}, bf16[1024,256]{1,0:T(8,128)(2,1)S(1)}, u32[]{:S(2)}, u32[]{:S(2)}) collective-permute-start(bf16[1024,256]{1,0:T(8,128)(2,1)S(1)} %slice_select_fusion), channel_id=1, source_target_pairs={{0,4},{4,0},{8,12},{12,8},{1,5},{5,1},{9,13},{13,9},{2,6},{6,2},{1... | collective-permute-start | bytes 1572872 | tf_op jit(solution)/shard_map/ppermute | solution.py:62
  40.5 1.1 constant_dynamic-slice_fusion.9
  41.7 6.4 %collective-permute-start.7 = (bf16[1024,256]{1,0:T(8,128)(2,1)S(1)}, bf16[1024,256]{1,0:T(8,128)(2,1)S(1)}, u32[]{:S(2)}, u32[]{:S(2)}) collective-permute-start(bf16[1024,256]{1,0:T(8,128)(2,1)S(1)} %maximum_select_fusion), channel_id=1, source_target_pairs={{0,4},{4,0},{8,12},{12,8},{1,5},{5,1},{9,13},{13,9},{2,6},{6,2},{1... | collective-permute-start | bytes 1572872 | tf_op jit(solution)/shard_map/ppermute | solution.py:62
  48.1 0.7 collective-permute-start.10
  48.9 0.5 fusion.24
  49.3 1.1 fusion
  50.5 0.7 collective-permute-start.12
  51.2 1.5 %collective-permute-done.5 = bf16[1024,256]{1,0:T(8,128)(2,1)S(1)} collective-permute-done((bf16[1024,256]{1,0:T(8,128)(2,1)S(1)}, bf16[1024,256]{1,0:T(8,128)(2,1)S(1)}, u32[]{:S(2)}, u32[]{:S(2)}) %collective-permute-start.5) | collective-permute-done | bytes 524320 | tf_op jit(solution)/shard_map/ppermute | solution.py:62
  53.0 10.2 %collective-permute-start.9 = (bf16[1024,256]{1,0:T(8,128)(2,1)S(1)}, bf16[1024,256]{1,0:T(8,128)(2,1)S(1)}, u32[]{:S(2)}, u32[]{:S(2)}) collective-permute-start(bf16[1024,256]{1,0:T(8,128)(2,1)S(1)} %maximum_select_fusion.1), channel_id=1, source_target_pairs={{0,4},{4,0},{8,12},{12,8},{1,5},{5,1},{9,13},{13,9},{2,6},{6,2},{1... | collective-permute-start | bytes 1572872 | tf_op jit(solution)/shard_map/ppermute | solution.py:62
  63.2 0.5 add_add_fusion.1
  63.9 6.7 %collective-permute-start.11 = (bf16[1024,256]{1,0:T(8,128)(2,1)S(1)}, bf16[1024,256]{1,0:T(8,128)(2,1)S(1)}, u32[]{:S(2)}, u32[]{:S(2)}) collective-permute-start(bf16[1024,256]{1,0:T(8,128)(2,1)S(1)} %maximum_select_fusion.2), channel_id=1, source_target_pairs={{0,4},{4,0},{8,12},{12,8},{1,5},{5,1},{9,13},{13,9},{2,6},{6,2},{1... | collective-permute-start | bytes 1572872 | tf_op jit(solution)/shard_map/ppermute | solution.py:62
  70.6 0.4 fusion.12
  71.0 0.5 fusion.3
  71.5 1.6 %collective-permute-start.14 = (f32[512,256]{1,0:T(8,128)S(1)}, f32[512,256]{1,0:T(8,128)S(1)}, u32[]{:S(2)}, u32[]{:S(2)}) collective-permute-start(f32[512,256]{1,0:T(8,128)S(1)} %fusion.3), channel_id=1, source_target_pairs={{0,2},{2,0},{1,3},{3,1},{4,6},{6,4},{5,7},{7,5},{8,10},{10,8},{9,1... | collective-permute-start | bytes 1572872 | tf_op jit(solution)/shard_map/ppermute | solution.py:128
  73.1 0.7 collective-permute-start.15
  73.8 0.2 fusion.90
  74.0 0.4 fusion.20
  74.5 0.7 collective-permute-start.17
  75.2 4.5 %collective-permute-start.13 = (bf16[512,256]{1,0:T(8,128)(2,1)S(1)}, bf16[512,256]{1,0:T(8,128)(2,1)S(1)}, u32[]{:S(2)}, u32[]{:S(2)}) collective-permute-start(bf16[512,256]{1,0:T(8,128)(2,1)S(1)} %slice_select_fusion.2), channel_id=1, source_target_pairs={{0,4},{4,0},{8,12},{12,8},{1,5},{5,1},{9,13},{13,9},{2,6},{6,2},{1... | collective-permute-start | bytes 786440 | tf_op jit(solution)/shard_map/ppermute | solution.py:62
  79.8 0.2 fusion.87
  80.0 0.5 add_add_fusion
  80.5 0.2 convolution_add_fusion.8
  80.7 0.2 fusion.6
  81.3 5.2 %collective-permute-done.11 = bf16[1024,256]{1,0:T(8,128)(2,1)S(1)} collective-permute-done((bf16[1024,256]{1,0:T(8,128)(2,1)S(1)}, bf16[1024,256]{1,0:T(8,128)(2,1)S(1)}, u32[]{:S(2)}, u32[]{:S(2)}) %collective-permute-start.11) | collective-permute-done | bytes 524320 | tf_op jit(solution)/shard_map/ppermute | solution.py:62
  86.6 3.4 %collective-permute-start.16 = (bf16[1024,256]{1,0:T(8,128)(2,1)S(1)}, bf16[1024,256]{1,0:T(8,128)(2,1)S(1)}, u32[]{:S(2)}, u32[]{:S(2)}) collective-permute-start(bf16[1024,256]{1,0:T(8,128)(2,1)S(1)} %maximum_select_fusion.3), channel_id=1, source_target_pairs={{0,4},{4,0},{8,12},{12,8},{1,5},{5,1},{9,13},{13,9},{2,6},{6,2},{1... | collective-permute-start | bytes 1572872 | tf_op jit(solution)/shard_map/ppermute | solution.py:62
  90.0 0.7 collective-permute-start.19
  90.7 4.9 %collective-permute-start.21 = (f32[512,256]{1,0:T(8,128)S(1)}, f32[512,256]{1,0:T(8,128)S(1)}, u32[]{:S(2)}, u32[]{:S(2)}) collective-permute-start(f32[512,256]{1,0:T(8,128)S(1)} %add_multiply_fusion.2), channel_id=1, source_target_pairs={{0,4},{12,8},{1,5},{13,9},{2,6},{14,10},{3,7},{15,11},{16,20},{28,... | collective-permute-start | bytes 1572872 | tf_op jit(solution)/shard_map/ppermute | solution.py:130
  95.6 0.2 fusion.84
  95.9 0.2 fusion.5
  96.1 0.3 fusion.45
  96.4 0.3 fusion.43
  96.8 0.5 fusion.7
  97.5 3.8 %collective-permute-start.18 = (bf16[1024,256]{1,0:T(8,128)(2,1)S(1)}, bf16[1024,256]{1,0:T(8,128)(2,1)S(1)}, u32[]{:S(2)}, u32[]{:S(2)}) collective-permute-start(bf16[1024,256]{1,0:T(8,128)(2,1)S(1)} %maximum_select_fusion.4), channel_id=1, source_target_pairs={{0,4},{4,0},{8,12},{12,8},{1,5},{5,1},{9,13},{13,9},{2,6},{6,2},{1... | collective-permute-start | bytes 1572872 | tf_op jit(solution)/shard_map/ppermute | solution.py:62
  101.3 0.7 collective-permute-start.23
  102.0 1.3 collective-permute-done.16
  103.3 0.4 convolution_add_fusion.1
  103.7 0.2 fusion.81
  104.0 0.2 fusion.4
  104.2 1.3 collective-permute-start.20
  105.5 15.7 %collective-permute-done.18 = bf16[1024,256]{1,0:T(8,128)(2,1)S(1)} collective-permute-done((bf16[1024,256]{1,0:T(8,128)(2,1)S(1)}, bf16[1024,256]{1,0:T(8,128)(2,1)S(1)}, u32[]{:S(2)}, u32[]{:S(2)}) %collective-permute-start.18) | collective-permute-done | bytes 524320 | tf_op jit(solution)/shard_map/ppermute | solution.py:62
  121.2 1.3 collective-permute-start.24
  122.7 0.5 convolution_add_fusion
  123.1 0.2 convolution_add_fusion.5
  123.5 1.3 collective-permute-start.22
  124.8 4.6 %collective-permute-done.24 = bf16[512,256]{1,0:T(8,128)(2,1)S(1)} collective-permute-done((bf16[512,256]{1,0:T(8,128)(2,1)S(1)}, bf16[512,256]{1,0:T(8,128)(2,1)S(1)}, u32[]{:S(2)}, u32[]{:S(2)}) %collective-permute-start.24) | collective-permute-done | bytes 262176 | tf_op jit(solution)/shard_map/ppermute | solution.py:62
  129.4 0.3 fusion.41
  129.7 0.5 fusion.8
  130.6 1.5 %collective-permute-start.25 = (f32[2,32]{1,0:T(2,128)S(1)}, f32[2,32]{1,0:T(2,128)S(1)}, u32[]{:S(2)}, u32[]{:S(2)}) collective-permute-start(f32[2,32]{1,0:T(2,128)S(1)} %reduce_sum.29), channel_id=1, source_target_pairs={{0,2},{2,0},{1,3},{3,1},{4,6},{6,4},{5,7},{7,5},{8,10},{10,8},{9,1... | collective-permute-start | bytes 776 | tf_op jit(solution)/shard_map/ppermute | solution.py:180
  132.1 2.1 %collective-permute-done.25 = f32[2,32]{1,0:T(2,128)S(1)} collective-permute-done((f32[2,32]{1,0:T(2,128)S(1)}, f32[2,32]{1,0:T(2,128)S(1)}, u32[]{:S(2)}, u32[]{:S(2)}) %collective-permute-start.25) | collective-permute-done | bytes 288 | tf_op jit(solution)/shard_map/ppermute | solution.py:180
  134.2 0.6 multiply_bitcast_fusion
  (50 shorter events, 2.4 us)
Async XLA Ops:
  0.0 28.4 %copy-start = (bf16[1,3584,256]{2,1,0:T(8,128)(2,1)S(1)}, bf16[1,3584,256]{2,1,0:T(8,128)(2,1)}, u32[]{:S(2)}) copy-start(bf16[1,3584,256]{2,1,0:T(8,128)(2,1)} %param.8) | copy-start | bytes 5505028
  0.0 16.0 %collective-permute-start = (bf16[1024,256]{1,0:T(8,128)(2,1)}, bf16[1024,256]{1,0:T(8,128)(2,1)S(1)}, u32[]{:S(2)}, u32[]{:S(2)}) collective-permute-start(bf16[1024,256]{1,0:T(8,128)(2,1)} %bitcast.114), channel_id=1, source_target_pairs={{0,4},{4,0},{8,12},{12,8},{1,5},{5,1},{9,13},{13,9},{2,6},{6,2},{1... | collective-permute-start | bytes 1572872 | tf_op jit(solution)/shard_map/ppermute | solution.py:62
  3.0 13.0 %collective-permute-start.1 = (bf16[1024,256]{1,0:T(8,128)(2,1)}, bf16[1024,256]{1,0:T(8,128)(2,1)S(1)}, u32[]{:S(2)}, u32[]{:S(2)}) collective-permute-start(bf16[1024,256]{1,0:T(8,128)(2,1)} %bitcast.115), channel_id=1, source_target_pairs={{4,8},{8,4},{5,9},{9,5},{6,10},{10,6},{7,11},{11,7},{20,24},{24,20... | collective-permute-start | bytes 1572872 | tf_op jit(solution)/shard_map/ppermute | solution.py:62
  5.6 22.8 %collective-permute-start.4 = (bf16[1024,256]{1,0:T(8,128)(2,1)}, bf16[1024,256]{1,0:T(8,128)(2,1)S(1)}, u32[]{:S(2)}, u32[]{:S(2)}) collective-permute-start(bf16[1024,256]{1,0:T(8,128)(2,1)} %slice_bitcast_fusion), channel_id=1, source_target_pairs={{0,4},{4,0},{8,12},{12,8},{1,5},{5,1},{9,13},{13,9},{2,6},{6,2},{1... | collective-permute-start | bytes 1572872 | tf_op jit(solution)/shard_map/ppermute | solution.py:62
  16.0 14.8 %collective-permute-start.3 = (bf16[1024,256]{1,0:T(8,128)(2,1)S(1)}, bf16[1024,256]{1,0:T(8,128)(2,1)S(1)}, u32[]{:S(2)}, u32[]{:S(2)}) collective-permute-start(bf16[1024,256]{1,0:T(8,128)(2,1)S(1)} %collective-permute-done), channel_id=1, source_target_pairs={{4,8},{8,4},{5,9},{9,5},{6,10},{10,6},{7,11},{11,7},{20,24},{24,20... | collective-permute-start | bytes 1572872 | tf_op jit(solution)/shard_map/ppermute | solution.py:62
  16.7 32.2 %copy-start.1 = (bf16[1,512,14336]{2,1,0:T(8,128)(2,1)S(1)}, bf16[1,512,14336]{2,1,0:T(8,128)(2,1)}, u32[]{:S(2)}) copy-start(bf16[1,512,14336]{2,1,0:T(8,128)(2,1)} %param.6) | copy-start | bytes 44040196
  17.9 22.5 %collective-permute-start.2 = (bf16[1024,256]{1,0:T(8,128)(2,1)S(1)}, bf16[1024,256]{1,0:T(8,128)(2,1)S(1)}, u32[]{:S(2)}, u32[]{:S(2)}) collective-permute-start(bf16[1024,256]{1,0:T(8,128)(2,1)S(1)} %slice_select_fusion.1), channel_id=1, source_target_pairs={{0,4},{4,0},{8,12},{12,8},{1,5},{5,1},{9,13},{13,9},{2,6},{6,2},{1... | collective-permute-start | bytes 1572872 | tf_op jit(solution)/shard_map/ppermute | solution.py:62
  28.4 13.1 %collective-permute-start.6 = (bf16[1024,256]{1,0:T(8,128)(2,1)S(1)}, bf16[1024,256]{1,0:T(8,128)(2,1)S(1)}, u32[]{:S(2)}, u32[]{:S(2)}) collective-permute-start(bf16[1024,256]{1,0:T(8,128)(2,1)S(1)} %slice.121), channel_id=1, source_target_pairs={{4,8},{8,4},{5,9},{9,5},{6,10},{10,6},{7,11},{11,7},{20,24},{24,20... | collective-permute-start | bytes 1572872 | tf_op jit(solution)/shard_map/ppermute | solution.py:62
  30.9 19.6 %collective-permute-start.8 = (bf16[1024,256]{1,0:T(8,128)(2,1)S(1)}, bf16[1024,256]{1,0:T(8,128)(2,1)S(1)}, u32[]{:S(2)}, u32[]{:S(2)}) collective-permute-start(bf16[1024,256]{1,0:T(8,128)(2,1)S(1)} %slice.122), channel_id=1, source_target_pairs={{4,8},{8,4},{5,9},{9,5},{6,10},{10,6},{7,11},{11,7},{20,24},{24,20... | collective-permute-start | bytes 1572872 | tf_op jit(solution)/shard_map/ppermute | solution.py:62
  31.7 21.1 %collective-permute-start.5 = (bf16[1024,256]{1,0:T(8,128)(2,1)S(1)}, bf16[1024,256]{1,0:T(8,128)(2,1)S(1)}, u32[]{:S(2)}, u32[]{:S(2)}) collective-permute-start(bf16[1024,256]{1,0:T(8,128)(2,1)S(1)} %slice_select_fusion), channel_id=1, source_target_pairs={{0,4},{4,0},{8,12},{12,8},{1,5},{5,1},{9,13},{13,9},{2,6},{6,2},{1... | collective-permute-start | bytes 1572872 | tf_op jit(solution)/shard_map/ppermute | solution.py:62
  41.7 21.9 %collective-permute-start.7 = (bf16[1024,256]{1,0:T(8,128)(2,1)S(1)}, bf16[1024,256]{1,0:T(8,128)(2,1)S(1)}, u32[]{:S(2)}, u32[]{:S(2)}) collective-permute-start(bf16[1024,256]{1,0:T(8,128)(2,1)S(1)} %maximum_select_fusion), channel_id=1, source_target_pairs={{0,4},{4,0},{8,12},{12,8},{1,5},{5,1},{9,13},{13,9},{2,6},{6,2},{1... | collective-permute-start | bytes 1572872 | tf_op jit(solution)/shard_map/ppermute | solution.py:62
  48.1 15.6 %collective-permute-start.10 = (bf16[1024,256]{1,0:T(8,128)(2,1)S(1)}, bf16[1024,256]{1,0:T(8,128)(2,1)S(1)}, u32[]{:S(2)}, u32[]{:S(2)}) collective-permute-start(bf16[1024,256]{1,0:T(8,128)(2,1)S(1)} %slice.135), channel_id=1, source_target_pairs={{4,8},{8,4},{5,9},{9,5},{6,10},{10,6},{7,11},{11,7},{20,24},{24,20... | collective-permute-start | bytes 1572872 | tf_op jit(solution)/shard_map/ppermute | solution.py:62
  50.5 23.9 %collective-permute-start.12 = (bf16[512,256]{1,0:T(8,128)(2,1)S(1)}, bf16[512,256]{1,0:T(8,128)(2,1)S(1)}, u32[]{:S(2)}, u32[]{:S(2)}) collective-permute-start(bf16[512,256]{1,0:T(8,128)(2,1)S(1)} %slice.137), channel_id=1, source_target_pairs={{4,8},{8,4},{5,9},{9,5},{6,10},{10,6},{7,11},{11,7},{20,24},{24,20... | collective-permute-start | bytes 786440 | tf_op jit(solution)/shard_map/ppermute | solution.py:62
  52.8 17.8 %copy-start.2 = (bf16[1,512,4096]{2,1,0:T(8,128)(2,1)S(1)}, bf16[1,512,4096]{2,1,0:T(8,128)(2,1)}, u32[]{:S(2)}) copy-start(bf16[1,512,4096]{2,1,0:T(8,128)(2,1)} %param.5) | copy-start | bytes 12582916
  53.0 22.2 %collective-permute-start.9 = (bf16[1024,256]{1,0:T(8,128)(2,1)S(1)}, bf16[1024,256]{1,0:T(8,128)(2,1)S(1)}, u32[]{:S(2)}, u32[]{:S(2)}) collective-permute-start(bf16[1024,256]{1,0:T(8,128)(2,1)S(1)} %maximum_select_fusion.1), channel_id=1, source_target_pairs={{0,4},{4,0},{8,12},{12,8},{1,5},{5,1},{9,13},{13,9},{2,6},{6,2},{1... | collective-permute-start | bytes 1572872 | tf_op jit(solution)/shard_map/ppermute | solution.py:62
  63.9 22.5 %collective-permute-start.11 = (bf16[1024,256]{1,0:T(8,128)(2,1)S(1)}, bf16[1024,256]{1,0:T(8,128)(2,1)S(1)}, u32[]{:S(2)}, u32[]{:S(2)}) collective-permute-start(bf16[1024,256]{1,0:T(8,128)(2,1)S(1)} %maximum_select_fusion.2), channel_id=1, source_target_pairs={{0,4},{4,0},{8,12},{12,8},{1,5},{5,1},{9,13},{13,9},{2,6},{6,2},{1... | collective-permute-start | bytes 1572872 | tf_op jit(solution)/shard_map/ppermute | solution.py:62
  71.5 9.6 %collective-permute-start.14 = (f32[512,256]{1,0:T(8,128)S(1)}, f32[512,256]{1,0:T(8,128)S(1)}, u32[]{:S(2)}, u32[]{:S(2)}) collective-permute-start(f32[512,256]{1,0:T(8,128)S(1)} %fusion.3), channel_id=1, source_target_pairs={{0,2},{2,0},{1,3},{3,1},{4,6},{6,4},{5,7},{7,5},{8,10},{10,8},{9,1... | collective-permute-start | bytes 1572872 | tf_op jit(solution)/shard_map/ppermute | solution.py:128
  73.1 13.4 %collective-permute-start.15 = (bf16[1024,256]{1,0:T(8,128)(2,1)S(1)}, bf16[1024,256]{1,0:T(8,128)(2,1)S(1)}, u32[]{:S(2)}, u32[]{:S(2)}) collective-permute-start(bf16[1024,256]{1,0:T(8,128)(2,1)S(1)} %collective-permute-done.4), channel_id=1, source_target_pairs={{4,8},{8,4},{5,9},{9,5},{6,10},{10,6},{7,11},{11,7},{20,24},{24,20... | collective-permute-start | bytes 1572872 | tf_op jit(solution)/shard_map/ppermute | solution.py:62
  74.5 22.9 %collective-permute-start.17 = (bf16[1024,256]{1,0:T(8,128)(2,1)S(1)}, bf16[1024,256]{1,0:T(8,128)(2,1)S(1)}, u32[]{:S(2)}, u32[]{:S(2)}) collective-permute-start(bf16[1024,256]{1,0:T(8,128)(2,1)S(1)} %collective-permute-done.2), channel_id=1, source_target_pairs={{4,8},{8,4},{5,9},{9,5},{6,10},{10,6},{7,11},{11,7},{20,24},{24,20... | collective-permute-start | bytes 1572872 | tf_op jit(solution)/shard_map/ppermute | solution.py:62
  75.2 20.9 %collective-permute-start.13 = (bf16[512,256]{1,0:T(8,128)(2,1)S(1)}, bf16[512,256]{1,0:T(8,128)(2,1)S(1)}, u32[]{:S(2)}, u32[]{:S(2)}) collective-permute-start(bf16[512,256]{1,0:T(8,128)(2,1)S(1)} %slice_select_fusion.2), channel_id=1, source_target_pairs={{0,4},{4,0},{8,12},{12,8},{1,5},{5,1},{9,13},{13,9},{2,6},{6,2},{1... | collective-permute-start | bytes 786440 | tf_op jit(solution)/shard_map/ppermute | solution.py:62
  86.6 16.6 %collective-permute-start.16 = (bf16[1024,256]{1,0:T(8,128)(2,1)S(1)}, bf16[1024,256]{1,0:T(8,128)(2,1)S(1)}, u32[]{:S(2)}, u32[]{:S(2)}) collective-permute-start(bf16[1024,256]{1,0:T(8,128)(2,1)S(1)} %maximum_select_fusion.3), channel_id=1, source_target_pairs={{0,4},{4,0},{8,12},{12,8},{1,5},{5,1},{9,13},{13,9},{2,6},{6,2},{1... | collective-permute-start | bytes 1572872 | tf_op jit(solution)/shard_map/ppermute | solution.py:62
  90.0 11.3 %collective-permute-start.19 = (bf16[1024,256]{1,0:T(8,128)(2,1)S(1)}, bf16[1024,256]{1,0:T(8,128)(2,1)S(1)}, u32[]{:S(2)}, u32[]{:S(2)}) collective-permute-start(bf16[1024,256]{1,0:T(8,128)(2,1)S(1)} %collective-permute-done.5), channel_id=1, source_target_pairs={{4,8},{8,4},{5,9},{9,5},{6,10},{10,6},{7,11},{11,7},{20,24},{24,20... | collective-permute-start | bytes 1572872 | tf_op jit(solution)/shard_map/ppermute | solution.py:62
  90.7 32.7 %collective-permute-start.21 = (f32[512,256]{1,0:T(8,128)S(1)}, f32[512,256]{1,0:T(8,128)S(1)}, u32[]{:S(2)}, u32[]{:S(2)}) collective-permute-start(f32[512,256]{1,0:T(8,128)S(1)} %add_multiply_fusion.2), channel_id=1, source_target_pairs={{0,4},{12,8},{1,5},{13,9},{2,6},{14,10},{3,7},{15,11},{16,20},{28,... | collective-permute-start | bytes 1572872 | tf_op jit(solution)/shard_map/ppermute | solution.py:130
  97.5 23.7 %collective-permute-start.18 = (bf16[1024,256]{1,0:T(8,128)(2,1)S(1)}, bf16[1024,256]{1,0:T(8,128)(2,1)S(1)}, u32[]{:S(2)}, u32[]{:S(2)}) collective-permute-start(bf16[1024,256]{1,0:T(8,128)(2,1)S(1)} %maximum_select_fusion.4), channel_id=1, source_target_pairs={{0,4},{4,0},{8,12},{12,8},{1,5},{5,1},{9,13},{13,9},{2,6},{6,2},{1... | collective-permute-start | bytes 1572872 | tf_op jit(solution)/shard_map/ppermute | solution.py:62
  101.3 19.9 %collective-permute-start.23 = (bf16[512,256]{1,0:T(8,128)(2,1)S(1)}, bf16[512,256]{1,0:T(8,128)(2,1)S(1)}, u32[]{:S(2)}, u32[]{:S(2)}) collective-permute-start(bf16[512,256]{1,0:T(8,128)(2,1)S(1)} %collective-permute-done.13), channel_id=1, source_target_pairs={{4,8},{8,4},{5,9},{9,5},{6,10},{10,6},{7,11},{11,7},{20,24},{24,20... | collective-permute-start | bytes 786440 | tf_op jit(solution)/shard_map/ppermute | solution.py:62
  104.2 25.5 %collective-permute-start.20 = (bf16[1024,256]{1,0:T(8,128)(2,1)S(1)}, bf16[1024,256]{1,0:T(8,128)(2,1)S(1)}, u32[]{:S(2)}, u32[]{:S(2)}) collective-permute-start(bf16[1024,256]{1,0:T(8,128)(2,1)S(1)} %collective-permute-done.19), channel_id=1, source_target_pairs={{4,0},{8,12},{5,1},{9,13},{6,2},{10,14},{7,3},{11,15},{20,16},{24,... | collective-permute-start | bytes 1572872 | tf_op jit(solution)/shard_map/ppermute | solution.py:62
  121.2 8.3 %collective-permute-start.24 = (bf16[512,256]{1,0:T(8,128)(2,1)S(1)}, bf16[512,256]{1,0:T(8,128)(2,1)S(1)}, u32[]{:S(2)}, u32[]{:S(2)}) collective-permute-start(bf16[512,256]{1,0:T(8,128)(2,1)S(1)} %collective-permute-done.23), channel_id=1, source_target_pairs={{4,0},{8,12},{5,1},{9,13},{6,2},{10,14},{7,3},{11,15},{20,16},{24,... | collective-permute-start | bytes 786440 | tf_op jit(solution)/shard_map/ppermute | solution.py:62
  123.5 6.7 %collective-permute-start.22 = (f32[2,256]{1,0:T(2,128)S(1)}, f32[2,256]{1,0:T(2,128)S(1)}, u32[]{:S(2)}, u32[]{:S(2)}) collective-permute-start(f32[2,256]{1,0:T(2,128)S(1)} %bitcast_reduce_fusion.1), channel_id=1, source_target_pairs={{4,0},{8,12},{5,1},{9,13},{6,2},{10,14},{7,3},{11,15},{20,16},{24,... | collective-permute-start | bytes 6152 | tf_op jit(solution)/shard_map/ppermute | solution.py:174
  130.6 3.6 %collective-permute-start.25 = (f32[2,32]{1,0:T(2,128)S(1)}, f32[2,32]{1,0:T(2,128)S(1)}, u32[]{:S(2)}, u32[]{:S(2)}) collective-permute-start(f32[2,32]{1,0:T(2,128)S(1)} %reduce_sum.29), channel_id=1, source_target_pairs={{0,2},{2,0},{1,3},{3,1},{4,6},{6,4},{5,7},{7,5},{8,10},{10,8},{9,1... | collective-permute-start | bytes 776 | tf_op jit(solution)/shard_map/ppermute | solution.py:180

commit v2 on v1

--- a/solution.py
+++ b/solution.py
@@ -119,7 +119,7 @@
     x["C1E"] = trade(either(guest(4, trade), y["C1E"]))
     y["C3E"] = across(after(x["C3M"], y["C2E"]))
     x["C2E"] = trade(trade.ready(y["C2E"]), TO_END)
-    x["C3E"] = trade(trade.ready(y["C3E"]), TO_END)
+    x["C3E"] = trade(y["C3E"], TO_END)
 
     proj_acts = dot(columns(after(acts, x["A"], y["AM"]), place, 0, unit), left)
     proj_acts += dot(columns(acts, near, 0, unit), x["A"])
@@ -127,7 +127,10 @@
     proj_acts += dot(columns(acts, far_end, 0, unit), either(x["AE"], y["AE"]))
     other_acts = lax.ppermute(proj_acts, "mp", [(0, 1), (1, 0)])
     masked = after((proj_acts + other_acts) * live_rows(seq_len, row_count))
-    guest_acts = lax.ppermute(masked, "dp", TO_MIDDLE)
+    by_seq = masked.reshape(seq_count, -1, masked.shape[1])
+    scale = jnp.maximum(jnp.max(jnp.abs(by_seq), axis=1, keepdims=True), 1e-30) / 32767
+    coded = jnp.round(by_seq / scale).astype(jnp.int16).reshape(masked.shape)
+    guest_acts = lax.ppermute(coded, "dp", TO_MIDDLE)
 
     def near_term(name, got):
         if name != "B":
@@ -171,7 +174,7 @@
     proj_grads, guest_grads = lax.optimization_barrier((proj_grads, guest_grads))
     proj_grads += end_term("C1")
     guest_grads += guest_term(4, x["C1E"])
-    guest_scores = lax.ppermute(column_scores(guest_acts, guest_grads, seq_count), "dp", TO_END)
+    guest_scores = lax.ppermute(column_scores(guest_acts.astype(jnp.float32), guest_grads, seq_count), "dp", TO_END) * scale[:, 0]
 
     proj_grads = after(proj_grads)
     proj_grads = after(proj_grads + end_term("C2"), guest_scores)

time: 135 us -> 133 us (0.985)
  waiting for transfers between devices: 35.9 us -> 33.3 us
    ppermute x22, waiting for transfers between devices: 33.6 us -> 25.7 us  [__call__(): self.came.append(lax.ppermute(x, 'dp', pairs or self.pairs))]
    ppermute x2, waiting for transfers between devices: 0.01 us -> 5.52 us  [the longest x1 5.52 us: on_line(): lax.ppermute(column_scores(guest_acts.astype(jnp.float32), guest_grads, s...]
  transfers between devices with their start and end apart: 26 -> 26, of which waited for: 8 -> 9; matrix products, arithmetic and copies ran while one was open for 15% -> 15% of each run, Pallas kernels for 0% -> 0%
where the time goes in v2:
time: 133 us; the launch traced here: 132 us
  starting transfers between devices  76.8 us (58%)
  waiting for transfers between devices  33.3 us (25%)
  matrix products  14 us (11%)
  other arithmetic  4 us (3%)
  local copies, waits for them, and re-layouts  3.47 us (3%)
    ppermute x22, starting transfers between devices, __call__(): self.came.append(lax.ppermute(x, 'dp', pairs or self.pairs))  67.4 us
    ppermute x22, waiting for transfers between devices, __call__(): self.came.append(lax.ppermute(x, 'dp', pairs or self.pairs))  25.7 us
    dot_general x27, matrix products, dot(): return jnp.dot(a, b, preferred_element_type=jnp.float32)  14 us
    ppermute x1, waiting for transfers between devices, on_line(): lax.ppermute(column_scores(guest_acts.astype(jnp.float32), guest_grads, s...  5.52 us
    ppermute x1, starting transfers between devices, on_line(): guest_acts = lax.ppermute(coded, 'dp', TO_MIDDLE)  4.9 us
  transfers between devices with their start and end apart: 26, of which 9 were waited for; matrix products, arithmetic and copies ran while one was open for 15% of the time, Pallas kernels for 0%

profile of v2, /device:TPU:0, one launch (start us, length us, event | category | flops | bytes accessed | tf_op | source)
XLA Modules:
  0.0 132.2 jit_solution(11230179970085057073)
XLA Ops:
  0.0 3.0 %collective-permute-start = (bf16[1024,256]{1,0:T(8,128)(2,1)}, bf16[1024,256]{1,0:T(8,128)(2,1)S(1)}, u32[]{:S(2)}, u32[]{:S(2)}) collective-permute-start(bf16[1024,256]{1,0:T(8,128)(2,1)} %bitcast.124), channel_id=1, source_target_pairs={{0,4},{4,0},{8,12},{12,8},{1,5},{5,1},{9,13},{13,9},{2,6},{6,2},{1... | collective-permute-start | bytes 1572872 | tf_op jit(solution)/shard_map/ppermute | solution.py:62
  3.0 0.7 collective-permute-start.1
  3.7 1.9 %slice_bitcast_fusion = bf16[1024,256]{1,0:T(8,128)(2,1)} fusion(bf16[1,3584,256]{2,1,0:T(8,128)(2,1)} %param.8), kind=kLoop, calls=%fused_computation.87 | loop fusion | bytes 1048576 | tf_op jit(solution)/shard_map/slice | solution.py:103
  5.6 4.4 %collective-permute-start.4 = (bf16[1024,256]{1,0:T(8,128)(2,1)}, bf16[1024,256]{1,0:T(8,128)(2,1)S(1)}, u32[]{:S(2)}, u32[]{:S(2)}) collective-permute-start(bf16[1024,256]{1,0:T(8,128)(2,1)} %slice_bitcast_fusion), channel_id=1, source_target_pairs={{0,4},{4,0},{8,12},{12,8},{1,5},{5,1},{9,13},{13,9},{2,6},{6,2},{1... | collective-permute-start | bytes 1572872 | tf_op jit(solution)/shard_map/ppermute | solution.py:62
  10.0 0.7 fusion.143
  10.7 5.3 %collective-permute-done = bf16[1024,256]{1,0:T(8,128)(2,1)S(1)} collective-permute-done((bf16[1024,256]{1,0:T(8,128)(2,1)}, bf16[1024,256]{1,0:T(8,128)(2,1)S(1)}, u32[]{:S(2)}, u32[]{:S(2)}) %collective-permute-start) | collective-permute-done | bytes 524320 | tf_op jit(solution)/shard_map/ppermute | solution.py:62
  16.0 0.7 collective-permute-start.3
  16.7 1.3 slice_select_fusion.1
  17.9 6.9 %collective-permute-start.2 = (bf16[1024,256]{1,0:T(8,128)(2,1)S(1)}, bf16[1024,256]{1,0:T(8,128)(2,1)S(1)}, u32[]{:S(2)}, u32[]{:S(2)}) collective-permute-start(bf16[1024,256]{1,0:T(8,128)(2,1)S(1)} %slice_select_fusion.1), channel_id=1, source_target_pairs={{0,4},{4,0},{8,12},{12,8},{1,5},{5,1},{9,13},{13,9},{2,6},{6,2},{1... | collective-permute-start | bytes 1572872 | tf_op jit(solution)/shard_map/ppermute | solution.py:62
  24.9 1.7 %fusion.16 = f32[512,256]{1,0:T(8,128)S(1)} fusion(bf16[1024,256]{1,0:T(8,128)(2,1)S(1)} %collective-permute-done, bf16[1,512,4096]{2,1,0:T(8,128)(2,1)} %param.5, s32[]{:T(128)S(6)} %select_n.204), kind=kOutput, calls=%fused_computation.27 | convolution fusion | flops 268435456 | bytes 2097156 | tf_op jit(solution)/shard_map/dot_general | solution.py:36
  26.6 1.8 %convolution_add_fusion.3 = f32[512,256]{1,0:T(8,128)S(1)} fusion(f32[512,256]{1,0:T(8,128)S(1)} %fusion.16, bf16[512,4096]{1,0:T(8,128)(2,1)} %bitcast.123, s32[]{:T(128)S(6)} %select_n.203, bf16[1,1024,256]{2,1,0:T(8,128)(2,1)} %param.7), kind=kOutput, calls=%fused_computation.5 | convolution fusion | flops 268566528 | bytes 2621444 | tf_op jit(solution)/shard_map/dot_general | solution.py:36
  28.4 0.7 collective-permute-start.6
  29.2 1.7 %fusion.27 = f32[512,256]{1,0:T(8,128)S(1)} fusion(bf16[1024,256]{1,0:T(8,128)(2,1)S(1)} %collective-permute-done.4, bf16[1,512,14336]{2,1,0:T(8,128)(2,1)} %param.6, s32[]{:T(128)S(6)} %select_n.178), kind=kOutput, calls=%fused_computation.38 | convolution fusion | flops 268435456 | bytes 2097156 | tf_op jit(solution)/shard_map/dot_general | solution.py:36
  30.9 0.7 collective-permute-start.8
  31.7 8.8 %collective-permute-start.5 = (bf16[1024,256]{1,0:T(8,128)(2,1)S(1)}, bf16[1024,256]{1,0:T(8,128)(2,1)S(1)}, u32[]{:S(2)}, u32[]{:S(2)}) collective-permute-start(bf16[1024,256]{1,0:T(8,128)(2,1)S(1)} %slice_select_fusion), channel_id=1, source_target_pairs={{0,4},{4,0},{8,12},{12,8},{1,5},{5,1},{9,13},{13,9},{2,6},{6,2},{1... | collective-permute-start | bytes 1572872 | tf_op jit(solution)/shard_map/ppermute | solution.py:62
  40.5 1.1 constant_dynamic-slice_fusion.9
  41.7 6.4 %collective-permute-start.7 = (bf16[1024,256]{1,0:T(8,128)(2,1)S(1)}, bf16[1024,256]{1,0:T(8,128)(2,1)S(1)}, u32[]{:S(2)}, u32[]{:S(2)}) collective-permute-start(bf16[1024,256]{1,0:T(8,128)(2,1)S(1)} %maximum_select_fusion), channel_id=1, source_target_pairs={{0,4},{4,0},{8,12},{12,8},{1,5},{5,1},{9,13},{13,9},{2,6},{6,2},{1... | collective-permute-start | bytes 1572872 | tf_op jit(solution)/shard_map/ppermute | solution.py:62
  48.1 0.7 collective-permute-start.10
  48.9 0.5 fusion.25
  49.3 1.1 fusion
  50.5 0.7 collective-permute-start.12
  51.2 1.5 %collective-permute-done.5 = bf16[1024,256]{1,0:T(8,128)(2,1)S(1)} collective-permute-done((bf16[1024,256]{1,0:T(8,128)(2,1)S(1)}, bf16[1024,256]{1,0:T(8,128)(2,1)S(1)}, u32[]{:S(2)}, u32[]{:S(2)}) %collective-permute-start.5) | collective-permute-done | bytes 524320 | tf_op jit(solution)/shard_map/ppermute | solution.py:62
  53.0 10.2 %collective-permute-start.9 = (bf16[1024,256]{1,0:T(8,128)(2,1)S(1)}, bf16[1024,256]{1,0:T(8,128)(2,1)S(1)}, u32[]{:S(2)}, u32[]{:S(2)}) collective-permute-start(bf16[1024,256]{1,0:T(8,128)(2,1)S(1)} %maximum_select_fusion.1), channel_id=1, source_target_pairs={{0,4},{4,0},{8,12},{12,8},{1,5},{5,1},{9,13},{13,9},{2,6},{6,2},{1... | collective-permute-start | bytes 1572872 | tf_op jit(solution)/shard_map/ppermute | solution.py:62
  63.2 0.5 add_add_fusion.1
  63.9 6.7 %collective-permute-start.11 = (bf16[1024,256]{1,0:T(8,128)(2,1)S(1)}, bf16[1024,256]{1,0:T(8,128)(2,1)S(1)}, u32[]{:S(2)}, u32[]{:S(2)}) collective-permute-start(bf16[1024,256]{1,0:T(8,128)(2,1)S(1)} %maximum_select_fusion.2), channel_id=1, source_target_pairs={{0,4},{4,0},{8,12},{12,8},{1,5},{5,1},{9,13},{13,9},{2,6},{6,2},{1... | collective-permute-start | bytes 1572872 | tf_op jit(solution)/shard_map/ppermute | solution.py:62
  70.6 0.4 fusion.13
  71.0 0.5 fusion.3
  71.5 1.6 %collective-permute-start.14 = (f32[512,256]{1,0:T(8,128)S(1)}, f32[512,256]{1,0:T(8,128)S(1)}, u32[]{:S(2)}, u32[]{:S(2)}) collective-permute-start(f32[512,256]{1,0:T(8,128)S(1)} %fusion.3), channel_id=1, source_target_pairs={{0,2},{2,0},{1,3},{3,1},{4,6},{6,4},{5,7},{7,5},{8,10},{10,8},{9,1... | collective-permute-start | bytes 1572872 | tf_op jit(solution)/shard_map/ppermute | solution.py:128
  73.1 0.7 collective-permute-start.15
  74.0 0.4 fusion.21
  74.5 0.7 collective-permute-start.17
  75.2 4.5 %collective-permute-start.13 = (bf16[512,256]{1,0:T(8,128)(2,1)S(1)}, bf16[512,256]{1,0:T(8,128)(2,1)S(1)}, u32[]{:S(2)}, u32[]{:S(2)}) collective-permute-start(bf16[512,256]{1,0:T(8,128)(2,1)S(1)} %slice_select_fusion.2), channel_id=1, source_target_pairs={{0,4},{4,0},{8,12},{12,8},{1,5},{5,1},{9,13},{13,9},{2,6},{6,2},{1... | collective-permute-start | bytes 786440 | tf_op jit(solution)/shard_map/ppermute | solution.py:62
  79.8 0.2 fusion.91
  80.0 0.5 add_add_fusion
  80.5 0.2 convolution_add_fusion.8
  80.7 0.2 fusion.6
  81.3 5.2 %collective-permute-done.11 = bf16[1024,256]{1,0:T(8,128)(2,1)S(1)} collective-permute-done((bf16[1024,256]{1,0:T(8,128)(2,1)S(1)}, bf16[1024,256]{1,0:T(8,128)(2,1)S(1)}, u32[]{:S(2)}, u32[]{:S(2)}) %collective-permute-start.11) | collective-permute-done | bytes 524320 | tf_op jit(solution)/shard_map/ppermute | solution.py:62
  86.7 3.4 %collective-permute-start.16 = (bf16[1024,256]{1,0:T(8,128)(2,1)S(1)}, bf16[1024,256]{1,0:T(8,128)(2,1)S(1)}, u32[]{:S(2)}, u32[]{:S(2)}) collective-permute-start(bf16[1024,256]{1,0:T(8,128)(2,1)S(1)} %maximum_select_fusion.3), channel_id=1, source_target_pairs={{0,4},{4,0},{8,12},{12,8},{1,5},{5,1},{9,13},{13,9},{2,6},{6,2},{1... | collective-permute-start | bytes 1572872 | tf_op jit(solution)/shard_map/ppermute | solution.py:62
  90.0 0.7 collective-permute-start.19
  90.9 4.9 %collective-permute-start.21 = (s16[512,256]{1,0:T(8,128)(2,1)S(1)}, s16[512,256]{1,0:T(8,128)(2,1)S(1)}, u32[]{:S(2)}, u32[]{:S(2)}) collective-permute-start(s16[512,256]{1,0:T(8,128)(2,1)S(1)} %fusion.46), channel_id=1, source_target_pairs={{0,4},{12,8},{1,5},{13,9},{2,6},{14,10},{3,7},{15,11},{16,20},{28,... | collective-permute-start | bytes 786440 | tf_op jit(solution)/shard_map/ppermute | solution.py:133
  96.0 0.2 fusion.5
  96.3 0.3 fusion.49
  96.6 0.3 fusion.47
  96.9 0.5 fusion.7
  97.6 3.7 %collective-permute-start.18 = (bf16[1024,256]{1,0:T(8,128)(2,1)S(1)}, bf16[1024,256]{1,0:T(8,128)(2,1)S(1)}, u32[]{:S(2)}, u32[]{:S(2)}) collective-permute-start(bf16[1024,256]{1,0:T(8,128)(2,1)S(1)} %maximum_select_fusion.4), channel_id=1, source_target_pairs={{0,4},{4,0},{8,12},{12,8},{1,5},{5,1},{9,13},{13,9},{2,6},{6,2},{1... | collective-permute-start | bytes 1572872 | tf_op jit(solution)/shard_map/ppermute | solution.py:62
  101.3 2.0 %collective-permute-done.16 = bf16[1024,256]{1,0:T(8,128)(2,1)S(1)} collective-permute-done((bf16[1024,256]{1,0:T(8,128)(2,1)S(1)}, bf16[1024,256]{1,0:T(8,128)(2,1)S(1)}, u32[]{:S(2)}, u32[]{:S(2)}) %collective-permute-start.16) | collective-permute-done | bytes 524320 | tf_op jit(solution)/shard_map/ppermute | solution.py:62
  103.3 0.2 fusion.85
  103.5 0.2 fusion.4
  103.8 0.5 convolution_add_fusion.1
  104.2 1.3 collective-permute-start.20
  105.5 0.7 collective-permute-start.23
  106.2 9.3 %collective-permute-done.18 = bf16[1024,256]{1,0:T(8,128)(2,1)S(1)} collective-permute-done((bf16[1024,256]{1,0:T(8,128)(2,1)S(1)}, bf16[1024,256]{1,0:T(8,128)(2,1)S(1)}, u32[]{:S(2)}, u32[]{:S(2)}) %collective-permute-start.18) | collective-permute-done | bytes 524320 | tf_op jit(solution)/shard_map/ppermute | solution.py:62
  115.5 0.2 fusion.82
  115.8 0.2 convolution_add_fusion.5
  116.2 1.3 collective-permute-start.22
  117.5 0.4 convolution_add_fusion
  117.9 1.3 collective-permute-start.24
  119.2 5.5 %collective-permute-done.22 = f32[2,256]{1,0:T(2,128)S(1)} collective-permute-done((f32[2,256]{1,0:T(2,128)S(1)}, f32[2,256]{1,0:T(2,128)S(1)}, u32[]{:S(2)}, u32[]{:S(2)}) %collective-permute-start.22) | collective-permute-done | bytes 2080 | tf_op jit(solution)/shard_map/ppermute | solution.py:177
  124.8 0.4 fusion.9
  125.3 2.3 %collective-permute-done.24 = bf16[512,256]{1,0:T(8,128)(2,1)S(1)} collective-permute-done((bf16[512,256]{1,0:T(8,128)(2,1)S(1)}, bf16[512,256]{1,0:T(8,128)(2,1)S(1)}, u32[]{:S(2)}, u32[]{:S(2)}) %collective-permute-start.24) | collective-permute-done | bytes 262176 | tf_op jit(solution)/shard_map/ppermute | solution.py:62
  127.6 0.3 bitcast_reduce_fusion
  128.1 1.7 %collective-permute-start.25 = (f32[2,32]{1,0:T(2,128)S(1)}, f32[2,32]{1,0:T(2,128)S(1)}, u32[]{:S(2)}, u32[]{:S(2)}) collective-permute-start(f32[2,32]{1,0:T(2,128)S(1)} %reduce_sum.29), channel_id=1, source_target_pairs={{0,2},{2,0},{1,3},{3,1},{4,6},{6,4},{5,7},{7,5},{8,10},{10,8},{9,1... | collective-permute-start | bytes 776 | tf_op jit(solution)/shard_map/ppermute | solution.py:183
  129.7 1.9 %collective-permute-done.25 = f32[2,32]{1,0:T(2,128)S(1)} collective-permute-done((f32[2,32]{1,0:T(2,128)S(1)}, f32[2,32]{1,0:T(2,128)S(1)}, u32[]{:S(2)}, u32[]{:S(2)}) %collective-permute-start.25) | collective-permute-done | bytes 288 | tf_op jit(solution)/shard_map/ppermute | solution.py:183
  131.6 0.6 multiply_bitcast_fusion
  (53 shorter events, 2.7 us)
Async XLA Ops:
  0.0 28.4 %copy-start = (bf16[1,3584,256]{2,1,0:T(8,128)(2,1)S(1)}, bf16[1,3584,256]{2,1,0:T(8,128)(2,1)}, u32[]{:S(2)}) copy-start(bf16[1,3584,256]{2,1,0:T(8,128)(2,1)} %param.8) | copy-start | bytes 5505028
  0.0 16.0 %collective-permute-start = (bf16[1024,256]{1,0:T(8,128)(2,1)}, bf16[1024,256]{1,0:T(8,128)(2,1)S(1)}, u32[]{:S(2)}, u32[]{:S(2)}) collective-permute-start(bf16[1024,256]{1,0:T(8,128)(2,1)} %bitcast.124), channel_id=1, source_target_pairs={{0,4},{4,0},{8,12},{12,8},{1,5},{5,1},{9,13},{13,9},{2,6},{6,2},{1... | collective-permute-start | bytes 1572872 | tf_op jit(solution)/shard_map/ppermute | solution.py:62
  3.0 13.0 %collective-permute-start.1 = (bf16[1024,256]{1,0:T(8,128)(2,1)}, bf16[1024,256]{1,0:T(8,128)(2,1)S(1)}, u32[]{:S(2)}, u32[]{:S(2)}) collective-permute-start(bf16[1024,256]{1,0:T(8,128)(2,1)} %bitcast.125), channel_id=1, source_target_pairs={{4,8},{8,4},{5,9},{9,5},{6,10},{10,6},{7,11},{11,7},{20,24},{24,20... | collective-permute-start | bytes 1572872 | tf_op jit(solution)/shard_map/ppermute | solution.py:62
  5.6 22.8 %collective-permute-start.4 = (bf16[1024,256]{1,0:T(8,128)(2,1)}, bf16[1024,256]{1,0:T(8,128)(2,1)S(1)}, u32[]{:S(2)}, u32[]{:S(2)}) collective-permute-start(bf16[1024,256]{1,0:T(8,128)(2,1)} %slice_bitcast_fusion), channel_id=1, source_target_pairs={{0,4},{4,0},{8,12},{12,8},{1,5},{5,1},{9,13},{13,9},{2,6},{6,2},{1... | collective-permute-start | bytes 1572872 | tf_op jit(solution)/shard_map/ppermute | solution.py:62
  16.0 14.8 %collective-permute-start.3 = (bf16[1024,256]{1,0:T(8,128)(2,1)S(1)}, bf16[1024,256]{1,0:T(8,128)(2,1)S(1)}, u32[]{:S(2)}, u32[]{:S(2)}) collective-permute-start(bf16[1024,256]{1,0:T(8,128)(2,1)S(1)} %collective-permute-done), channel_id=1, source_target_pairs={{4,8},{8,4},{5,9},{9,5},{6,10},{10,6},{7,11},{11,7},{20,24},{24,20... | collective-permute-start | bytes 1572872 | tf_op jit(solution)/shard_map/ppermute | solution.py:62
  16.7 32.2 %copy-start.1 = (bf16[1,512,14336]{2,1,0:T(8,128)(2,1)S(1)}, bf16[1,512,14336]{2,1,0:T(8,128)(2,1)}, u32[]{:S(2)}) copy-start(bf16[1,512,14336]{2,1,0:T(8,128)(2,1)} %param.6) | copy-start | bytes 44040196
  17.9 22.5 %collective-permute-start.2 = (bf16[1024,256]{1,0:T(8,128)(2,1)S(1)}, bf16[1024,256]{1,0:T(8,128)(2,1)S(1)}, u32[]{:S(2)}, u32[]{:S(2)}) collective-permute-start(bf16[1024,256]{1,0:T(8,128)(2,1)S(1)} %slice_select_fusion.1), channel_id=1, source_target_pairs={{0,4},{4,0},{8,12},{12,8},{1,5},{5,1},{9,13},{13,9},{2,6},{6,2},{1... | collective-permute-start | bytes 1572872 | tf_op jit(solution)/shard_map/ppermute | solution.py:62
  28.4 13.1 %collective-permute-start.6 = (bf16[1024,256]{1,0:T(8,128)(2,1)S(1)}, bf16[1024,256]{1,0:T(8,128)(2,1)S(1)}, u32[]{:S(2)}, u32[]{:S(2)}) collective-permute-start(bf16[1024,256]{1,0:T(8,128)(2,1)S(1)} %slice.121), channel_id=1, source_target_pairs={{4,8},{8,4},{5,9},{9,5},{6,10},{10,6},{7,11},{11,7},{20,24},{24,20... | collective-permute-start | bytes 1572872 | tf_op jit(solution)/shard_map/ppermute | solution.py:62
  30.9 19.6 %collective-permute-start.8 = (bf16[1024,256]{1,0:T(8,128)(2,1)S(1)}, bf16[1024,256]{1,0:T(8,128)(2,1)S(1)}, u32[]{:S(2)}, u32[]{:S(2)}) collective-permute-start(bf16[1024,256]{1,0:T(8,128)(2,1)S(1)} %slice.122), channel_id=1, source_target_pairs={{4,8},{8,4},{5,9},{9,5},{6,10},{10,6},{7,11},{11,7},{20,24},{24,20... | collective-permute-start | bytes 1572872 | tf_op jit(solution)/shard_map/ppermute | solution.py:62
  31.7 21.1 %collective-permute-start.5 = (bf16[1024,256]{1,0:T(8,128)(2,1)S(1)}, bf16[1024,256]{1,0:T(8,128)(2,1)S(1)}, u32[]{:S(2)}, u32[]{:S(2)}) collective-permute-start(bf16[1024,256]{1,0:T(8,128)(2,1)S(1)} %slice_select_fusion), channel_id=1, source_target_pairs={{0,4},{4,0},{8,12},{12,8},{1,5},{5,1},{9,13},{13,9},{2,6},{6,2},{1... | collective-permute-start | bytes 1572872 | tf_op jit(solution)/shard_map/ppermute | solution.py:62
  41.7 21.9 %collective-permute-start.7 = (bf16[1024,256]{1,0:T(8,128)(2,1)S(1)}, bf16[1024,256]{1,0:T(8,128)(2,1)S(1)}, u32[]{:S(2)}, u32[]{:S(2)}) collective-permute-start(bf16[1024,256]{1,0:T(8,128)(2,1)S(1)} %maximum_select_fusion), channel_id=1, source_target_pairs={{0,4},{4,0},{8,12},{12,8},{1,5},{5,1},{9,13},{13,9},{2,6},{6,2},{1... | collective-permute-start | bytes 1572872 | tf_op jit(solution)/shard_map/ppermute | solution.py:62
  48.1 15.6 %collective-permute-start.10 = (bf16[1024,256]{1,0:T(8,128)(2,1)S(1)}, bf16[1024,256]{1,0:T(8,128)(2,1)S(1)}, u32[]{:S(2)}, u32[]{:S(2)}) collective-permute-start(bf16[1024,256]{1,0:T(8,128)(2,1)S(1)} %slice.135), channel_id=1, source_target_pairs={{4,8},{8,4},{5,9},{9,5},{6,10},{10,6},{7,11},{11,7},{20,24},{24,20... | collective-permute-start | bytes 1572872 | tf_op jit(solution)/shard_map/ppermute | solution.py:62
  50.5 23.9 %collective-permute-start.12 = (bf16[512,256]{1,0:T(8,128)(2,1)S(1)}, bf16[512,256]{1,0:T(8,128)(2,1)S(1)}, u32[]{:S(2)}, u32[]{:S(2)}) collective-permute-start(bf16[512,256]{1,0:T(8,128)(2,1)S(1)} %slice.137), channel_id=1, source_target_pairs={{4,8},{8,4},{5,9},{9,5},{6,10},{10,6},{7,11},{11,7},{20,24},{24,20... | collective-permute-start | bytes 786440 | tf_op jit(solution)/shard_map/ppermute | solution.py:62
  52.8 17.8 %copy-start.2 = (bf16[1,512,4096]{2,1,0:T(8,128)(2,1)S(1)}, bf16[1,512,4096]{2,1,0:T(8,128)(2,1)}, u32[]{:S(2)}) copy-start(bf16[1,512,4096]{2,1,0:T(8,128)(2,1)} %param.5) | copy-start | bytes 12582916
  53.0 22.2 %collective-permute-start.9 = (bf16[1024,256]{1,0:T(8,128)(2,1)S(1)}, bf16[1024,256]{1,0:T(8,128)(2,1)S(1)}, u32[]{:S(2)}, u32[]{:S(2)}) collective-permute-start(bf16[1024,256]{1,0:T(8,128)(2,1)S(1)} %maximum_select_fusion.1), channel_id=1, source_target_pairs={{0,4},{4,0},{8,12},{12,8},{1,5},{5,1},{9,13},{13,9},{2,6},{6,2},{1... | collective-permute-start | bytes 1572872 | tf_op jit(solution)/shard_map/ppermute | solution.py:62
  63.9 22.5 %collective-permute-start.11 = (bf16[1024,256]{1,0:T(8,128)(2,1)S(1)}, bf16[1024,256]{1,0:T(8,128)(2,1)S(1)}, u32[]{:S(2)}, u32[]{:S(2)}) collective-permute-start(bf16[1024,256]{1,0:T(8,128)(2,1)S(1)} %maximum_select_fusion.2), channel_id=1, source_target_pairs={{0,4},{4,0},{8,12},{12,8},{1,5},{5,1},{9,13},{13,9},{2,6},{6,2},{1... | collective-permute-start | bytes 1572872 | tf_op jit(solution)/shard_map/ppermute | solution.py:62
  71.5 9.6 %collective-permute-start.14 = (f32[512,256]{1,0:T(8,128)S(1)}, f32[512,256]{1,0:T(8,128)S(1)}, u32[]{:S(2)}, u32[]{:S(2)}) collective-permute-start(f32[512,256]{1,0:T(8,128)S(1)} %fusion.3), channel_id=1, source_target_pairs={{0,2},{2,0},{1,3},{3,1},{4,6},{6,4},{5,7},{7,5},{8,10},{10,8},{9,1... | collective-permute-start | bytes 1572872 | tf_op jit(solution)/shard_map/ppermute | solution.py:128
  73.1 13.4 %collective-permute-start.15 = (bf16[1024,256]{1,0:T(8,128)(2,1)S(1)}, bf16[1024,256]{1,0:T(8,128)(2,1)S(1)}, u32[]{:S(2)}, u32[]{:S(2)}) collective-permute-start(bf16[1024,256]{1,0:T(8,128)(2,1)S(1)} %collective-permute-done.4), channel_id=1, source_target_pairs={{4,8},{8,4},{5,9},{9,5},{6,10},{10,6},{7,11},{11,7},{20,24},{24,20... | collective-permute-start | bytes 1572872 | tf_op jit(solution)/shard_map/ppermute | solution.py:62
  74.5 23.0 %collective-permute-start.17 = (bf16[1024,256]{1,0:T(8,128)(2,1)S(1)}, bf16[1024,256]{1,0:T(8,128)(2,1)S(1)}, u32[]{:S(2)}, u32[]{:S(2)}) collective-permute-start(bf16[1024,256]{1,0:T(8,128)(2,1)S(1)} %collective-permute-done.2), channel_id=1, source_target_pairs={{4,8},{8,4},{5,9},{9,5},{6,10},{10,6},{7,11},{11,7},{20,24},{24,20... | collective-permute-start | bytes 1572872 | tf_op jit(solution)/shard_map/ppermute | solution.py:62
  75.2 21.0 %collective-permute-start.13 = (bf16[512,256]{1,0:T(8,128)(2,1)S(1)}, bf16[512,256]{1,0:T(8,128)(2,1)S(1)}, u32[]{:S(2)}, u32[]{:S(2)}) collective-permute-start(bf16[512,256]{1,0:T(8,128)(2,1)S(1)} %slice_select_fusion.2), channel_id=1, source_target_pairs={{0,4},{4,0},{8,12},{12,8},{1,5},{5,1},{9,13},{13,9},{2,6},{6,2},{1... | collective-permute-start | bytes 786440 | tf_op jit(solution)/shard_map/ppermute | solution.py:62
  86.7 16.6 %collective-permute-start.16 = (bf16[1024,256]{1,0:T(8,128)(2,1)S(1)}, bf16[1024,256]{1,0:T(8,128)(2,1)S(1)}, u32[]{:S(2)}, u32[]{:S(2)}) collective-permute-start(bf16[1024,256]{1,0:T(8,128)(2,1)S(1)} %maximum_select_fusion.3), channel_id=1, source_target_pairs={{0,4},{4,0},{8,12},{12,8},{1,5},{5,1},{9,13},{13,9},{2,6},{6,2},{1... | collective-permute-start | bytes 1572872 | tf_op jit(solution)/shard_map/ppermute | solution.py:62
  90.0 14.2 %collective-permute-start.19 = (bf16[1024,256]{1,0:T(8,128)(2,1)S(1)}, bf16[1024,256]{1,0:T(8,128)(2,1)S(1)}, u32[]{:S(2)}, u32[]{:S(2)}) collective-permute-start(bf16[1024,256]{1,0:T(8,128)(2,1)S(1)} %collective-permute-done.5), channel_id=1, source_target_pairs={{4,8},{8,4},{5,9},{9,5},{6,10},{10,6},{7,11},{11,7},{20,24},{24,20... | collective-permute-start | bytes 1572872 | tf_op jit(solution)/shard_map/ppermute | solution.py:62
  90.9 25.1 %collective-permute-start.21 = (s16[512,256]{1,0:T(8,128)(2,1)S(1)}, s16[512,256]{1,0:T(8,128)(2,1)S(1)}, u32[]{:S(2)}, u32[]{:S(2)}) collective-permute-start(s16[512,256]{1,0:T(8,128)(2,1)S(1)} %fusion.46), channel_id=1, source_target_pairs={{0,4},{12,8},{1,5},{13,9},{2,6},{14,10},{3,7},{15,11},{16,20},{28,... | collective-permute-start | bytes 786440 | tf_op jit(solution)/shard_map/ppermute | solution.py:133
  97.6 17.9 %collective-permute-start.18 = (bf16[1024,256]{1,0:T(8,128)(2,1)S(1)}, bf16[1024,256]{1,0:T(8,128)(2,1)S(1)}, u32[]{:S(2)}, u32[]{:S(2)}) collective-permute-start(bf16[1024,256]{1,0:T(8,128)(2,1)S(1)} %maximum_select_fusion.4), channel_id=1, source_target_pairs={{0,4},{4,0},{8,12},{12,8},{1,5},{5,1},{9,13},{13,9},{2,6},{6,2},{1... | collective-permute-start | bytes 1572872 | tf_op jit(solution)/shard_map/ppermute | solution.py:62
  104.2 20.5 %collective-permute-start.20 = (bf16[1024,256]{1,0:T(8,128)(2,1)S(1)}, bf16[1024,256]{1,0:T(8,128)(2,1)S(1)}, u32[]{:S(2)}, u32[]{:S(2)}) collective-permute-start(bf16[1024,256]{1,0:T(8,128)(2,1)S(1)} %collective-permute-done.19), channel_id=1, source_target_pairs={{4,0},{8,12},{5,1},{9,13},{6,2},{10,14},{7,3},{11,15},{20,16},{24,... | collective-permute-start | bytes 1572872 | tf_op jit(solution)/shard_map/ppermute | solution.py:62
  105.5 12.4 %collective-permute-start.23 = (bf16[512,256]{1,0:T(8,128)(2,1)S(1)}, bf16[512,256]{1,0:T(8,128)(2,1)S(1)}, u32[]{:S(2)}, u32[]{:S(2)}) collective-permute-start(bf16[512,256]{1,0:T(8,128)(2,1)S(1)} %collective-permute-done.13), channel_id=1, source_target_pairs={{4,8},{8,4},{5,9},{9,5},{6,10},{10,6},{7,11},{11,7},{20,24},{24,20... | collective-permute-start | bytes 786440 | tf_op jit(solution)/shard_map/ppermute | solution.py:62
  116.2 8.6 %collective-permute-start.22 = (f32[2,256]{1,0:T(2,128)S(1)}, f32[2,256]{1,0:T(2,128)S(1)}, u32[]{:S(2)}, u32[]{:S(2)}) collective-permute-start(f32[2,256]{1,0:T(2,128)S(1)} %bitcast_reduce_fusion.1), channel_id=1, source_target_pairs={{4,0},{8,12},{5,1},{9,13},{6,2},{10,14},{7,3},{11,15},{20,16},{24,... | collective-permute-start | bytes 6152 | tf_op jit(solution)/shard_map/ppermute | solution.py:177
  117.9 9.6 %collective-permute-start.24 = (bf16[512,256]{1,0:T(8,128)(2,1)S(1)}, bf16[512,256]{1,0:T(8,128)(2,1)S(1)}, u32[]{:S(2)}, u32[]{:S(2)}) collective-permute-start(bf16[512,256]{1,0:T(8,128)(2,1)S(1)} %collective-permute-done.23), channel_id=1, source_target_pairs={{4,0},{8,12},{5,1},{9,13},{6,2},{10,14},{7,3},{11,15},{20,16},{24,... | collective-permute-start | bytes 786440 | tf_op jit(solution)/shard_map/ppermute | solution.py:62
  128.1 3.6 %collective-permute-start.25 = (f32[2,32]{1,0:T(2,128)S(1)}, f32[2,32]{1,0:T(2,128)S(1)}, u32[]{:S(2)}, u32[]{:S(2)}) collective-permute-start(f32[2,32]{1,0:T(2,128)S(1)} %reduce_sum.29), channel_id=1, source_target_pairs={{0,2},{2,0},{1,3},{3,1},{4,6},{6,4},{5,7},{7,5},{8,10},{10,8},{9,1... | collective-permute-start | bytes 776 | tf_op jit(solution)/shard_map/ppermute | solution.py:183

commit v3 on v2

--- a/solution.py
+++ b/solution.py
@@ -121,6 +121,8 @@
     x["C2E"] = trade(trade.ready(y["C2E"]), TO_END)
     x["C3E"] = trade(y["C3E"], TO_END)
 
+    x["C1E"] = after(x["C1E"], y["C3E"])
+
     proj_acts = dot(columns(after(acts, x["A"], y["AM"]), place, 0, unit), left)
     proj_acts += dot(columns(acts, near, 0, unit), x["A"])
     proj_acts += dot(columns(acts, far_middle, 0, unit), either(x["AM"], y["AM"]))

time: 133 us -> 133 us (level)
  no operation moved by 1% of the time
where the time goes in v3:
time: 133 us; the launch traced here: 132 us
  starting transfers between devices  76.8 us (58%)
  waiting for transfers between devices  33.3 us (25%)
  matrix products  14 us (11%)
  other arithmetic  4 us (3%)
  local copies, waits for them, and re-layouts  3.47 us (3%)
    ppermute x22, starting transfers between devices, __call__(): self.came.append(lax.ppermute(x, 'dp', pairs or self.pairs))  67.4 us
    ppermute x22, waiting for transfers between devices, __call__(): self.came.append(lax.ppermute(x, 'dp', pairs or self.pairs))  25.7 us
    dot_general x27, matrix products, dot(): return jnp.dot(a, b, preferred_element_type=jnp.float32)  14 us
    ppermute x1, waiting for transfers between devices, on_line(): lax.ppermute(column_scores(guest_acts.astype(jnp.float32), guest_grads, s...  5.52 us
    ppermute x1, starting transfers between devices, on_line(): guest_acts = lax.ppermute(coded, 'dp', TO_MIDDLE)  4.9 us
  transfers between devices with their start and end apart: 26, of which 9 were waited for; matrix products, arithmetic and copies ran while one was open for 15% of the time, Pallas kernels for 0%

profile of v3, /device:TPU:0, one launch (start us, length us, event | category | flops | bytes accessed | tf_op | source)
XLA Modules:
  0.0 132.2 jit_solution(4916677302120377902)
XLA Ops:
  0.0 3.0 %collective-permute-start = (bf16[1024,256]{1,0:T(8,128)(2,1)}, bf16[1024,256]{1,0:T(8,128)(2,1)S(1)}, u32[]{:S(2)}, u32[]{:S(2)}) collective-permute-start(bf16[1024,256]{1,0:T(8,128)(2,1)} %bitcast.124), channel_id=1, source_target_pairs={{0,4},{4,0},{8,12},{12,8},{1,5},{5,1},{9,13},{13,9},{2,6},{6,2},{1... | collective-permute-start | bytes 1572872 | tf_op jit(solution)/shard_map/ppermute | solution.py:62
  3.0 0.7 collective-permute-start.1
  3.7 1.9 %slice_bitcast_fusion = bf16[1024,256]{1,0:T(8,128)(2,1)} fusion(bf16[1,3584,256]{2,1,0:T(8,128)(2,1)} %param.8), kind=kLoop, calls=%fused_computation.87 | loop fusion | bytes 1048576 | tf_op jit(solution)/shard_map/slice | solution.py:103
  5.6 4.4 %collective-permute-start.4 = (bf16[1024,256]{1,0:T(8,128)(2,1)}, bf16[1024,256]{1,0:T(8,128)(2,1)S(1)}, u32[]{:S(2)}, u32[]{:S(2)}) collective-permute-start(bf16[1024,256]{1,0:T(8,128)(2,1)} %slice_bitcast_fusion), channel_id=1, source_target_pairs={{0,4},{4,0},{8,12},{12,8},{1,5},{5,1},{9,13},{13,9},{2,6},{6,2},{1... | collective-permute-start | bytes 1572872 | tf_op jit(solution)/shard_map/ppermute | solution.py:62
  10.0 0.7 fusion.143
  10.7 5.3 %collective-permute-done = bf16[1024,256]{1,0:T(8,128)(2,1)S(1)} collective-permute-done((bf16[1024,256]{1,0:T(8,128)(2,1)}, bf16[1024,256]{1,0:T(8,128)(2,1)S(1)}, u32[]{:S(2)}, u32[]{:S(2)}) %collective-permute-start) | collective-permute-done | bytes 524320 | tf_op jit(solution)/shard_map/ppermute | solution.py:62
  16.0 0.7 collective-permute-start.3
  16.7 1.3 slice_select_fusion.1
  17.9 6.9 %collective-permute-start.2 = (bf16[1024,256]{1,0:T(8,128)(2,1)S(1)}, bf16[1024,256]{1,0:T(8,128)(2,1)S(1)}, u32[]{:S(2)}, u32[]{:S(2)}) collective-permute-start(bf16[1024,256]{1,0:T(8,128)(2,1)S(1)} %slice_select_fusion.1), channel_id=1, source_target_pairs={{0,4},{4,0},{8,12},{12,8},{1,5},{5,1},{9,13},{13,9},{2,6},{6,2},{1... | collective-permute-start | bytes 1572872 | tf_op jit(solution)/shard_map/ppermute | solution.py:62
  24.9 1.7 %fusion.16 = f32[512,256]{1,0:T(8,128)S(1)} fusion(bf16[1024,256]{1,0:T(8,128)(2,1)S(1)} %collective-permute-done, bf16[1,512,4096]{2,1,0:T(8,128)(2,1)} %param.5, s32[]{:T(128)S(6)} %select_n.204), kind=kOutput, calls=%fused_computation.27 | convolution fusion | flops 268435456 | bytes 2097156 | tf_op jit(solution)/shard_map/dot_general | solution.py:36
  26.6 1.8 %convolution_add_fusion.3 = f32[512,256]{1,0:T(8,128)S(1)} fusion(f32[512,256]{1,0:T(8,128)S(1)} %fusion.16, bf16[512,4096]{1,0:T(8,128)(2,1)} %bitcast.123, s32[]{:T(128)S(6)} %select_n.203, bf16[1,1024,256]{2,1,0:T(8,128)(2,1)} %param.7), kind=kOutput, calls=%fused_computation.5 | convolution fusion | flops 268566528 | bytes 2621444 | tf_op jit(solution)/shard_map/dot_general | solution.py:36
  28.4 0.7 collective-permute-start.6
  29.2 1.7 %fusion.27 = f32[512,256]{1,0:T(8,128)S(1)} fusion(bf16[1024,256]{1,0:T(8,128)(2,1)S(1)} %collective-permute-done.4, bf16[1,512,14336]{2,1,0:T(8,128)(2,1)} %param.6, s32[]{:T(128)S(6)} %select_n.178), kind=kOutput, calls=%fused_computation.38 | convolution fusion | flops 268435456 | bytes 2097156 | tf_op jit(solution)/shard_map/dot_general | solution.py:36
  30.9 0.7 collective-permute-start.8
  31.7 8.8 %collective-permute-start.5 = (bf16[1024,256]{1,0:T(8,128)(2,1)S(1)}, bf16[1024,256]{1,0:T(8,128)(2,1)S(1)}, u32[]{:S(2)}, u32[]{:S(2)}) collective-permute-start(bf16[1024,256]{1,0:T(8,128)(2,1)S(1)} %slice_select_fusion), channel_id=1, source_target_pairs={{0,4},{4,0},{8,12},{12,8},{1,5},{5,1},{9,13},{13,9},{2,6},{6,2},{1... | collective-permute-start | bytes 1572872 | tf_op jit(solution)/shard_map/ppermute | solution.py:62
  40.5 1.1 constant_dynamic-slice_fusion.9
  41.7 6.4 %collective-permute-start.7 = (bf16[1024,256]{1,0:T(8,128)(2,1)S(1)}, bf16[1024,256]{1,0:T(8,128)(2,1)S(1)}, u32[]{:S(2)}, u32[]{:S(2)}) collective-permute-start(bf16[1024,256]{1,0:T(8,128)(2,1)S(1)} %maximum_select_fusion), channel_id=1, source_target_pairs={{0,4},{4,0},{8,12},{12,8},{1,5},{5,1},{9,13},{13,9},{2,6},{6,2},{1... | collective-permute-start | bytes 1572872 | tf_op jit(solution)/shard_map/ppermute | solution.py:62
  48.1 0.7 collective-permute-start.10
  48.9 0.5 fusion.25
  49.3 1.1 fusion
  50.5 0.7 collective-permute-start.12
  51.2 1.5 %collective-permute-done.5 = bf16[1024,256]{1,0:T(8,128)(2,1)S(1)} collective-permute-done((bf16[1024,256]{1,0:T(8,128)(2,1)S(1)}, bf16[1024,256]{1,0:T(8,128)(2,1)S(1)}, u32[]{:S(2)}, u32[]{:S(2)}) %collective-permute-start.5) | collective-permute-done | bytes 524320 | tf_op jit(solution)/shard_map/ppermute | solution.py:62
  53.0 10.2 %collective-permute-start.9 = (bf16[1024,256]{1,0:T(8,128)(2,1)S(1)}, bf16[1024,256]{1,0:T(8,128)(2,1)S(1)}, u32[]{:S(2)}, u32[]{:S(2)}) collective-permute-start(bf16[1024,256]{1,0:T(8,128)(2,1)S(1)} %maximum_select_fusion.1), channel_id=1, source_target_pairs={{0,4},{4,0},{8,12},{12,8},{1,5},{5,1},{9,13},{13,9},{2,6},{6,2},{1... | collective-permute-start | bytes 1572872 | tf_op jit(solution)/shard_map/ppermute | solution.py:62
  63.2 0.5 add_add_fusion.1
  63.9 6.7 %collective-permute-start.11 = (bf16[1024,256]{1,0:T(8,128)(2,1)S(1)}, bf16[1024,256]{1,0:T(8,128)(2,1)S(1)}, u32[]{:S(2)}, u32[]{:S(2)}) collective-permute-start(bf16[1024,256]{1,0:T(8,128)(2,1)S(1)} %maximum_select_fusion.2), channel_id=1, source_target_pairs={{0,4},{4,0},{8,12},{12,8},{1,5},{5,1},{9,13},{13,9},{2,6},{6,2},{1... | collective-permute-start | bytes 1572872 | tf_op jit(solution)/shard_map/ppermute | solution.py:62
  70.6 0.4 fusion.13
  71.0 0.5 fusion.3
  71.5 1.6 %collective-permute-start.14 = (f32[512,256]{1,0:T(8,128)S(1)}, f32[512,256]{1,0:T(8,128)S(1)}, u32[]{:S(2)}, u32[]{:S(2)}) collective-permute-start(f32[512,256]{1,0:T(8,128)S(1)} %fusion.3), channel_id=1, source_target_pairs={{0,2},{2,0},{1,3},{3,1},{4,6},{6,4},{5,7},{7,5},{8,10},{10,8},{9,1... | collective-permute-start | bytes 1572872 | tf_op jit(solution)/shard_map/ppermute | solution.py:130
  73.1 0.7 collective-permute-start.15
  73.8 0.2 fusion.91
  74.0 0.4 fusion.21
  74.5 0.7 collective-permute-start.17
  75.2 4.5 %collective-permute-start.13 = (bf16[512,256]{1,0:T(8,128)(2,1)S(1)}, bf16[512,256]{1,0:T(8,128)(2,1)S(1)}, u32[]{:S(2)}, u32[]{:S(2)}) collective-permute-start(bf16[512,256]{1,0:T(8,128)(2,1)S(1)} %slice_select_fusion.2), channel_id=1, source_target_pairs={{0,4},{4,0},{8,12},{12,8},{1,5},{5,1},{9,13},{13,9},{2,6},{6,2},{1... | collective-permute-start | bytes 786440 | tf_op jit(solution)/shard_map/ppermute | solution.py:62
  79.8 0.2 fusion.88
  80.0 0.5 add_add_fusion
  80.5 0.2 convolution_add_fusion.8
  80.7 0.2 fusion.6
  81.3 5.2 %collective-permute-done.11 = bf16[1024,256]{1,0:T(8,128)(2,1)S(1)} collective-permute-done((bf16[1024,256]{1,0:T(8,128)(2,1)S(1)}, bf16[1024,256]{1,0:T(8,128)(2,1)S(1)}, u32[]{:S(2)}, u32[]{:S(2)}) %collective-permute-start.11) | collective-permute-done | bytes 524320 | tf_op jit(solution)/shard_map/ppermute | solution.py:62
  86.7 3.4 %collective-permute-start.16 = (bf16[1024,256]{1,0:T(8,128)(2,1)S(1)}, bf16[1024,256]{1,0:T(8,128)(2,1)S(1)}, u32[]{:S(2)}, u32[]{:S(2)}) collective-permute-start(bf16[1024,256]{1,0:T(8,128)(2,1)S(1)} %maximum_select_fusion.3), channel_id=1, source_target_pairs={{0,4},{4,0},{8,12},{12,8},{1,5},{5,1},{9,13},{13,9},{2,6},{6,2},{1... | collective-permute-start | bytes 1572872 | tf_op jit(solution)/shard_map/ppermute | solution.py:62
  90.0 0.7 collective-permute-start.19
  90.9 4.9 %collective-permute-start.22 = (s16[512,256]{1,0:T(8,128)(2,1)S(1)}, s16[512,256]{1,0:T(8,128)(2,1)S(1)}, u32[]{:S(2)}, u32[]{:S(2)}) collective-permute-start(s16[512,256]{1,0:T(8,128)(2,1)S(1)} %fusion.46), channel_id=1, source_target_pairs={{0,4},{12,8},{1,5},{13,9},{2,6},{14,10},{3,7},{15,11},{16,20},{28,... | collective-permute-start | bytes 786440 | tf_op jit(solution)/shard_map/ppermute | solution.py:135
  96.0 0.2 fusion.5
  96.3 0.3 fusion.49
  96.6 0.3 fusion.47
  96.9 0.5 fusion.7
  97.6 3.7 %collective-permute-start.18 = (bf16[1024,256]{1,0:T(8,128)(2,1)S(1)}, bf16[1024,256]{1,0:T(8,128)(2,1)S(1)}, u32[]{:S(2)}, u32[]{:S(2)}) collective-permute-start(bf16[1024,256]{1,0:T(8,128)(2,1)S(1)} %maximum_select_fusion.4), channel_id=1, source_target_pairs={{0,4},{4,0},{8,12},{12,8},{1,5},{5,1},{9,13},{13,9},{2,6},{6,2},{1... | collective-permute-start | bytes 1572872 | tf_op jit(solution)/shard_map/ppermute | solution.py:62
  101.3 0.7 collective-permute-start.20
  101.9 1.3 %collective-permute-done.16 = bf16[1024,256]{1,0:T(8,128)(2,1)S(1)} collective-permute-done((bf16[1024,256]{1,0:T(8,128)(2,1)S(1)}, bf16[1024,256]{1,0:T(8,128)(2,1)S(1)}, u32[]{:S(2)}, u32[]{:S(2)}) %collective-permute-start.16) | collective-permute-done | bytes 524320 | tf_op jit(solution)/shard_map/ppermute | solution.py:62
  103.3 0.4 convolution_add_fusion.1
  104.0 0.2 fusion.4
  104.2 1.3 collective-permute-start.21
  105.5 10.0 %collective-permute-done.18 = bf16[1024,256]{1,0:T(8,128)(2,1)S(1)} collective-permute-done((bf16[1024,256]{1,0:T(8,128)(2,1)S(1)}, bf16[1024,256]{1,0:T(8,128)(2,1)S(1)}, u32[]{:S(2)}, u32[]{:S(2)}) %collective-permute-start.18) | collective-permute-done | bytes 524320 | tf_op jit(solution)/shard_map/ppermute | solution.py:62
  115.5 0.2 fusion.95
  115.8 0.2 convolution_add_fusion.5
  116.2 1.3 collective-permute-start.23
  117.5 0.5 convolution_add_fusion
  117.9 1.3 collective-permute-start.24
  119.2 5.5 %collective-permute-done.23 = f32[2,256]{1,0:T(2,128)S(1)} collective-permute-done((f32[2,256]{1,0:T(2,128)S(1)}, f32[2,256]{1,0:T(2,128)S(1)}, u32[]{:S(2)}, u32[]{:S(2)}) %collective-permute-start.23) | collective-permute-done | bytes 2080 | tf_op jit(solution)/shard_map/ppermute | solution.py:179
  124.8 0.4 fusion.9
  125.3 2.3 %collective-permute-done.24 = bf16[512,256]{1,0:T(8,128)(2,1)S(1)} collective-permute-done((bf16[512,256]{1,0:T(8,128)(2,1)S(1)}, bf16[512,256]{1,0:T(8,128)(2,1)S(1)}, u32[]{:S(2)}, u32[]{:S(2)}) %collective-permute-start.24) | collective-permute-done | bytes 262176 | tf_op jit(solution)/shard_map/ppermute | solution.py:62
  127.6 0.3 bitcast_reduce_fusion
  128.1 1.7 %collective-permute-start.25 = (f32[2,32]{1,0:T(2,128)S(1)}, f32[2,32]{1,0:T(2,128)S(1)}, u32[]{:S(2)}, u32[]{:S(2)}) collective-permute-start(f32[2,32]{1,0:T(2,128)S(1)} %reduce_sum.29), channel_id=1, source_target_pairs={{0,2},{2,0},{1,3},{3,1},{4,6},{6,4},{5,7},{7,5},{8,10},{10,8},{9,1... | collective-permute-start | bytes 776 | tf_op jit(solution)/shard_map/ppermute | solution.py:185
  129.7 1.9 %collective-permute-done.25 = f32[2,32]{1,0:T(2,128)S(1)} collective-permute-done((f32[2,32]{1,0:T(2,128)S(1)}, f32[2,32]{1,0:T(2,128)S(1)}, u32[]{:S(2)}, u32[]{:S(2)}) %collective-permute-start.25) | collective-permute-done | bytes 288 | tf_op jit(solution)/shard_map/ppermute | solution.py:185
  131.6 0.6 multiply_bitcast_fusion
  (53 shorter events, 2.7 us)
Async XLA Ops:
  0.0 28.4 %copy-start = (bf16[1,3584,256]{2,1,0:T(8,128)(2,1)S(1)}, bf16[1,3584,256]{2,1,0:T(8,128)(2,1)}, u32[]{:S(2)}) copy-start(bf16[1,3584,256]{2,1,0:T(8,128)(2,1)} %param.8) | copy-start | bytes 5505028
  0.0 16.0 %collective-permute-start = (bf16[1024,256]{1,0:T(8,128)(2,1)}, bf16[1024,256]{1,0:T(8,128)(2,1)S(1)}, u32[]{:S(2)}, u32[]{:S(2)}) collective-permute-start(bf16[1024,256]{1,0:T(8,128)(2,1)} %bitcast.124), channel_id=1, source_target_pairs={{0,4},{4,0},{8,12},{12,8},{1,5},{5,1},{9,13},{13,9},{2,6},{6,2},{1... | collective-permute-start | bytes 1572872 | tf_op jit(solution)/shard_map/ppermute | solution.py:62
  3.0 13.0 %collective-permute-start.1 = (bf16[1024,256]{1,0:T(8,128)(2,1)}, bf16[1024,256]{1,0:T(8,128)(2,1)S(1)}, u32[]{:S(2)}, u32[]{:S(2)}) collective-permute-start(bf16[1024,256]{1,0:T(8,128)(2,1)} %bitcast.125), channel_id=1, source_target_pairs={{4,8},{8,4},{5,9},{9,5},{6,10},{10,6},{7,11},{11,7},{20,24},{24,20... | collective-permute-start | bytes 1572872 | tf_op jit(solution)/shard_map/ppermute | solution.py:62
  5.6 22.8 %collective-permute-start.4 = (bf16[1024,256]{1,0:T(8,128)(2,1)}, bf16[1024,256]{1,0:T(8,128)(2,1)S(1)}, u32[]{:S(2)}, u32[]{:S(2)}) collective-permute-start(bf16[1024,256]{1,0:T(8,128)(2,1)} %slice_bitcast_fusion), channel_id=1, source_target_pairs={{0,4},{4,0},{8,12},{12,8},{1,5},{5,1},{9,13},{13,9},{2,6},{6,2},{1... | collective-permute-start | bytes 1572872 | tf_op jit(solution)/shard_map/ppermute | solution.py:62
  16.0 14.8 %collective-permute-start.3 = (bf16[1024,256]{1,0:T(8,128)(2,1)S(1)}, bf16[1024,256]{1,0:T(8,128)(2,1)S(1)}, u32[]{:S(2)}, u32[]{:S(2)}) collective-permute-start(bf16[1024,256]{1,0:T(8,128)(2,1)S(1)} %collective-permute-done), channel_id=1, source_target_pairs={{4,8},{8,4},{5,9},{9,5},{6,10},{10,6},{7,11},{11,7},{20,24},{24,20... | collective-permute-start | bytes 1572872 | tf_op jit(solution)/shard_map/ppermute | solution.py:62
  16.7 32.2 %copy-start.1 = (bf16[1,512,14336]{2,1,0:T(8,128)(2,1)S(1)}, bf16[1,512,14336]{2,1,0:T(8,128)(2,1)}, u32[]{:S(2)}) copy-start(bf16[1,512,14336]{2,1,0:T(8,128)(2,1)} %param.6) | copy-start | bytes 44040196
  17.9 22.5 %collective-permute-start.2 = (bf16[1024,256]{1,0:T(8,128)(2,1)S(1)}, bf16[1024,256]{1,0:T(8,128)(2,1)S(1)}, u32[]{:S(2)}, u32[]{:S(2)}) collective-permute-start(bf16[1024,256]{1,0:T(8,128)(2,1)S(1)} %slice_select_fusion.1), channel_id=1, source_target_pairs={{0,4},{4,0},{8,12},{12,8},{1,5},{5,1},{9,13},{13,9},{2,6},{6,2},{1... | collective-permute-start | bytes 1572872 | tf_op jit(solution)/shard_map/ppermute | solution.py:62
  28.4 13.1 %collective-permute-start.6 = (bf16[1024,256]{1,0:T(8,128)(2,1)S(1)}, bf16[1024,256]{1,0:T(8,128)(2,1)S(1)}, u32[]{:S(2)}, u32[]{:S(2)}) collective-permute-start(bf16[1024,256]{1,0:T(8,128)(2,1)S(1)} %slice.121), channel_id=1, source_target_pairs={{4,8},{8,4},{5,9},{9,5},{6,10},{10,6},{7,11},{11,7},{20,24},{24,20... | collective-permute-start | bytes 1572872 | tf_op jit(solution)/shard_map/ppermute | solution.py:62
  30.9 19.6 %collective-permute-start.8 = (bf16[1024,256]{1,0:T(8,128)(2,1)S(1)}, bf16[1024,256]{1,0:T(8,128)(2,1)S(1)}, u32[]{:S(2)}, u32[]{:S(2)}) collective-permute-start(bf16[1024,256]{1,0:T(8,128)(2,1)S(1)} %slice.122), channel_id=1, source_target_pairs={{4,8},{8,4},{5,9},{9,5},{6,10},{10,6},{7,11},{11,7},{20,24},{24,20... | collective-permute-start | bytes 1572872 | tf_op jit(solution)/shard_map/ppermute | solution.py:62
  31.7 21.1 %collective-permute-start.5 = (bf16[1024,256]{1,0:T(8,128)(2,1)S(1)}, bf16[1024,256]{1,0:T(8,128)(2,1)S(1)}, u32[]{:S(2)}, u32[]{:S(2)}) collective-permute-start(bf16[1024,256]{1,0:T(8,128)(2,1)S(1)} %slice_select_fusion), channel_id=1, source_target_pairs={{0,4},{4,0},{8,12},{12,8},{1,5},{5,1},{9,13},{13,9},{2,6},{6,2},{1... | collective-permute-start | bytes 1572872 | tf_op jit(solution)/shard_map/ppermute | solution.py:62
  41.7 21.9 %collective-permute-start.7 = (bf16[1024,256]{1,0:T(8,128)(2,1)S(1)}, bf16[1024,256]{1,0:T(8,128)(2,1)S(1)}, u32[]{:S(2)}, u32[]{:S(2)}) collective-permute-start(bf16[1024,256]{1,0:T(8,128)(2,1)S(1)} %maximum_select_fusion), channel_id=1, source_target_pairs={{0,4},{4,0},{8,12},{12,8},{1,5},{5,1},{9,13},{13,9},{2,6},{6,2},{1... | collective-permute-start | bytes 1572872 | tf_op jit(solution)/shard_map/ppermute | solution.py:62
  48.1 15.6 %collective-permute-start.10 = (bf16[1024,256]{1,0:T(8,128)(2,1)S(1)}, bf16[1024,256]{1,0:T(8,128)(2,1)S(1)}, u32[]{:S(2)}, u32[]{:S(2)}) collective-permute-start(bf16[1024,256]{1,0:T(8,128)(2,1)S(1)} %slice.135), channel_id=1, source_target_pairs={{4,8},{8,4},{5,9},{9,5},{6,10},{10,6},{7,11},{11,7},{20,24},{24,20... | collective-permute-start | bytes 1572872 | tf_op jit(solution)/shard_map/ppermute | solution.py:62
  50.5 23.9 %collective-permute-start.12 = (bf16[512,256]{1,0:T(8,128)(2,1)S(1)}, bf16[512,256]{1,0:T(8,128)(2,1)S(1)}, u32[]{:S(2)}, u32[]{:S(2)}) collective-permute-start(bf16[512,256]{1,0:T(8,128)(2,1)S(1)} %slice.137), channel_id=1, source_target_pairs={{4,8},{8,4},{5,9},{9,5},{6,10},{10,6},{7,11},{11,7},{20,24},{24,20... | collective-permute-start | bytes 786440 | tf_op jit(solution)/shard_map/ppermute | solution.py:62
  52.8 17.8 %copy-start.2 = (bf16[1,512,4096]{2,1,0:T(8,128)(2,1)S(1)}, bf16[1,512,4096]{2,1,0:T(8,128)(2,1)}, u32[]{:S(2)}) copy-start(bf16[1,512,4096]{2,1,0:T(8,128)(2,1)} %param.5) | copy-start | bytes 12582916
  53.0 22.2 %collective-permute-start.9 = (bf16[1024,256]{1,0:T(8,128)(2,1)S(1)}, bf16[1024,256]{1,0:T(8,128)(2,1)S(1)}, u32[]{:S(2)}, u32[]{:S(2)}) collective-permute-start(bf16[1024,256]{1,0:T(8,128)(2,1)S(1)} %maximum_select_fusion.1), channel_id=1, source_target_pairs={{0,4},{4,0},{8,12},{12,8},{1,5},{5,1},{9,13},{13,9},{2,6},{6,2},{1... | collective-permute-start | bytes 1572872 | tf_op jit(solution)/shard_map/ppermute | solution.py:62
  63.9 22.5 %collective-permute-start.11 = (bf16[1024,256]{1,0:T(8,128)(2,1)S(1)}, bf16[1024,256]{1,0:T(8,128)(2,1)S(1)}, u32[]{:S(2)}, u32[]{:S(2)}) collective-permute-start(bf16[1024,256]{1,0:T(8,128)(2,1)S(1)} %maximum_select_fusion.2), channel_id=1, source_target_pairs={{0,4},{4,0},{8,12},{12,8},{1,5},{5,1},{9,13},{13,9},{2,6},{6,2},{1... | collective-permute-start | bytes 1572872 | tf_op jit(solution)/shard_map/ppermute | solution.py:62
  71.5 9.6 %collective-permute-start.14 = (f32[512,256]{1,0:T(8,128)S(1)}, f32[512,256]{1,0:T(8,128)S(1)}, u32[]{:S(2)}, u32[]{:S(2)}) collective-permute-start(f32[512,256]{1,0:T(8,128)S(1)} %fusion.3), channel_id=1, source_target_pairs={{0,2},{2,0},{1,3},{3,1},{4,6},{6,4},{5,7},{7,5},{8,10},{10,8},{9,1... | collective-permute-start | bytes 1572872 | tf_op jit(solution)/shard_map/ppermute | solution.py:130
  73.1 13.4 %collective-permute-start.15 = (bf16[1024,256]{1,0:T(8,128)(2,1)S(1)}, bf16[1024,256]{1,0:T(8,128)(2,1)S(1)}, u32[]{:S(2)}, u32[]{:S(2)}) collective-permute-start(bf16[1024,256]{1,0:T(8,128)(2,1)S(1)} %collective-permute-done.4), channel_id=1, source_target_pairs={{4,8},{8,4},{5,9},{9,5},{6,10},{10,6},{7,11},{11,7},{20,24},{24,20... | collective-permute-start | bytes 1572872 | tf_op jit(solution)/shard_map/ppermute | solution.py:62
  74.5 23.0 %collective-permute-start.17 = (bf16[1024,256]{1,0:T(8,128)(2,1)S(1)}, bf16[1024,256]{1,0:T(8,128)(2,1)S(1)}, u32[]{:S(2)}, u32[]{:S(2)}) collective-permute-start(bf16[1024,256]{1,0:T(8,128)(2,1)S(1)} %collective-permute-done.2), channel_id=1, source_target_pairs={{4,8},{8,4},{5,9},{9,5},{6,10},{10,6},{7,11},{11,7},{20,24},{24,20... | collective-permute-start | bytes 1572872 | tf_op jit(solution)/shard_map/ppermute | solution.py:62
  75.2 21.0 %collective-permute-start.13 = (bf16[512,256]{1,0:T(8,128)(2,1)S(1)}, bf16[512,256]{1,0:T(8,128)(2,1)S(1)}, u32[]{:S(2)}, u32[]{:S(2)}) collective-permute-start(bf16[512,256]{1,0:T(8,128)(2,1)S(1)} %slice_select_fusion.2), channel_id=1, source_target_pairs={{0,4},{4,0},{8,12},{12,8},{1,5},{5,1},{9,13},{13,9},{2,6},{6,2},{1... | collective-permute-start | bytes 786440 | tf_op jit(solution)/shard_map/ppermute | solution.py:62
  86.7 16.6 %collective-permute-start.16 = (bf16[1024,256]{1,0:T(8,128)(2,1)S(1)}, bf16[1024,256]{1,0:T(8,128)(2,1)S(1)}, u32[]{:S(2)}, u32[]{:S(2)}) collective-permute-start(bf16[1024,256]{1,0:T(8,128)(2,1)S(1)} %maximum_select_fusion.3), channel_id=1, source_target_pairs={{0,4},{4,0},{8,12},{12,8},{1,5},{5,1},{9,13},{13,9},{2,6},{6,2},{1... | collective-permute-start | bytes 1572872 | tf_op jit(solution)/shard_map/ppermute | solution.py:62
  90.0 11.2 %collective-permute-start.19 = (bf16[1024,256]{1,0:T(8,128)(2,1)S(1)}, bf16[1024,256]{1,0:T(8,128)(2,1)S(1)}, u32[]{:S(2)}, u32[]{:S(2)}) collective-permute-start(bf16[1024,256]{1,0:T(8,128)(2,1)S(1)} %collective-permute-done.5), channel_id=1, source_target_pairs={{4,8},{8,4},{5,9},{9,5},{6,10},{10,6},{7,11},{11,7},{20,24},{24,20... | collective-permute-start | bytes 1572872 | tf_op jit(solution)/shard_map/ppermute | solution.py:62
  90.9 25.1 %collective-permute-start.22 = (s16[512,256]{1,0:T(8,128)(2,1)S(1)}, s16[512,256]{1,0:T(8,128)(2,1)S(1)}, u32[]{:S(2)}, u32[]{:S(2)}) collective-permute-start(s16[512,256]{1,0:T(8,128)(2,1)S(1)} %fusion.46), channel_id=1, source_target_pairs={{0,4},{12,8},{1,5},{13,9},{2,6},{14,10},{3,7},{15,11},{16,20},{28,... | collective-permute-start | bytes 786440 | tf_op jit(solution)/shard_map/ppermute | solution.py:135
  97.6 17.9 %collective-permute-start.18 = (bf16[1024,256]{1,0:T(8,128)(2,1)S(1)}, bf16[1024,256]{1,0:T(8,128)(2,1)S(1)}, u32[]{:S(2)}, u32[]{:S(2)}) collective-permute-start(bf16[1024,256]{1,0:T(8,128)(2,1)S(1)} %maximum_select_fusion.4), channel_id=1, source_target_pairs={{0,4},{4,0},{8,12},{12,8},{1,5},{5,1},{9,13},{13,9},{2,6},{6,2},{1... | collective-permute-start | bytes 1572872 | tf_op jit(solution)/shard_map/ppermute | solution.py:62
  101.3 14.3 %collective-permute-start.20 = (bf16[512,256]{1,0:T(8,128)(2,1)S(1)}, bf16[512,256]{1,0:T(8,128)(2,1)S(1)}, u32[]{:S(2)}, u32[]{:S(2)}) collective-permute-start(bf16[512,256]{1,0:T(8,128)(2,1)S(1)} %collective-permute-done.13), channel_id=1, source_target_pairs={{4,8},{8,4},{5,9},{9,5},{6,10},{10,6},{7,11},{11,7},{20,24},{24,20... | collective-permute-start | bytes 786440 | tf_op jit(solution)/shard_map/ppermute | solution.py:62
  104.2 20.5 %collective-permute-start.21 = (bf16[1024,256]{1,0:T(8,128)(2,1)S(1)}, bf16[1024,256]{1,0:T(8,128)(2,1)S(1)}, u32[]{:S(2)}, u32[]{:S(2)}) collective-permute-start(bf16[1024,256]{1,0:T(8,128)(2,1)S(1)} %collective-permute-done.19), channel_id=1, source_target_pairs={{4,0},{8,12},{5,1},{9,13},{6,2},{10,14},{7,3},{11,15},{20,16},{24,... | collective-permute-start | bytes 1572872 | tf_op jit(solution)/shard_map/ppermute | solution.py:62
  116.2 8.6 %collective-permute-start.23 = (f32[2,256]{1,0:T(2,128)S(1)}, f32[2,256]{1,0:T(2,128)S(1)}, u32[]{:S(2)}, u32[]{:S(2)}) collective-permute-start(f32[2,256]{1,0:T(2,128)S(1)} %bitcast_reduce_fusion.1), channel_id=1, source_target_pairs={{4,0},{8,12},{5,1},{9,13},{6,2},{10,14},{7,3},{11,15},{20,16},{24,... | collective-permute-start | bytes 6152 | tf_op jit(solution)/shard_map/ppermute | solution.py:179
  117.9 9.6 %collective-permute-start.24 = (bf16[512,256]{1,0:T(8,128)(2,1)S(1)}, bf16[512,256]{1,0:T(8,128)(2,1)S(1)}, u32[]{:S(2)}, u32[]{:S(2)}) collective-permute-start(bf16[512,256]{1,0:T(8,128)(2,1)S(1)} %collective-permute-done.20), channel_id=1, source_target_pairs={{4,0},{8,12},{5,1},{9,13},{6,2},{10,14},{7,3},{11,15},{20,16},{24,... | collective-permute-start | bytes 786440 | tf_op jit(solution)/shard_map/ppermute | solution.py:62
  128.1 3.6 %collective-permute-start.25 = (f32[2,32]{1,0:T(2,128)S(1)}, f32[2,32]{1,0:T(2,128)S(1)}, u32[]{:S(2)}, u32[]{:S(2)}) collective-permute-start(f32[2,32]{1,0:T(2,128)S(1)} %reduce_sum.29), channel_id=1, source_target_pairs={{0,2},{2,0},{1,3},{3,1},{4,6},{6,4},{5,7},{7,5},{8,10},{10,8},{9,1... | collective-permute-start | bytes 776 | tf_op jit(solution)/shard_map/ppermute | solution.py:185

commit v4 on v2

--- a/solution.py
+++ b/solution.py
@@ -163,7 +163,7 @@
     guest_grads = guest_term(0, x["BM"])
     proj_grads += middle_term("C1")
     guest_grads += guest_term(1, x["C1M"])
-    proj_grads, guest_grads = lax.optimization_barrier((proj_grads, guest_grads))
+    proj_grads, guest_grads, coded = lax.optimization_barrier((proj_grads, guest_grads, coded))
     proj_grads += middle_term("C2")
     guest_grads += guest_term(2, x["C2M"])
     proj_grads += middle_term("C3")

time: 133 us -> 133 us (level)
  waiting for transfers between devices: 33.3 us -> 38 us
  starting transfers between devices: 76.8 us -> 72.2 us
    ppermute x22, waiting for transfers between devices: 25.7 us -> 30.6 us  [__call__(): self.came.append(lax.ppermute(x, 'dp', pairs or self.pairs))]
    ppermute x1, starting transfers between devices: 4.9 us -> 1.94 us  [on_line(): guest_acts = lax.ppermute(coded, 'dp', TO_MIDDLE)]
    ppermute x22, starting transfers between devices: 67.4 us -> 65.7 us  [__call__(): self.came.append(lax.ppermute(x, 'dp', pairs or self.pairs))]
  transfers between devices with their start and end apart: 26 -> 26, of which waited for: 9 -> 10; matrix products, arithmetic and copies ran while one was open for 15% -> 15% of each run, Pallas kernels for 0% -> 0%
where the time goes in v4:
time: 133 us; the launch traced here: 132 us
  starting transfers between devices  72.2 us (54%)
  waiting for transfers between devices  38 us (29%)
  matrix products  14 us (11%)
  other arithmetic  3.99 us (3%)
  local copies, waits for them, and re-layouts  3.47 us (3%)
    ppermute x22, starting transfers between devices, __call__(): self.came.append(lax.ppermute(x, 'dp', pairs or self.pairs))  65.7 us
    ppermute x22, waiting for transfers between devices, __call__(): self.came.append(lax.ppermute(x, 'dp', pairs or self.pairs))  30.6 us
    dot_general x27, matrix products, dot(): return jnp.dot(a, b, preferred_element_type=jnp.float32)  14 us
    ppermute x1, waiting for transfers between devices, on_line(): lax.ppermute(column_scores(guest_acts.astype(jnp.float32), guest_grads, s...  5.52 us
  transfers between devices with their start and end apart: 26, of which 10 were waited for; matrix products, arithmetic and copies ran while one was open for 15% of the time, Pallas kernels for 0%

profile of v4, /device:TPU:0, one launch (start us, length us, event | category | flops | bytes accessed | tf_op | source)
XLA Modules:
  0.0 132.2 jit_solution(3377884965139070865)
XLA Ops:
  0.0 3.0 %collective-permute-start = (bf16[1024,256]{1,0:T(8,128)(2,1)}, bf16[1024,256]{1,0:T(8,128)(2,1)S(1)}, u32[]{:S(2)}, u32[]{:S(2)}) collective-permute-start(bf16[1024,256]{1,0:T(8,128)(2,1)} %bitcast.124), channel_id=1, source_target_pairs={{0,4},{4,0},{8,12},{12,8},{1,5},{5,1},{9,13},{13,9},{2,6},{6,2},{1... | collective-permute-start | bytes 1572872 | tf_op jit(solution)/shard_map/ppermute | solution.py:62
  3.0 0.7 collective-permute-start.1
  3.7 1.9 %slice_bitcast_fusion = bf16[1024,256]{1,0:T(8,128)(2,1)} fusion(bf16[1,3584,256]{2,1,0:T(8,128)(2,1)} %param.8), kind=kLoop, calls=%fused_computation.87 | loop fusion | bytes 1048576 | tf_op jit(solution)/shard_map/slice | solution.py:103
  5.6 4.4 %collective-permute-start.4 = (bf16[1024,256]{1,0:T(8,128)(2,1)}, bf16[1024,256]{1,0:T(8,128)(2,1)S(1)}, u32[]{:S(2)}, u32[]{:S(2)}) collective-permute-start(bf16[1024,256]{1,0:T(8,128)(2,1)} %slice_bitcast_fusion), channel_id=1, source_target_pairs={{0,4},{4,0},{8,12},{12,8},{1,5},{5,1},{9,13},{13,9},{2,6},{6,2},{1... | collective-permute-start | bytes 1572872 | tf_op jit(solution)/shard_map/ppermute | solution.py:62
  10.0 0.7 fusion.143
  10.7 5.3 %collective-permute-done = bf16[1024,256]{1,0:T(8,128)(2,1)S(1)} collective-permute-done((bf16[1024,256]{1,0:T(8,128)(2,1)}, bf16[1024,256]{1,0:T(8,128)(2,1)S(1)}, u32[]{:S(2)}, u32[]{:S(2)}) %collective-permute-start) | collective-permute-done | bytes 524320 | tf_op jit(solution)/shard_map/ppermute | solution.py:62
  16.0 0.7 collective-permute-start.3
  16.7 1.3 slice_select_fusion.1
  17.9 6.9 %collective-permute-start.2 = (bf16[1024,256]{1,0:T(8,128)(2,1)S(1)}, bf16[1024,256]{1,0:T(8,128)(2,1)S(1)}, u32[]{:S(2)}, u32[]{:S(2)}) collective-permute-start(bf16[1024,256]{1,0:T(8,128)(2,1)S(1)} %slice_select_fusion.1), channel_id=1, source_target_pairs={{0,4},{4,0},{8,12},{12,8},{1,5},{5,1},{9,13},{13,9},{2,6},{6,2},{1... | collective-permute-start | bytes 1572872 | tf_op jit(solution)/shard_map/ppermute | solution.py:62
  24.9 1.7 %fusion.17 = f32[512,256]{1,0:T(8,128)S(1)} fusion(bf16[1024,256]{1,0:T(8,128)(2,1)S(1)} %collective-permute-done, bf16[1,512,4096]{2,1,0:T(8,128)(2,1)} %param.5, s32[]{:T(128)S(6)} %select_n.194), kind=kOutput, calls=%fused_computation.28 | convolution fusion | flops 268435456 | bytes 2097156 | tf_op jit(solution)/shard_map/dot_general | solution.py:36
  26.6 1.8 %convolution_add_fusion.4 = f32[512,256]{1,0:T(8,128)S(1)} fusion(f32[512,256]{1,0:T(8,128)S(1)} %fusion.17, bf16[512,4096]{1,0:T(8,128)(2,1)} %bitcast.123, s32[]{:T(128)S(6)} %select_n.193, bf16[1,1024,256]{2,1,0:T(8,128)(2,1)} %param.7), kind=kOutput, calls=%fused_computation.6 | convolution fusion | flops 268566528 | bytes 2621444 | tf_op jit(solution)/shard_map/dot_general | solution.py:36
  28.4 0.7 collective-permute-start.6
  29.2 1.7 %fusion.27 = f32[512,256]{1,0:T(8,128)S(1)} fusion(bf16[1024,256]{1,0:T(8,128)(2,1)S(1)} %collective-permute-done.4, bf16[1,512,14336]{2,1,0:T(8,128)(2,1)} %param.6, s32[]{:T(128)S(6)} %select_n.178), kind=kOutput, calls=%fused_computation.38 | convolution fusion | flops 268435456 | bytes 2097156 | tf_op jit(solution)/shard_map/dot_general | solution.py:36
  30.9 0.7 collective-permute-start.8
  31.7 8.8 %collective-permute-start.5 = (bf16[1024,256]{1,0:T(8,128)(2,1)S(1)}, bf16[1024,256]{1,0:T(8,128)(2,1)S(1)}, u32[]{:S(2)}, u32[]{:S(2)}) collective-permute-start(bf16[1024,256]{1,0:T(8,128)(2,1)S(1)} %slice_select_fusion), channel_id=1, source_target_pairs={{0,4},{4,0},{8,12},{12,8},{1,5},{5,1},{9,13},{13,9},{2,6},{6,2},{1... | collective-permute-start | bytes 1572872 | tf_op jit(solution)/shard_map/ppermute | solution.py:62
  40.5 1.1 constant_dynamic-slice_fusion.9
  41.7 6.4 %collective-permute-start.7 = (bf16[1024,256]{1,0:T(8,128)(2,1)S(1)}, bf16[1024,256]{1,0:T(8,128)(2,1)S(1)}, u32[]{:S(2)}, u32[]{:S(2)}) collective-permute-start(bf16[1024,256]{1,0:T(8,128)(2,1)S(1)} %maximum_select_fusion), channel_id=1, source_target_pairs={{0,4},{4,0},{8,12},{12,8},{1,5},{5,1},{9,13},{13,9},{2,6},{6,2},{1... | collective-permute-start | bytes 1572872 | tf_op jit(solution)/shard_map/ppermute | solution.py:62
  48.1 0.7 collective-permute-start.11
  48.9 0.5 fusion.25
  49.3 1.1 fusion
  50.5 0.8 collective-permute-start.13
  51.3 1.4 %collective-permute-done.5 = bf16[1024,256]{1,0:T(8,128)(2,1)S(1)} collective-permute-done((bf16[1024,256]{1,0:T(8,128)(2,1)S(1)}, bf16[1024,256]{1,0:T(8,128)(2,1)S(1)}, u32[]{:S(2)}, u32[]{:S(2)}) %collective-permute-start.5) | collective-permute-done | bytes 524320 | tf_op jit(solution)/shard_map/ppermute | solution.py:62
  52.9 10.2 %collective-permute-start.9 = (bf16[1024,256]{1,0:T(8,128)(2,1)S(1)}, bf16[1024,256]{1,0:T(8,128)(2,1)S(1)}, u32[]{:S(2)}, u32[]{:S(2)}) collective-permute-start(bf16[1024,256]{1,0:T(8,128)(2,1)S(1)} %maximum_select_fusion.1), channel_id=1, source_target_pairs={{0,4},{4,0},{8,12},{12,8},{1,5},{5,1},{9,13},{13,9},{2,6},{6,2},{1... | collective-permute-start | bytes 1572872 | tf_op jit(solution)/shard_map/ppermute | solution.py:62
  63.1 0.4 fusion.14
  63.6 0.5 fusion.2
  64.1 1.6 %collective-permute-start.10 = (f32[512,256]{1,0:T(8,128)S(1)}, f32[512,256]{1,0:T(8,128)S(1)}, u32[]{:S(2)}, u32[]{:S(2)}) collective-permute-start(f32[512,256]{1,0:T(8,128)S(1)} %fusion.2), channel_id=1, source_target_pairs={{0,2},{2,0},{1,3},{3,1},{4,6},{6,4},{5,7},{7,5},{8,10},{10,8},{9,1... | collective-permute-start | bytes 1572872 | tf_op jit(solution)/shard_map/ppermute | solution.py:128
  65.9 4.7 %collective-permute-start.12 = (bf16[1024,256]{1,0:T(8,128)(2,1)S(1)}, bf16[1024,256]{1,0:T(8,128)(2,1)S(1)}, u32[]{:S(2)}, u32[]{:S(2)}) collective-permute-start(bf16[1024,256]{1,0:T(8,128)(2,1)S(1)} %maximum_select_fusion.2), channel_id=1, source_target_pairs={{0,4},{4,0},{8,12},{12,8},{1,5},{5,1},{9,13},{13,9},{2,6},{6,2},{1... | collective-permute-start | bytes 1572872 | tf_op jit(solution)/shard_map/ppermute | solution.py:62
  70.6 0.7 collective-permute-start.15
  71.3 0.5 add_add_fusion.1
  72.0 0.4 fusion.21
  72.4 0.7 collective-permute-start.17
  73.1 2.1 %collective-permute-done.9 = bf16[1024,256]{1,0:T(8,128)(2,1)S(1)} collective-permute-done((bf16[1024,256]{1,0:T(8,128)(2,1)S(1)}, bf16[1024,256]{1,0:T(8,128)(2,1)S(1)}, u32[]{:S(2)}, u32[]{:S(2)}) %collective-permute-start.9) | collective-permute-done | bytes 524320 | tf_op jit(solution)/shard_map/ppermute | solution.py:62
  75.2 4.5 %collective-permute-start.14 = (bf16[512,256]{1,0:T(8,128)(2,1)S(1)}, bf16[512,256]{1,0:T(8,128)(2,1)S(1)}, u32[]{:S(2)}, u32[]{:S(2)}) collective-permute-start(bf16[512,256]{1,0:T(8,128)(2,1)S(1)} %slice_select_fusion.2), channel_id=1, source_target_pairs={{0,4},{4,0},{8,12},{12,8},{1,5},{5,1},{9,13},{13,9},{2,6},{6,2},{1... | collective-permute-start | bytes 786440 | tf_op jit(solution)/shard_map/ppermute | solution.py:62
  80.1 1.9 %collective-permute-start.21 = (s16[512,256]{1,0:T(8,128)(2,1)S(1)}, s16[512,256]{1,0:T(8,128)(2,1)S(1)}, u32[]{:S(2)}, u32[]{:S(2)}) collective-permute-start(s16[512,256]{1,0:T(8,128)(2,1)S(1)} %fusion.50), channel_id=1, source_target_pairs={{0,4},{12,8},{1,5},{13,9},{2,6},{14,10},{3,7},{15,11},{16,20},{28,... | collective-permute-start | bytes 786440 | tf_op jit(solution)/shard_map/ppermute | solution.py:133
  82.2 0.2 convolution_add_fusion.8
  82.5 0.2 fusion.6
  82.7 0.5 add_add_fusion
  83.2 3.3 %collective-permute-done.12 = bf16[1024,256]{1,0:T(8,128)(2,1)S(1)} collective-permute-done((bf16[1024,256]{1,0:T(8,128)(2,1)S(1)}, bf16[1024,256]{1,0:T(8,128)(2,1)S(1)}, u32[]{:S(2)}, u32[]{:S(2)}) %collective-permute-start.12) | collective-permute-done | bytes 524320 | tf_op jit(solution)/shard_map/ppermute | solution.py:62
  86.6 1.8 %collective-permute-start.16 = (bf16[1024,256]{1,0:T(8,128)(2,1)S(1)}, bf16[1024,256]{1,0:T(8,128)(2,1)S(1)}, u32[]{:S(2)}, u32[]{:S(2)}) collective-permute-start(bf16[1024,256]{1,0:T(8,128)(2,1)S(1)} %maximum_select_fusion.3), channel_id=1, source_target_pairs={{0,4},{4,0},{8,12},{12,8},{1,5},{5,1},{9,13},{13,9},{2,6},{6,2},{1... | collective-permute-start | bytes 1572872 | tf_op jit(solution)/shard_map/ppermute | solution.py:62
  88.5 0.7 collective-permute-start.19
  89.4 0.2 fusion.5
  89.6 2.4 %collective-permute-done.14 = bf16[512,256]{1,0:T(8,128)(2,1)S(1)} collective-permute-done((bf16[512,256]{1,0:T(8,128)(2,1)S(1)}, bf16[512,256]{1,0:T(8,128)(2,1)S(1)}, u32[]{:S(2)}, u32[]{:S(2)}) %collective-permute-start.14) | collective-permute-done | bytes 262176 | tf_op jit(solution)/shard_map/ppermute | solution.py:62
  92.0 0.3 fusion.47
  92.4 0.3 fusion.45
  92.7 0.5 fusion.7
  93.4 5.4 %collective-permute-start.18 = (bf16[1024,256]{1,0:T(8,128)(2,1)S(1)}, bf16[1024,256]{1,0:T(8,128)(2,1)S(1)}, u32[]{:S(2)}, u32[]{:S(2)}) collective-permute-start(bf16[1024,256]{1,0:T(8,128)(2,1)S(1)} %maximum_select_fusion.4), channel_id=1, source_target_pairs={{0,4},{4,0},{8,12},{12,8},{1,5},{5,1},{9,13},{13,9},{2,6},{6,2},{1... | collective-permute-start | bytes 1572872 | tf_op jit(solution)/shard_map/ppermute | solution.py:62
  98.8 9.4 %collective-permute-done.16 = bf16[1024,256]{1,0:T(8,128)(2,1)S(1)} collective-permute-done((bf16[1024,256]{1,0:T(8,128)(2,1)S(1)}, bf16[1024,256]{1,0:T(8,128)(2,1)S(1)}, u32[]{:S(2)}, u32[]{:S(2)}) %collective-permute-start.16) | collective-permute-done | bytes 524320 | tf_op jit(solution)/shard_map/ppermute | solution.py:62
  108.2 0.2 fusion.85
  108.4 0.2 fusion.4
  108.6 0.4 convolution_add_fusion.1
  109.1 1.3 collective-permute-start.20
  110.4 0.7 collective-permute-start.23
  111.1 4.5 %collective-permute-done.18 = bf16[1024,256]{1,0:T(8,128)(2,1)S(1)} collective-permute-done((bf16[1024,256]{1,0:T(8,128)(2,1)S(1)}, bf16[1024,256]{1,0:T(8,128)(2,1)S(1)}, u32[]{:S(2)}, u32[]{:S(2)}) %collective-permute-start.18) | collective-permute-done | bytes 524320 | tf_op jit(solution)/shard_map/ppermute | solution.py:62
  115.8 0.2 convolution_add_fusion.5
  116.2 1.3 collective-permute-start.22
  117.5 0.5 convolution_add_fusion
  117.9 1.3 collective-permute-start.24
  119.2 5.5 %collective-permute-done.22 = f32[2,256]{1,0:T(2,128)S(1)} collective-permute-done((f32[2,256]{1,0:T(2,128)S(1)}, f32[2,256]{1,0:T(2,128)S(1)}, u32[]{:S(2)}, u32[]{:S(2)}) %collective-permute-start.22) | collective-permute-done | bytes 2080 | tf_op jit(solution)/shard_map/ppermute | solution.py:177
  124.8 0.4 fusion.9
  125.3 2.3 %collective-permute-done.24 = bf16[512,256]{1,0:T(8,128)(2,1)S(1)} collective-permute-done((bf16[512,256]{1,0:T(8,128)(2,1)S(1)}, bf16[512,256]{1,0:T(8,128)(2,1)S(1)}, u32[]{:S(2)}, u32[]{:S(2)}) %collective-permute-start.24) | collective-permute-done | bytes 262176 | tf_op jit(solution)/shard_map/ppermute | solution.py:62
  127.6 0.3 bitcast_reduce_fusion
  128.1 1.7 %collective-permute-start.25 = (f32[2,32]{1,0:T(2,128)S(1)}, f32[2,32]{1,0:T(2,128)S(1)}, u32[]{:S(2)}, u32[]{:S(2)}) collective-permute-start(f32[2,32]{1,0:T(2,128)S(1)} %reduce_sum.29), channel_id=1, source_target_pairs={{0,2},{2,0},{1,3},{3,1},{4,6},{6,4},{5,7},{7,5},{8,10},{10,8},{9,1... | collective-permute-start | bytes 776 | tf_op jit(solution)/shard_map/ppermute | solution.py:183
  129.7 1.9 %collective-permute-done.25 = f32[2,32]{1,0:T(2,128)S(1)} collective-permute-done((f32[2,32]{1,0:T(2,128)S(1)}, f32[2,32]{1,0:T(2,128)S(1)}, u32[]{:S(2)}, u32[]{:S(2)}) %collective-permute-start.25) | collective-permute-done | bytes 288 | tf_op jit(solution)/shard_map/ppermute | solution.py:183
  131.6 0.6 multiply_bitcast_fusion
  (53 shorter events, 2.9 us)
Async XLA Ops:
  0.0 28.4 %copy-start = (bf16[1,3584,256]{2,1,0:T(8,128)(2,1)S(1)}, bf16[1,3584,256]{2,1,0:T(8,128)(2,1)}, u32[]{:S(2)}) copy-start(bf16[1,3584,256]{2,1,0:T(8,128)(2,1)} %param.8) | copy-start | bytes 5505028
  0.0 16.0 %collective-permute-start = (bf16[1024,256]{1,0:T(8,128)(2,1)}, bf16[1024,256]{1,0:T(8,128)(2,1)S(1)}, u32[]{:S(2)}, u32[]{:S(2)}) collective-permute-start(bf16[1024,256]{1,0:T(8,128)(2,1)} %bitcast.124), channel_id=1, source_target_pairs={{0,4},{4,0},{8,12},{12,8},{1,5},{5,1},{9,13},{13,9},{2,6},{6,2},{1... | collective-permute-start | bytes 1572872 | tf_op jit(solution)/shard_map/ppermute | solution.py:62
  3.0 13.0 %collective-permute-start.1 = (bf16[1024,256]{1,0:T(8,128)(2,1)}, bf16[1024,256]{1,0:T(8,128)(2,1)S(1)}, u32[]{:S(2)}, u32[]{:S(2)}) collective-permute-start(bf16[1024,256]{1,0:T(8,128)(2,1)} %bitcast.125), channel_id=1, source_target_pairs={{4,8},{8,4},{5,9},{9,5},{6,10},{10,6},{7,11},{11,7},{20,24},{24,20... | collective-permute-start | bytes 1572872 | tf_op jit(solution)/shard_map/ppermute | solution.py:62
  5.6 22.8 %collective-permute-start.4 = (bf16[1024,256]{1,0:T(8,128)(2,1)}, bf16[1024,256]{1,0:T(8,128)(2,1)S(1)}, u32[]{:S(2)}, u32[]{:S(2)}) collective-permute-start(bf16[1024,256]{1,0:T(8,128)(2,1)} %slice_bitcast_fusion), channel_id=1, source_target_pairs={{0,4},{4,0},{8,12},{12,8},{1,5},{5,1},{9,13},{13,9},{2,6},{6,2},{1... | collective-permute-start | bytes 1572872 | tf_op jit(solution)/shard_map/ppermute | solution.py:62
  16.0 14.8 %collective-permute-start.3 = (bf16[1024,256]{1,0:T(8,128)(2,1)S(1)}, bf16[1024,256]{1,0:T(8,128)(2,1)S(1)}, u32[]{:S(2)}, u32[]{:S(2)}) collective-permute-start(bf16[1024,256]{1,0:T(8,128)(2,1)S(1)} %collective-permute-done), channel_id=1, source_target_pairs={{4,8},{8,4},{5,9},{9,5},{6,10},{10,6},{7,11},{11,7},{20,24},{24,20... | collective-permute-start | bytes 1572872 | tf_op jit(solution)/shard_map/ppermute | solution.py:62
  16.7 32.2 %copy-start.1 = (bf16[1,512,14336]{2,1,0:T(8,128)(2,1)S(1)}, bf16[1,512,14336]{2,1,0:T(8,128)(2,1)}, u32[]{:S(2)}) copy-start(bf16[1,512,14336]{2,1,0:T(8,128)(2,1)} %param.6) | copy-start | bytes 44040196
  17.9 22.5 %collective-permute-start.2 = (bf16[1024,256]{1,0:T(8,128)(2,1)S(1)}, bf16[1024,256]{1,0:T(8,128)(2,1)S(1)}, u32[]{:S(2)}, u32[]{:S(2)}) collective-permute-start(bf16[1024,256]{1,0:T(8,128)(2,1)S(1)} %slice_select_fusion.1), channel_id=1, source_target_pairs={{0,4},{4,0},{8,12},{12,8},{1,5},{5,1},{9,13},{13,9},{2,6},{6,2},{1... | collective-permute-start | bytes 1572872 | tf_op jit(solution)/shard_map/ppermute | solution.py:62
  28.4 13.1 %collective-permute-start.6 = (bf16[1024,256]{1,0:T(8,128)(2,1)S(1)}, bf16[1024,256]{1,0:T(8,128)(2,1)S(1)}, u32[]{:S(2)}, u32[]{:S(2)}) collective-permute-start(bf16[1024,256]{1,0:T(8,128)(2,1)S(1)} %slice.121), channel_id=1, source_target_pairs={{4,8},{8,4},{5,9},{9,5},{6,10},{10,6},{7,11},{11,7},{20,24},{24,20... | collective-permute-start | bytes 1572872 | tf_op jit(solution)/shard_map/ppermute | solution.py:62
  30.9 19.6 %collective-permute-start.8 = (bf16[1024,256]{1,0:T(8,128)(2,1)S(1)}, bf16[1024,256]{1,0:T(8,128)(2,1)S(1)}, u32[]{:S(2)}, u32[]{:S(2)}) collective-permute-start(bf16[1024,256]{1,0:T(8,128)(2,1)S(1)} %slice.122), channel_id=1, source_target_pairs={{4,8},{8,4},{5,9},{9,5},{6,10},{10,6},{7,11},{11,7},{20,24},{24,20... | collective-permute-start | bytes 1572872 | tf_op jit(solution)/shard_map/ppermute | solution.py:62
  31.7 21.1 %collective-permute-start.5 = (bf16[1024,256]{1,0:T(8,128)(2,1)S(1)}, bf16[1024,256]{1,0:T(8,128)(2,1)S(1)}, u32[]{:S(2)}, u32[]{:S(2)}) collective-permute-start(bf16[1024,256]{1,0:T(8,128)(2,1)S(1)} %slice_select_fusion), channel_id=1, source_target_pairs={{0,4},{4,0},{8,12},{12,8},{1,5},{5,1},{9,13},{13,9},{2,6},{6,2},{1... | collective-permute-start | bytes 1572872 | tf_op jit(solution)/shard_map/ppermute | solution.py:62
  41.7 24.0 %collective-permute-start.7 = (bf16[1024,256]{1,0:T(8,128)(2,1)S(1)}, bf16[1024,256]{1,0:T(8,128)(2,1)S(1)}, u32[]{:S(2)}, u32[]{:S(2)}) collective-permute-start(bf16[1024,256]{1,0:T(8,128)(2,1)S(1)} %maximum_select_fusion), channel_id=1, source_target_pairs={{0,4},{4,0},{8,12},{12,8},{1,5},{5,1},{9,13},{13,9},{2,6},{6,2},{1... | collective-permute-start | bytes 1572872 | tf_op jit(solution)/shard_map/ppermute | solution.py:62
  48.1 17.6 %collective-permute-start.11 = (bf16[1024,256]{1,0:T(8,128)(2,1)S(1)}, bf16[1024,256]{1,0:T(8,128)(2,1)S(1)}, u32[]{:S(2)}, u32[]{:S(2)}) collective-permute-start(bf16[1024,256]{1,0:T(8,128)(2,1)S(1)} %slice.135), channel_id=1, source_target_pairs={{4,8},{8,4},{5,9},{9,5},{6,10},{10,6},{7,11},{11,7},{20,24},{24,20... | collective-permute-start | bytes 1572872 | tf_op jit(solution)/shard_map/ppermute | solution.py:62
  49.3 13.8 %copy-start.2 = (bf16[1,512,4096]{2,1,0:T(8,128)(2,1)S(1)}, bf16[1,512,4096]{2,1,0:T(8,128)(2,1)}, u32[]{:S(2)}) copy-start(bf16[1,512,4096]{2,1,0:T(8,128)(2,1)} %param.5) | copy-start | bytes 12582916
  50.5 21.9 %collective-permute-start.13 = (bf16[512,256]{1,0:T(8,128)(2,1)S(1)}, bf16[512,256]{1,0:T(8,128)(2,1)S(1)}, u32[]{:S(2)}, u32[]{:S(2)}) collective-permute-start(bf16[512,256]{1,0:T(8,128)(2,1)S(1)} %slice.137), channel_id=1, source_target_pairs={{4,8},{8,4},{5,9},{9,5},{6,10},{10,6},{7,11},{11,7},{20,24},{24,20... | collective-permute-start | bytes 786440 | tf_op jit(solution)/shard_map/ppermute | solution.py:62
  52.9 22.3 %collective-permute-start.9 = (bf16[1024,256]{1,0:T(8,128)(2,1)S(1)}, bf16[1024,256]{1,0:T(8,128)(2,1)S(1)}, u32[]{:S(2)}, u32[]{:S(2)}) collective-permute-start(bf16[1024,256]{1,0:T(8,128)(2,1)S(1)} %maximum_select_fusion.1), channel_id=1, source_target_pairs={{0,4},{4,0},{8,12},{12,8},{1,5},{5,1},{9,13},{13,9},{2,6},{6,2},{1... | collective-permute-start | bytes 1572872 | tf_op jit(solution)/shard_map/ppermute | solution.py:62
  64.1 15.6 %collective-permute-start.10 = (f32[512,256]{1,0:T(8,128)S(1)}, f32[512,256]{1,0:T(8,128)S(1)}, u32[]{:S(2)}, u32[]{:S(2)}) collective-permute-start(f32[512,256]{1,0:T(8,128)S(1)} %fusion.2), channel_id=1, source_target_pairs={{0,2},{2,0},{1,3},{3,1},{4,6},{6,4},{5,7},{7,5},{8,10},{10,8},{9,1... | collective-permute-start | bytes 1572872 | tf_op jit(solution)/shard_map/ppermute | solution.py:128
  65.9 20.5 %collective-permute-start.12 = (bf16[1024,256]{1,0:T(8,128)(2,1)S(1)}, bf16[1024,256]{1,0:T(8,128)(2,1)S(1)}, u32[]{:S(2)}, u32[]{:S(2)}) collective-permute-start(bf16[1024,256]{1,0:T(8,128)(2,1)S(1)} %maximum_select_fusion.2), channel_id=1, source_target_pairs={{0,4},{4,0},{8,12},{12,8},{1,5},{5,1},{9,13},{13,9},{2,6},{6,2},{1... | collective-permute-start | bytes 1572872 | tf_op jit(solution)/shard_map/ppermute | solution.py:62
  70.6 15.9 %collective-permute-start.15 = (bf16[1024,256]{1,0:T(8,128)(2,1)S(1)}, bf16[1024,256]{1,0:T(8,128)(2,1)S(1)}, u32[]{:S(2)}, u32[]{:S(2)}) collective-permute-start(bf16[1024,256]{1,0:T(8,128)(2,1)S(1)} %collective-permute-done.4), channel_id=1, source_target_pairs={{4,8},{8,4},{5,9},{9,5},{6,10},{10,6},{7,11},{11,7},{20,24},{24,20... | collective-permute-start | bytes 1572872 | tf_op jit(solution)/shard_map/ppermute | solution.py:62
  72.4 20.8 %collective-permute-start.17 = (bf16[1024,256]{1,0:T(8,128)(2,1)S(1)}, bf16[1024,256]{1,0:T(8,128)(2,1)S(1)}, u32[]{:S(2)}, u32[]{:S(2)}) collective-permute-start(bf16[1024,256]{1,0:T(8,128)(2,1)S(1)} %collective-permute-done.2), channel_id=1, source_target_pairs={{4,8},{8,4},{5,9},{9,5},{6,10},{10,6},{7,11},{11,7},{20,24},{24,20... | collective-permute-start | bytes 1572872 | tf_op jit(solution)/shard_map/ppermute | solution.py:62
  75.2 16.8 %collective-permute-start.14 = (bf16[512,256]{1,0:T(8,128)(2,1)S(1)}, bf16[512,256]{1,0:T(8,128)(2,1)S(1)}, u32[]{:S(2)}, u32[]{:S(2)}) collective-permute-start(bf16[512,256]{1,0:T(8,128)(2,1)S(1)} %slice_select_fusion.2), channel_id=1, source_target_pairs={{0,4},{4,0},{8,12},{12,8},{1,5},{5,1},{9,13},{13,9},{2,6},{6,2},{1... | collective-permute-start | bytes 786440 | tf_op jit(solution)/shard_map/ppermute | solution.py:62
  80.1 35.9 %collective-permute-start.21 = (s16[512,256]{1,0:T(8,128)(2,1)S(1)}, s16[512,256]{1,0:T(8,128)(2,1)S(1)}, u32[]{:S(2)}, u32[]{:S(2)}) collective-permute-start(s16[512,256]{1,0:T(8,128)(2,1)S(1)} %fusion.50), channel_id=1, source_target_pairs={{0,4},{12,8},{1,5},{13,9},{2,6},{14,10},{3,7},{15,11},{16,20},{28,... | collective-permute-start | bytes 786440 | tf_op jit(solution)/shard_map/ppermute | solution.py:133
  86.6 21.5 %collective-permute-start.16 = (bf16[1024,256]{1,0:T(8,128)(2,1)S(1)}, bf16[1024,256]{1,0:T(8,128)(2,1)S(1)}, u32[]{:S(2)}, u32[]{:S(2)}) collective-permute-start(bf16[1024,256]{1,0:T(8,128)(2,1)S(1)} %maximum_select_fusion.3), channel_id=1, source_target_pairs={{0,4},{4,0},{8,12},{12,8},{1,5},{5,1},{9,13},{13,9},{2,6},{6,2},{1... | collective-permute-start | bytes 1572872 | tf_op jit(solution)/shard_map/ppermute | solution.py:62
  88.5 20.6 %collective-permute-start.19 = (bf16[1024,256]{1,0:T(8,128)(2,1)S(1)}, bf16[1024,256]{1,0:T(8,128)(2,1)S(1)}, u32[]{:S(2)}, u32[]{:S(2)}) collective-permute-start(bf16[1024,256]{1,0:T(8,128)(2,1)S(1)} %collective-permute-done.5), channel_id=1, source_target_pairs={{4,8},{8,4},{5,9},{9,5},{6,10},{10,6},{7,11},{11,7},{20,24},{24,20... | collective-permute-start | bytes 1572872 | tf_op jit(solution)/shard_map/ppermute | solution.py:62
  93.4 22.2 %collective-permute-start.18 = (bf16[1024,256]{1,0:T(8,128)(2,1)S(1)}, bf16[1024,256]{1,0:T(8,128)(2,1)S(1)}, u32[]{:S(2)}, u32[]{:S(2)}) collective-permute-start(bf16[1024,256]{1,0:T(8,128)(2,1)S(1)} %maximum_select_fusion.4), channel_id=1, source_target_pairs={{0,4},{4,0},{8,12},{12,8},{1,5},{5,1},{9,13},{13,9},{2,6},{6,2},{1... | collective-permute-start | bytes 1572872 | tf_op jit(solution)/shard_map/ppermute | solution.py:62
  109.1 15.7 %collective-permute-start.20 = (bf16[1024,256]{1,0:T(8,128)(2,1)S(1)}, bf16[1024,256]{1,0:T(8,128)(2,1)S(1)}, u32[]{:S(2)}, u32[]{:S(2)}) collective-permute-start(bf16[1024,256]{1,0:T(8,128)(2,1)S(1)} %collective-permute-done.19), channel_id=1, source_target_pairs={{4,0},{8,12},{5,1},{9,13},{6,2},{10,14},{7,3},{11,15},{20,16},{24,... | collective-permute-start | bytes 1572872 | tf_op jit(solution)/shard_map/ppermute | solution.py:62
  110.4 7.5 %collective-permute-start.23 = (bf16[512,256]{1,0:T(8,128)(2,1)S(1)}, bf16[512,256]{1,0:T(8,128)(2,1)S(1)}, u32[]{:S(2)}, u32[]{:S(2)}) collective-permute-start(bf16[512,256]{1,0:T(8,128)(2,1)S(1)} %collective-permute-done.14), channel_id=1, source_target_pairs={{4,8},{8,4},{5,9},{9,5},{6,10},{10,6},{7,11},{11,7},{20,24},{24,20... | collective-permute-start | bytes 786440 | tf_op jit(solution)/shard_map/ppermute | solution.py:62
  116.2 8.6 %collective-permute-start.22 = (f32[2,256]{1,0:T(2,128)S(1)}, f32[2,256]{1,0:T(2,128)S(1)}, u32[]{:S(2)}, u32[]{:S(2)}) collective-permute-start(f32[2,256]{1,0:T(2,128)S(1)} %bitcast_reduce_fusion.1), channel_id=1, source_target_pairs={{4,0},{8,12},{5,1},{9,13},{6,2},{10,14},{7,3},{11,15},{20,16},{24,... | collective-permute-start | bytes 6152 | tf_op jit(solution)/shard_map/ppermute | solution.py:177
  117.9 9.6 %collective-permute-start.24 = (bf16[512,256]{1,0:T(8,128)(2,1)S(1)}, bf16[512,256]{1,0:T(8,128)(2,1)S(1)}, u32[]{:S(2)}, u32[]{:S(2)}) collective-permute-start(bf16[512,256]{1,0:T(8,128)(2,1)S(1)} %collective-permute-done.23), channel_id=1, source_target_pairs={{4,0},{8,12},{5,1},{9,13},{6,2},{10,14},{7,3},{11,15},{20,16},{24,... | collective-permute-start | bytes 786440 | tf_op jit(solution)/shard_map/ppermute | solution.py:62
  128.1 3.6 %collective-permute-start.25 = (f32[2,32]{1,0:T(2,128)S(1)}, f32[2,32]{1,0:T(2,128)S(1)}, u32[]{:S(2)}, u32[]{:S(2)}) collective-permute-start(f32[2,32]{1,0:T(2,128)S(1)} %reduce_sum.29), channel_id=1, source_target_pairs={{0,2},{2,0},{1,3},{3,1},{4,6},{6,4},{5,7},{7,5},{8,10},{10,8},{9,1... | collective-permute-start | bytes 776 | tf_op jit(solution)/shard_map/ppermute | solution.py:183

commit v5 on v4

--- a/solution.py
+++ b/solution.py
@@ -121,6 +121,8 @@
     x["C2E"] = trade(trade.ready(y["C2E"]), TO_END)
     x["C3E"] = trade(y["C3E"], TO_END)
 
+    x["C1E"] = after(x["C1E"], y["C3E"])
+
     proj_acts = dot(columns(after(acts, x["A"], y["AM"]), place, 0, unit), left)
     proj_acts += dot(columns(acts, near, 0, unit), x["A"])
     proj_acts += dot(columns(acts, far_middle, 0, unit), either(x["AM"], y["AM"]))

time: 133 us -> 133 us (level)
  no operation moved by 1% of the time
where the time goes in v5:
time: 133 us
  starting transfers between devices  72 us (54%)
  waiting for transfers between devices  38.9 us (29%)
  matrix products  14 us (11%)
  other arithmetic  3.98 us (3%)
  local copies, waits for them, and re-layouts  3.47 us (3%)
    ppermute x22, starting transfers between devices, __call__(): self.came.append(lax.ppermute(x, 'dp', pairs or self.pairs))  65.7 us
    ppermute x22, waiting for transfers between devices, __call__(): self.came.append(lax.ppermute(x, 'dp', pairs or self.pairs))  30.6 us
    dot_general x27, matrix products, dot(): return jnp.dot(a, b, preferred_element_type=jnp.float32)  14 us
    ppermute x1, waiting for transfers between devices, on_line(): lax.ppermute(column_scores(guest_acts.astype(jnp.float32), guest_grads, s...  6.2 us
  transfers between devices with their start and end apart: 26, of which 10 were waited for; matrix products, arithmetic and copies ran while one was open for 15% of the time, Pallas kernels for 0%

profile of v5, /device:TPU:0, one launch (start us, length us, event | category | flops | bytes accessed | tf_op | source)
XLA Modules:
  0.0 132.9 jit_solution(4105559829278821904)
XLA Ops:
  0.0 3.0 %collective-permute-start = (bf16[1024,256]{1,0:T(8,128)(2,1)}, bf16[1024,256]{1,0:T(8,128)(2,1)S(1)}, u32[]{:S(2)}, u32[]{:S(2)}) collective-permute-start(bf16[1024,256]{1,0:T(8,128)(2,1)} %bitcast.124), channel_id=1, source_target_pairs={{0,4},{4,0},{8,12},{12,8},{1,5},{5,1},{9,13},{13,9},{2,6},{6,2},{1... | collective-permute-start | bytes 1572872 | tf_op jit(solution)/shard_map/ppermute | solution.py:62
  3.0 0.7 collective-permute-start.1
  3.7 1.9 %slice_bitcast_fusion = bf16[1024,256]{1,0:T(8,128)(2,1)} fusion(bf16[1,3584,256]{2,1,0:T(8,128)(2,1)} %param.8), kind=kLoop, calls=%fused_computation.87 | loop fusion | bytes 1048576 | tf_op jit(solution)/shard_map/slice | solution.py:103
  5.6 4.4 %collective-permute-start.4 = (bf16[1024,256]{1,0:T(8,128)(2,1)}, bf16[1024,256]{1,0:T(8,128)(2,1)S(1)}, u32[]{:S(2)}, u32[]{:S(2)}) collective-permute-start(bf16[1024,256]{1,0:T(8,128)(2,1)} %slice_bitcast_fusion), channel_id=1, source_target_pairs={{0,4},{4,0},{8,12},{12,8},{1,5},{5,1},{9,13},{13,9},{2,6},{6,2},{1... | collective-permute-start | bytes 1572872 | tf_op jit(solution)/shard_map/ppermute | solution.py:62
  10.0 0.7 fusion.143
  10.7 5.3 %collective-permute-done = bf16[1024,256]{1,0:T(8,128)(2,1)S(1)} collective-permute-done((bf16[1024,256]{1,0:T(8,128)(2,1)}, bf16[1024,256]{1,0:T(8,128)(2,1)S(1)}, u32[]{:S(2)}, u32[]{:S(2)}) %collective-permute-start) | collective-permute-done | bytes 524320 | tf_op jit(solution)/shard_map/ppermute | solution.py:62
  16.0 0.7 collective-permute-start.3
  16.7 1.3 slice_select_fusion.1
  17.9 6.9 %collective-permute-start.2 = (bf16[1024,256]{1,0:T(8,128)(2,1)S(1)}, bf16[1024,256]{1,0:T(8,128)(2,1)S(1)}, u32[]{:S(2)}, u32[]{:S(2)}) collective-permute-start(bf16[1024,256]{1,0:T(8,128)(2,1)S(1)} %slice_select_fusion.1), channel_id=1, source_target_pairs={{0,4},{4,0},{8,12},{12,8},{1,5},{5,1},{9,13},{13,9},{2,6},{6,2},{1... | collective-permute-start | bytes 1572872 | tf_op jit(solution)/shard_map/ppermute | solution.py:62
  24.9 1.7 %fusion.17 = f32[512,256]{1,0:T(8,128)S(1)} fusion(bf16[1024,256]{1,0:T(8,128)(2,1)S(1)} %collective-permute-done, bf16[1,512,4096]{2,1,0:T(8,128)(2,1)} %param.5, s32[]{:T(128)S(6)} %select_n.194), kind=kOutput, calls=%fused_computation.28 | convolution fusion | flops 268435456 | bytes 2097156 | tf_op jit(solution)/shard_map/dot_general | solution.py:36
  26.6 1.8 %convolution_add_fusion.4 = f32[512,256]{1,0:T(8,128)S(1)} fusion(f32[512,256]{1,0:T(8,128)S(1)} %fusion.17, bf16[512,4096]{1,0:T(8,128)(2,1)} %bitcast.123, s32[]{:T(128)S(6)} %select_n.193, bf16[1,1024,256]{2,1,0:T(8,128)(2,1)} %param.7), kind=kOutput, calls=%fused_computation.6 | convolution fusion | flops 268566528 | bytes 2621444 | tf_op jit(solution)/shard_map/dot_general | solution.py:36
  28.4 0.7 collective-permute-start.6
  29.2 1.7 %fusion.27 = f32[512,256]{1,0:T(8,128)S(1)} fusion(bf16[1024,256]{1,0:T(8,128)(2,1)S(1)} %collective-permute-done.4, bf16[1,512,14336]{2,1,0:T(8,128)(2,1)} %param.6, s32[]{:T(128)S(6)} %select_n.178), kind=kOutput, calls=%fused_computation.38 | convolution fusion | flops 268435456 | bytes 2097156 | tf_op jit(solution)/shard_map/dot_general | solution.py:36
  30.9 0.7 collective-permute-start.8
  31.7 8.8 %collective-permute-start.5 = (bf16[1024,256]{1,0:T(8,128)(2,1)S(1)}, bf16[1024,256]{1,0:T(8,128)(2,1)S(1)}, u32[]{:S(2)}, u32[]{:S(2)}) collective-permute-start(bf16[1024,256]{1,0:T(8,128)(2,1)S(1)} %slice_select_fusion), channel_id=1, source_target_pairs={{0,4},{4,0},{8,12},{12,8},{1,5},{5,1},{9,13},{13,9},{2,6},{6,2},{1... | collective-permute-start | bytes 1572872 | tf_op jit(solution)/shard_map/ppermute | solution.py:62
  40.5 1.1 constant_dynamic-slice_fusion.9
  41.7 6.4 %collective-permute-start.7 = (bf16[1024,256]{1,0:T(8,128)(2,1)S(1)}, bf16[1024,256]{1,0:T(8,128)(2,1)S(1)}, u32[]{:S(2)}, u32[]{:S(2)}) collective-permute-start(bf16[1024,256]{1,0:T(8,128)(2,1)S(1)} %maximum_select_fusion), channel_id=1, source_target_pairs={{0,4},{4,0},{8,12},{12,8},{1,5},{5,1},{9,13},{13,9},{2,6},{6,2},{1... | collective-permute-start | bytes 1572872 | tf_op jit(solution)/shard_map/ppermute | solution.py:62
  48.1 0.7 collective-permute-start.11
  48.9 0.5 fusion.25
  49.3 1.1 fusion
  50.5 0.8 collective-permute-start.13
  51.3 1.4 %collective-permute-done.5 = bf16[1024,256]{1,0:T(8,128)(2,1)S(1)} collective-permute-done((bf16[1024,256]{1,0:T(8,128)(2,1)S(1)}, bf16[1024,256]{1,0:T(8,128)(2,1)S(1)}, u32[]{:S(2)}, u32[]{:S(2)}) %collective-permute-start.5) | collective-permute-done | bytes 524320 | tf_op jit(solution)/shard_map/ppermute | solution.py:62
  52.9 10.2 %collective-permute-start.9 = (bf16[1024,256]{1,0:T(8,128)(2,1)S(1)}, bf16[1024,256]{1,0:T(8,128)(2,1)S(1)}, u32[]{:S(2)}, u32[]{:S(2)}) collective-permute-start(bf16[1024,256]{1,0:T(8,128)(2,1)S(1)} %maximum_select_fusion.1), channel_id=1, source_target_pairs={{0,4},{4,0},{8,12},{12,8},{1,5},{5,1},{9,13},{13,9},{2,6},{6,2},{1... | collective-permute-start | bytes 1572872 | tf_op jit(solution)/shard_map/ppermute | solution.py:62
  63.1 0.4 fusion.14
  63.6 0.5 fusion.2
  64.1 1.6 %collective-permute-start.10 = (f32[512,256]{1,0:T(8,128)S(1)}, f32[512,256]{1,0:T(8,128)S(1)}, u32[]{:S(2)}, u32[]{:S(2)}) collective-permute-start(f32[512,256]{1,0:T(8,128)S(1)} %fusion.2), channel_id=1, source_target_pairs={{0,2},{2,0},{1,3},{3,1},{4,6},{6,4},{5,7},{7,5},{8,10},{10,8},{9,1... | collective-permute-start | bytes 1572872 | tf_op jit(solution)/shard_map/ppermute | solution.py:130
  65.9 4.7 %collective-permute-start.12 = (bf16[1024,256]{1,0:T(8,128)(2,1)S(1)}, bf16[1024,256]{1,0:T(8,128)(2,1)S(1)}, u32[]{:S(2)}, u32[]{:S(2)}) collective-permute-start(bf16[1024,256]{1,0:T(8,128)(2,1)S(1)} %maximum_select_fusion.2), channel_id=1, source_target_pairs={{0,4},{4,0},{8,12},{12,8},{1,5},{5,1},{9,13},{13,9},{2,6},{6,2},{1... | collective-permute-start | bytes 1572872 | tf_op jit(solution)/shard_map/ppermute | solution.py:62
  70.6 0.7 collective-permute-start.15
  71.3 0.5 add_add_fusion.1
  72.0 0.4 fusion.21
  72.4 0.7 collective-permute-start.17
  73.1 2.1 %collective-permute-done.9 = bf16[1024,256]{1,0:T(8,128)(2,1)S(1)} collective-permute-done((bf16[1024,256]{1,0:T(8,128)(2,1)S(1)}, bf16[1024,256]{1,0:T(8,128)(2,1)S(1)}, u32[]{:S(2)}, u32[]{:S(2)}) %collective-permute-start.9) | collective-permute-done | bytes 524320 | tf_op jit(solution)/shard_map/ppermute | solution.py:62
  75.2 4.5 %collective-permute-start.14 = (bf16[512,256]{1,0:T(8,128)(2,1)S(1)}, bf16[512,256]{1,0:T(8,128)(2,1)S(1)}, u32[]{:S(2)}, u32[]{:S(2)}) collective-permute-start(bf16[512,256]{1,0:T(8,128)(2,1)S(1)} %slice_select_fusion.2), channel_id=1, source_target_pairs={{0,4},{4,0},{8,12},{12,8},{1,5},{5,1},{9,13},{13,9},{2,6},{6,2},{1... | collective-permute-start | bytes 786440 | tf_op jit(solution)/shard_map/ppermute | solution.py:62
  80.1 1.9 %collective-permute-start.22 = (s16[512,256]{1,0:T(8,128)(2,1)S(1)}, s16[512,256]{1,0:T(8,128)(2,1)S(1)}, u32[]{:S(2)}, u32[]{:S(2)}) collective-permute-start(s16[512,256]{1,0:T(8,128)(2,1)S(1)} %fusion.50), channel_id=1, source_target_pairs={{0,4},{12,8},{1,5},{13,9},{2,6},{14,10},{3,7},{15,11},{16,20},{28,... | collective-permute-start | bytes 786440 | tf_op jit(solution)/shard_map/ppermute | solution.py:135
  82.2 0.2 convolution_add_fusion.8
  82.5 0.2 fusion.6
  82.7 0.5 add_add_fusion
  83.2 3.3 %collective-permute-done.12 = bf16[1024,256]{1,0:T(8,128)(2,1)S(1)} collective-permute-done((bf16[1024,256]{1,0:T(8,128)(2,1)S(1)}, bf16[1024,256]{1,0:T(8,128)(2,1)S(1)}, u32[]{:S(2)}, u32[]{:S(2)}) %collective-permute-start.12) | collective-permute-done | bytes 524320 | tf_op jit(solution)/shard_map/ppermute | solution.py:62
  86.6 1.8 %collective-permute-start.16 = (bf16[1024,256]{1,0:T(8,128)(2,1)S(1)}, bf16[1024,256]{1,0:T(8,128)(2,1)S(1)}, u32[]{:S(2)}, u32[]{:S(2)}) collective-permute-start(bf16[1024,256]{1,0:T(8,128)(2,1)S(1)} %maximum_select_fusion.3), channel_id=1, source_target_pairs={{0,4},{4,0},{8,12},{12,8},{1,5},{5,1},{9,13},{13,9},{2,6},{6,2},{1... | collective-permute-start | bytes 1572872 | tf_op jit(solution)/shard_map/ppermute | solution.py:62
  88.5 0.7 collective-permute-start.19
  89.4 0.2 fusion.5
  89.6 2.4 %collective-permute-done.14 = bf16[512,256]{1,0:T(8,128)(2,1)S(1)} collective-permute-done((bf16[512,256]{1,0:T(8,128)(2,1)S(1)}, bf16[512,256]{1,0:T(8,128)(2,1)S(1)}, u32[]{:S(2)}, u32[]{:S(2)}) %collective-permute-start.14) | collective-permute-done | bytes 262176 | tf_op jit(solution)/shard_map/ppermute | solution.py:62
  92.0 0.3 fusion.47
  92.4 0.3 fusion.45
  92.7 0.5 fusion.7
  93.4 5.4 %collective-permute-start.18 = (bf16[1024,256]{1,0:T(8,128)(2,1)S(1)}, bf16[1024,256]{1,0:T(8,128)(2,1)S(1)}, u32[]{:S(2)}, u32[]{:S(2)}) collective-permute-start(bf16[1024,256]{1,0:T(8,128)(2,1)S(1)} %maximum_select_fusion.4), channel_id=1, source_target_pairs={{0,4},{4,0},{8,12},{12,8},{1,5},{5,1},{9,13},{13,9},{2,6},{6,2},{1... | collective-permute-start | bytes 1572872 | tf_op jit(solution)/shard_map/ppermute | solution.py:62
  98.8 0.7 collective-permute-start.20
  99.5 8.7 %collective-permute-done.16 = bf16[1024,256]{1,0:T(8,128)(2,1)S(1)} collective-permute-done((bf16[1024,256]{1,0:T(8,128)(2,1)S(1)}, bf16[1024,256]{1,0:T(8,128)(2,1)S(1)}, u32[]{:S(2)}, u32[]{:S(2)}) %collective-permute-start.16) | collective-permute-done | bytes 524320 | tf_op jit(solution)/shard_map/ppermute | solution.py:62
  108.2 0.4 convolution_add_fusion.1
  108.6 0.2 fusion.82
  108.8 0.2 fusion.4
  109.1 1.3 collective-permute-start.21
  110.4 5.1 %collective-permute-done.18 = bf16[1024,256]{1,0:T(8,128)(2,1)S(1)} collective-permute-done((bf16[1024,256]{1,0:T(8,128)(2,1)S(1)}, bf16[1024,256]{1,0:T(8,128)(2,1)S(1)}, u32[]{:S(2)}, u32[]{:S(2)}) %collective-permute-start.18) | collective-permute-done | bytes 524320 | tf_op jit(solution)/shard_map/ppermute | solution.py:62
  115.8 0.2 convolution_add_fusion.5
  116.2 1.3 collective-permute-start.23
  117.5 0.5 convolution_add_fusion
  117.9 1.3 collective-permute-start.24
  119.2 6.2 %collective-permute-done.23 = f32[2,256]{1,0:T(2,128)S(1)} collective-permute-done((f32[2,256]{1,0:T(2,128)S(1)}, f32[2,256]{1,0:T(2,128)S(1)}, u32[]{:S(2)}, u32[]{:S(2)}) %collective-permute-start.23) | collective-permute-done | bytes 2080 | tf_op jit(solution)/shard_map/ppermute | solution.py:179
  125.4 0.4 fusion.9
  126.0 2.3 %collective-permute-done.24 = bf16[512,256]{1,0:T(8,128)(2,1)S(1)} collective-permute-done((bf16[512,256]{1,0:T(8,128)(2,1)S(1)}, bf16[512,256]{1,0:T(8,128)(2,1)S(1)}, u32[]{:S(2)}, u32[]{:S(2)}) %collective-permute-start.24) | collective-permute-done | bytes 262176 | tf_op jit(solution)/shard_map/ppermute | solution.py:62
  128.2 0.3 bitcast_reduce_fusion
  128.8 1.5 %collective-permute-start.25 = (f32[2,32]{1,0:T(2,128)S(1)}, f32[2,32]{1,0:T(2,128)S(1)}, u32[]{:S(2)}, u32[]{:S(2)}) collective-permute-start(f32[2,32]{1,0:T(2,128)S(1)} %reduce_sum.29), channel_id=1, source_target_pairs={{0,2},{2,0},{1,3},{3,1},{4,6},{6,4},{5,7},{7,5},{8,10},{10,8},{9,1... | collective-permute-start | bytes 776 | tf_op jit(solution)/shard_map/ppermute | solution.py:185
  130.2 2.1 %collective-permute-done.25 = f32[2,32]{1,0:T(2,128)S(1)} collective-permute-done((f32[2,32]{1,0:T(2,128)S(1)}, f32[2,32]{1,0:T(2,128)S(1)}, u32[]{:S(2)}, u32[]{:S(2)}) %collective-permute-start.25) | collective-permute-done | bytes 288 | tf_op jit(solution)/shard_map/ppermute | solution.py:185
  132.3 0.6 multiply_bitcast_fusion
  (53 shorter events, 2.9 us)
Async XLA Ops:
  0.0 28.4 %copy-start = (bf16[1,3584,256]{2,1,0:T(8,128)(2,1)S(1)}, bf16[1,3584,256]{2,1,0:T(8,128)(2,1)}, u32[]{:S(2)}) copy-start(bf16[1,3584,256]{2,1,0:T(8,128)(2,1)} %param.8) | copy-start | bytes 5505028
  0.0 16.0 %collective-permute-start = (bf16[1024,256]{1,0:T(8,128)(2,1)}, bf16[1024,256]{1,0:T(8,128)(2,1)S(1)}, u32[]{:S(2)}, u32[]{:S(2)}) collective-permute-start(bf16[1024,256]{1,0:T(8,128)(2,1)} %bitcast.124), channel_id=1, source_target_pairs={{0,4},{4,0},{8,12},{12,8},{1,5},{5,1},{9,13},{13,9},{2,6},{6,2},{1... | collective-permute-start | bytes 1572872 | tf_op jit(solution)/shard_map/ppermute | solution.py:62
  3.0 13.0 %collective-permute-start.1 = (bf16[1024,256]{1,0:T(8,128)(2,1)}, bf16[1024,256]{1,0:T(8,128)(2,1)S(1)}, u32[]{:S(2)}, u32[]{:S(2)}) collective-permute-start(bf16[1024,256]{1,0:T(8,128)(2,1)} %bitcast.125), channel_id=1, source_target_pairs={{4,8},{8,4},{5,9},{9,5},{6,10},{10,6},{7,11},{11,7},{20,24},{24,20... | collective-permute-start | bytes 1572872 | tf_op jit(solution)/shard_map/ppermute | solution.py:62
  5.6 22.8 %collective-permute-start.4 = (bf16[1024,256]{1,0:T(8,128)(2,1)}, bf16[1024,256]{1,0:T(8,128)(2,1)S(1)}, u32[]{:S(2)}, u32[]{:S(2)}) collective-permute-start(bf16[1024,256]{1,0:T(8,128)(2,1)} %slice_bitcast_fusion), channel_id=1, source_target_pairs={{0,4},{4,0},{8,12},{12,8},{1,5},{5,1},{9,13},{13,9},{2,6},{6,2},{1... | collective-permute-start | bytes 1572872 | tf_op jit(solution)/shard_map/ppermute | solution.py:62
  16.0 14.8 %collective-permute-start.3 = (bf16[1024,256]{1,0:T(8,128)(2,1)S(1)}, bf16[1024,256]{1,0:T(8,128)(2,1)S(1)}, u32[]{:S(2)}, u32[]{:S(2)}) collective-permute-start(bf16[1024,256]{1,0:T(8,128)(2,1)S(1)} %collective-permute-done), channel_id=1, source_target_pairs={{4,8},{8,4},{5,9},{9,5},{6,10},{10,6},{7,11},{11,7},{20,24},{24,20... | collective-permute-start | bytes 1572872 | tf_op jit(solution)/shard_map/ppermute | solution.py:62
  16.7 32.2 %copy-start.1 = (bf16[1,512,14336]{2,1,0:T(8,128)(2,1)S(1)}, bf16[1,512,14336]{2,1,0:T(8,128)(2,1)}, u32[]{:S(2)}) copy-start(bf16[1,512,14336]{2,1,0:T(8,128)(2,1)} %param.6) | copy-start | bytes 44040196
  17.9 22.5 %collective-permute-start.2 = (bf16[1024,256]{1,0:T(8,128)(2,1)S(1)}, bf16[1024,256]{1,0:T(8,128)(2,1)S(1)}, u32[]{:S(2)}, u32[]{:S(2)}) collective-permute-start(bf16[1024,256]{1,0:T(8,128)(2,1)S(1)} %slice_select_fusion.1), channel_id=1, source_target_pairs={{0,4},{4,0},{8,12},{12,8},{1,5},{5,1},{9,13},{13,9},{2,6},{6,2},{1... | collective-permute-start | bytes 1572872 | tf_op jit(solution)/shard_map/ppermute | solution.py:62
  28.4 13.1 %collective-permute-start.6 = (bf16[1024,256]{1,0:T(8,128)(2,1)S(1)}, bf16[1024,256]{1,0:T(8,128)(2,1)S(1)}, u32[]{:S(2)}, u32[]{:S(2)}) collective-permute-start(bf16[1024,256]{1,0:T(8,128)(2,1)S(1)} %slice.121), channel_id=1, source_target_pairs={{4,8},{8,4},{5,9},{9,5},{6,10},{10,6},{7,11},{11,7},{20,24},{24,20... | collective-permute-start | bytes 1572872 | tf_op jit(solution)/shard_map/ppermute | solution.py:62
  30.9 19.6 %collective-permute-start.8 = (bf16[1024,256]{1,0:T(8,128)(2,1)S(1)}, bf16[1024,256]{1,0:T(8,128)(2,1)S(1)}, u32[]{:S(2)}, u32[]{:S(2)}) collective-permute-start(bf16[1024,256]{1,0:T(8,128)(2,1)S(1)} %slice.122), channel_id=1, source_target_pairs={{4,8},{8,4},{5,9},{9,5},{6,10},{10,6},{7,11},{11,7},{20,24},{24,20... | collective-permute-start | bytes 1572872 | tf_op jit(solution)/shard_map/ppermute | solution.py:62
  31.7 21.1 %collective-permute-start.5 = (bf16[1024,256]{1,0:T(8,128)(2,1)S(1)}, bf16[1024,256]{1,0:T(8,128)(2,1)S(1)}, u32[]{:S(2)}, u32[]{:S(2)}) collective-permute-start(bf16[1024,256]{1,0:T(8,128)(2,1)S(1)} %slice_select_fusion), channel_id=1, source_target_pairs={{0,4},{4,0},{8,12},{12,8},{1,5},{5,1},{9,13},{13,9},{2,6},{6,2},{1... | collective-permute-start | bytes 1572872 | tf_op jit(solution)/shard_map/ppermute | solution.py:62
  41.7 24.0 %collective-permute-start.7 = (bf16[1024,256]{1,0:T(8,128)(2,1)S(1)}, bf16[1024,256]{1,0:T(8,128)(2,1)S(1)}, u32[]{:S(2)}, u32[]{:S(2)}) collective-permute-start(bf16[1024,256]{1,0:T(8,128)(2,1)S(1)} %maximum_select_fusion), channel_id=1, source_target_pairs={{0,4},{4,0},{8,12},{12,8},{1,5},{5,1},{9,13},{13,9},{2,6},{6,2},{1... | collective-permute-start | bytes 1572872 | tf_op jit(solution)/shard_map/ppermute | solution.py:62
  48.1 17.6 %collective-permute-start.11 = (bf16[1024,256]{1,0:T(8,128)(2,1)S(1)}, bf16[1024,256]{1,0:T(8,128)(2,1)S(1)}, u32[]{:S(2)}, u32[]{:S(2)}) collective-permute-start(bf16[1024,256]{1,0:T(8,128)(2,1)S(1)} %slice.135), channel_id=1, source_target_pairs={{4,8},{8,4},{5,9},{9,5},{6,10},{10,6},{7,11},{11,7},{20,24},{24,20... | collective-permute-start | bytes 1572872 | tf_op jit(solution)/shard_map/ppermute | solution.py:62
  49.3 13.8 %copy-start.2 = (bf16[1,512,4096]{2,1,0:T(8,128)(2,1)S(1)}, bf16[1,512,4096]{2,1,0:T(8,128)(2,1)}, u32[]{:S(2)}) copy-start(bf16[1,512,4096]{2,1,0:T(8,128)(2,1)} %param.5) | copy-start | bytes 12582916
  50.5 21.9 %collective-permute-start.13 = (bf16[512,256]{1,0:T(8,128)(2,1)S(1)}, bf16[512,256]{1,0:T(8,128)(2,1)S(1)}, u32[]{:S(2)}, u32[]{:S(2)}) collective-permute-start(bf16[512,256]{1,0:T(8,128)(2,1)S(1)} %slice.137), channel_id=1, source_target_pairs={{4,8},{8,4},{5,9},{9,5},{6,10},{10,6},{7,11},{11,7},{20,24},{24,20... | collective-permute-start | bytes 786440 | tf_op jit(solution)/shard_map/ppermute | solution.py:62
  52.9 22.3 %collective-permute-start.9 = (bf16[1024,256]{1,0:T(8,128)(2,1)S(1)}, bf16[1024,256]{1,0:T(8,128)(2,1)S(1)}, u32[]{:S(2)}, u32[]{:S(2)}) collective-permute-start(bf16[1024,256]{1,0:T(8,128)(2,1)S(1)} %maximum_select_fusion.1), channel_id=1, source_target_pairs={{0,4},{4,0},{8,12},{12,8},{1,5},{5,1},{9,13},{13,9},{2,6},{6,2},{1... | collective-permute-start | bytes 1572872 | tf_op jit(solution)/shard_map/ppermute | solution.py:62
  64.1 15.6 %collective-permute-start.10 = (f32[512,256]{1,0:T(8,128)S(1)}, f32[512,256]{1,0:T(8,128)S(1)}, u32[]{:S(2)}, u32[]{:S(2)}) collective-permute-start(f32[512,256]{1,0:T(8,128)S(1)} %fusion.2), channel_id=1, source_target_pairs={{0,2},{2,0},{1,3},{3,1},{4,6},{6,4},{5,7},{7,5},{8,10},{10,8},{9,1... | collective-permute-start | bytes 1572872 | tf_op jit(solution)/shard_map/ppermute | solution.py:130
  65.9 20.5 %collective-permute-start.12 = (bf16[1024,256]{1,0:T(8,128)(2,1)S(1)}, bf16[1024,256]{1,0:T(8,128)(2,1)S(1)}, u32[]{:S(2)}, u32[]{:S(2)}) collective-permute-start(bf16[1024,256]{1,0:T(8,128)(2,1)S(1)} %maximum_select_fusion.2), channel_id=1, source_target_pairs={{0,4},{4,0},{8,12},{12,8},{1,5},{5,1},{9,13},{13,9},{2,6},{6,2},{1... | collective-permute-start | bytes 1572872 | tf_op jit(solution)/shard_map/ppermute | solution.py:62
  70.6 15.9 %collective-permute-start.15 = (bf16[1024,256]{1,0:T(8,128)(2,1)S(1)}, bf16[1024,256]{1,0:T(8,128)(2,1)S(1)}, u32[]{:S(2)}, u32[]{:S(2)}) collective-permute-start(bf16[1024,256]{1,0:T(8,128)(2,1)S(1)} %collective-permute-done.4), channel_id=1, source_target_pairs={{4,8},{8,4},{5,9},{9,5},{6,10},{10,6},{7,11},{11,7},{20,24},{24,20... | collective-permute-start | bytes 1572872 | tf_op jit(solution)/shard_map/ppermute | solution.py:62
  72.4 20.8 %collective-permute-start.17 = (bf16[1024,256]{1,0:T(8,128)(2,1)S(1)}, bf16[1024,256]{1,0:T(8,128)(2,1)S(1)}, u32[]{:S(2)}, u32[]{:S(2)}) collective-permute-start(bf16[1024,256]{1,0:T(8,128)(2,1)S(1)} %collective-permute-done.2), channel_id=1, source_target_pairs={{4,8},{8,4},{5,9},{9,5},{6,10},{10,6},{7,11},{11,7},{20,24},{24,20... | collective-permute-start | bytes 1572872 | tf_op jit(solution)/shard_map/ppermute | solution.py:62
  75.2 16.8 %collective-permute-start.14 = (bf16[512,256]{1,0:T(8,128)(2,1)S(1)}, bf16[512,256]{1,0:T(8,128)(2,1)S(1)}, u32[]{:S(2)}, u32[]{:S(2)}) collective-permute-start(bf16[512,256]{1,0:T(8,128)(2,1)S(1)} %slice_select_fusion.2), channel_id=1, source_target_pairs={{0,4},{4,0},{8,12},{12,8},{1,5},{5,1},{9,13},{13,9},{2,6},{6,2},{1... | collective-permute-start | bytes 786440 | tf_op jit(solution)/shard_map/ppermute | solution.py:62
  80.1 35.9 %collective-permute-start.22 = (s16[512,256]{1,0:T(8,128)(2,1)S(1)}, s16[512,256]{1,0:T(8,128)(2,1)S(1)}, u32[]{:S(2)}, u32[]{:S(2)}) collective-permute-start(s16[512,256]{1,0:T(8,128)(2,1)S(1)} %fusion.50), channel_id=1, source_target_pairs={{0,4},{12,8},{1,5},{13,9},{2,6},{14,10},{3,7},{15,11},{16,20},{28,... | collective-permute-start | bytes 786440 | tf_op jit(solution)/shard_map/ppermute | solution.py:135
  86.6 21.5 %collective-permute-start.16 = (bf16[1024,256]{1,0:T(8,128)(2,1)S(1)}, bf16[1024,256]{1,0:T(8,128)(2,1)S(1)}, u32[]{:S(2)}, u32[]{:S(2)}) collective-permute-start(bf16[1024,256]{1,0:T(8,128)(2,1)S(1)} %maximum_select_fusion.3), channel_id=1, source_target_pairs={{0,4},{4,0},{8,12},{12,8},{1,5},{5,1},{9,13},{13,9},{2,6},{6,2},{1... | collective-permute-start | bytes 1572872 | tf_op jit(solution)/shard_map/ppermute | solution.py:62
  88.5 10.3 %collective-permute-start.19 = (bf16[1024,256]{1,0:T(8,128)(2,1)S(1)}, bf16[1024,256]{1,0:T(8,128)(2,1)S(1)}, u32[]{:S(2)}, u32[]{:S(2)}) collective-permute-start(bf16[1024,256]{1,0:T(8,128)(2,1)S(1)} %collective-permute-done.5), channel_id=1, source_target_pairs={{4,8},{8,4},{5,9},{9,5},{6,10},{10,6},{7,11},{11,7},{20,24},{24,20... | collective-permute-start | bytes 1572872 | tf_op jit(solution)/shard_map/ppermute | solution.py:62
  93.4 22.2 %collective-permute-start.18 = (bf16[1024,256]{1,0:T(8,128)(2,1)S(1)}, bf16[1024,256]{1,0:T(8,128)(2,1)S(1)}, u32[]{:S(2)}, u32[]{:S(2)}) collective-permute-start(bf16[1024,256]{1,0:T(8,128)(2,1)S(1)} %maximum_select_fusion.4), channel_id=1, source_target_pairs={{0,4},{4,0},{8,12},{12,8},{1,5},{5,1},{9,13},{13,9},{2,6},{6,2},{1... | collective-permute-start | bytes 1572872 | tf_op jit(solution)/shard_map/ppermute | solution.py:62
  98.8 16.8 %collective-permute-start.20 = (bf16[512,256]{1,0:T(8,128)(2,1)S(1)}, bf16[512,256]{1,0:T(8,128)(2,1)S(1)}, u32[]{:S(2)}, u32[]{:S(2)}) collective-permute-start(bf16[512,256]{1,0:T(8,128)(2,1)S(1)} %collective-permute-done.14), channel_id=1, source_target_pairs={{4,8},{8,4},{5,9},{9,5},{6,10},{10,6},{7,11},{11,7},{20,24},{24,20... | collective-permute-start | bytes 786440 | tf_op jit(solution)/shard_map/ppermute | solution.py:62
  109.1 16.3 %collective-permute-start.21 = (bf16[1024,256]{1,0:T(8,128)(2,1)S(1)}, bf16[1024,256]{1,0:T(8,128)(2,1)S(1)}, u32[]{:S(2)}, u32[]{:S(2)}) collective-permute-start(bf16[1024,256]{1,0:T(8,128)(2,1)S(1)} %collective-permute-done.19), channel_id=1, source_target_pairs={{4,0},{8,12},{5,1},{9,13},{6,2},{10,14},{7,3},{11,15},{20,16},{24,... | collective-permute-start | bytes 1572872 | tf_op jit(solution)/shard_map/ppermute | solution.py:62
  116.2 9.3 %collective-permute-start.23 = (f32[2,256]{1,0:T(2,128)S(1)}, f32[2,256]{1,0:T(2,128)S(1)}, u32[]{:S(2)}, u32[]{:S(2)}) collective-permute-start(f32[2,256]{1,0:T(2,128)S(1)} %bitcast_reduce_fusion.1), channel_id=1, source_target_pairs={{4,0},{8,12},{5,1},{9,13},{6,2},{10,14},{7,3},{11,15},{20,16},{24,... | collective-permute-start | bytes 6152 | tf_op jit(solution)/shard_map/ppermute | solution.py:179
  117.9 10.3 %collective-permute-start.24 = (bf16[512,256]{1,0:T(8,128)(2,1)S(1)}, bf16[512,256]{1,0:T(8,128)(2,1)S(1)}, u32[]{:S(2)}, u32[]{:S(2)}) collective-permute-start(bf16[512,256]{1,0:T(8,128)(2,1)S(1)} %collective-permute-done.20), channel_id=1, source_target_pairs={{4,0},{8,12},{5,1},{9,13},{6,2},{10,14},{7,3},{11,15},{20,16},{24,... | collective-permute-start | bytes 786440 | tf_op jit(solution)/shard_map/ppermute | solution.py:62
  128.8 3.6 %collective-permute-start.25 = (f32[2,32]{1,0:T(2,128)S(1)}, f32[2,32]{1,0:T(2,128)S(1)}, u32[]{:S(2)}, u32[]{:S(2)}) collective-permute-start(f32[2,32]{1,0:T(2,128)S(1)} %reduce_sum.29), channel_id=1, source_target_pairs={{0,2},{2,0},{1,3},{3,1},{4,6},{6,4},{5,7},{7,5},{8,10},{10,8},{9,1... | collective-permute-start | bytes 776 | tf_op jit(solution)/shard_map/ppermute | solution.py:185

commit v6 on v2

--- a/solution.py
+++ b/solution.py
@@ -111,7 +111,7 @@
     x["C1M"] = trade(either(guest(1, trade), y["C1M"]))
     y["C3M"] = across(own("C3", across))
     x["C2M"] = trade(either(guest(2, trade), y["C2M"]))
-    y["BE"] = across(across.ready(x["B"]))
+    y["BE"] = across(after(x["B"], y["C1M"]))
     x["C3M"] = trade(either(own("C3", trade), y["C3M"]))
     y["C1E"] = across(across.ready(x["AM"]))
     x["BE"] = trade(either(guest(3, trade), y["BE"]))

time: 133 us -> 133 us (level)
  no operation moved by 1% of the time
where the time goes in v6:
time: 133 us; the launch traced here: 132 us
  starting transfers between devices  76.8 us (58%)
  waiting for transfers between devices  33.3 us (25%)
  matrix products  14 us (11%)
  other arithmetic  4 us (3%)
  local copies, waits for them, and re-layouts  3.47 us (3%)
    ppermute x22, starting transfers between devices, __call__(): self.came.append(lax.ppermute(x, 'dp', pairs or self.pairs))  67.4 us
    ppermute x22, waiting for transfers between devices, __call__(): self.came.append(lax.ppermute(x, 'dp', pairs or self.pairs))  25.7 us
    dot_general x27, matrix products, dot(): return jnp.dot(a, b, preferred_element_type=jnp.float32)  14 us
    ppermute x1, waiting for transfers between devices, on_line(): lax.ppermute(column_scores(guest_acts.astype(jnp.float32), guest_grads, s...  5.52 us
    ppermute x1, starting transfers between devices, on_line(): guest_acts = lax.ppermute(coded, 'dp', TO_MIDDLE)  4.9 us
  transfers between devices with their start and end apart: 26, of which 9 were waited for; matrix products, arithmetic and copies ran while one was open for 15% of the time, Pallas kernels for 0%

profile of v6, /device:TPU:0, one launch (start us, length us, event | category | flops | bytes accessed | tf_op | source)
XLA Modules:
  0.0 132.2 jit_solution(11230179970085057073)
XLA Ops:
  0.0 3.0 %collective-permute-start = (bf16[1024,256]{1,0:T(8,128)(2,1)}, bf16[1024,256]{1,0:T(8,128)(2,1)S(1)}, u32[]{:S(2)}, u32[]{:S(2)}) collective-permute-start(bf16[1024,256]{1,0:T(8,128)(2,1)} %bitcast.124), channel_id=1, source_target_pairs={{0,4},{4,0},{8,12},{12,8},{1,5},{5,1},{9,13},{13,9},{2,6},{6,2},{1... | collective-permute-start | bytes 1572872 | tf_op jit(solution)/shard_map/ppermute | solution.py:62
  3.0 0.7 collective-permute-start.1
  3.7 1.9 %slice_bitcast_fusion = bf16[1024,256]{1,0:T(8,128)(2,1)} fusion(bf16[1,3584,256]{2,1,0:T(8,128)(2,1)} %param.8), kind=kLoop, calls=%fused_computation.87 | loop fusion | bytes 1048576 | tf_op jit(solution)/shard_map/slice | solution.py:103
  5.6 4.4 %collective-permute-start.4 = (bf16[1024,256]{1,0:T(8,128)(2,1)}, bf16[1024,256]{1,0:T(8,128)(2,1)S(1)}, u32[]{:S(2)}, u32[]{:S(2)}) collective-permute-start(bf16[1024,256]{1,0:T(8,128)(2,1)} %slice_bitcast_fusion), channel_id=1, source_target_pairs={{0,4},{4,0},{8,12},{12,8},{1,5},{5,1},{9,13},{13,9},{2,6},{6,2},{1... | collective-permute-start | bytes 1572872 | tf_op jit(solution)/shard_map/ppermute | solution.py:62
  10.0 0.7 fusion.143
  10.7 5.3 %collective-permute-done = bf16[1024,256]{1,0:T(8,128)(2,1)S(1)} collective-permute-done((bf16[1024,256]{1,0:T(8,128)(2,1)}, bf16[1024,256]{1,0:T(8,128)(2,1)S(1)}, u32[]{:S(2)}, u32[]{:S(2)}) %collective-permute-start) | collective-permute-done | bytes 524320 | tf_op jit(solution)/shard_map/ppermute | solution.py:62
  16.0 0.7 collective-permute-start.3
  16.7 1.3 slice_select_fusion.1
  17.9 6.9 %collective-permute-start.2 = (bf16[1024,256]{1,0:T(8,128)(2,1)S(1)}, bf16[1024,256]{1,0:T(8,128)(2,1)S(1)}, u32[]{:S(2)}, u32[]{:S(2)}) collective-permute-start(bf16[1024,256]{1,0:T(8,128)(2,1)S(1)} %slice_select_fusion.1), channel_id=1, source_target_pairs={{0,4},{4,0},{8,12},{12,8},{1,5},{5,1},{9,13},{13,9},{2,6},{6,2},{1... | collective-permute-start | bytes 1572872 | tf_op jit(solution)/shard_map/ppermute | solution.py:62
  24.9 1.7 %fusion.16 = f32[512,256]{1,0:T(8,128)S(1)} fusion(bf16[1024,256]{1,0:T(8,128)(2,1)S(1)} %collective-permute-done, bf16[1,512,4096]{2,1,0:T(8,128)(2,1)} %param.5, s32[]{:T(128)S(6)} %select_n.204), kind=kOutput, calls=%fused_computation.27 | convolution fusion | flops 268435456 | bytes 2097156 | tf_op jit(solution)/shard_map/dot_general | solution.py:36
  26.6 1.8 %convolution_add_fusion.3 = f32[512,256]{1,0:T(8,128)S(1)} fusion(f32[512,256]{1,0:T(8,128)S(1)} %fusion.16, bf16[512,4096]{1,0:T(8,128)(2,1)} %bitcast.123, s32[]{:T(128)S(6)} %select_n.203, bf16[1,1024,256]{2,1,0:T(8,128)(2,1)} %param.7), kind=kOutput, calls=%fused_computation.5 | convolution fusion | flops 268566528 | bytes 2621444 | tf_op jit(solution)/shard_map/dot_general | solution.py:36
  28.4 0.7 collective-permute-start.6
  29.2 1.7 %fusion.27 = f32[512,256]{1,0:T(8,128)S(1)} fusion(bf16[1024,256]{1,0:T(8,128)(2,1)S(1)} %collective-permute-done.4, bf16[1,512,14336]{2,1,0:T(8,128)(2,1)} %param.6, s32[]{:T(128)S(6)} %select_n.178), kind=kOutput, calls=%fused_computation.38 | convolution fusion | flops 268435456 | bytes 2097156 | tf_op jit(solution)/shard_map/dot_general | solution.py:36
  30.9 0.7 collective-permute-start.8
  31.7 8.8 %collective-permute-start.5 = (bf16[1024,256]{1,0:T(8,128)(2,1)S(1)}, bf16[1024,256]{1,0:T(8,128)(2,1)S(1)}, u32[]{:S(2)}, u32[]{:S(2)}) collective-permute-start(bf16[1024,256]{1,0:T(8,128)(2,1)S(1)} %slice_select_fusion), channel_id=1, source_target_pairs={{0,4},{4,0},{8,12},{12,8},{1,5},{5,1},{9,13},{13,9},{2,6},{6,2},{1... | collective-permute-start | bytes 1572872 | tf_op jit(solution)/shard_map/ppermute | solution.py:62
  40.5 1.1 constant_dynamic-slice_fusion.9
  41.7 6.4 %collective-permute-start.7 = (bf16[1024,256]{1,0:T(8,128)(2,1)S(1)}, bf16[1024,256]{1,0:T(8,128)(2,1)S(1)}, u32[]{:S(2)}, u32[]{:S(2)}) collective-permute-start(bf16[1024,256]{1,0:T(8,128)(2,1)S(1)} %maximum_select_fusion), channel_id=1, source_target_pairs={{0,4},{4,0},{8,12},{12,8},{1,5},{5,1},{9,13},{13,9},{2,6},{6,2},{1... | collective-permute-start | bytes 1572872 | tf_op jit(solution)/shard_map/ppermute | solution.py:62
  48.1 0.7 collective-permute-start.10
  48.9 0.5 fusion.25
  49.3 1.1 fusion
  50.5 0.7 collective-permute-start.12
  51.2 1.5 %collective-permute-done.5 = bf16[1024,256]{1,0:T(8,128)(2,1)S(1)} collective-permute-done((bf16[1024,256]{1,0:T(8,128)(2,1)S(1)}, bf16[1024,256]{1,0:T(8,128)(2,1)S(1)}, u32[]{:S(2)}, u32[]{:S(2)}) %collective-permute-start.5) | collective-permute-done | bytes 524320 | tf_op jit(solution)/shard_map/ppermute | solution.py:62
  53.0 10.2 %collective-permute-start.9 = (bf16[1024,256]{1,0:T(8,128)(2,1)S(1)}, bf16[1024,256]{1,0:T(8,128)(2,1)S(1)}, u32[]{:S(2)}, u32[]{:S(2)}) collective-permute-start(bf16[1024,256]{1,0:T(8,128)(2,1)S(1)} %maximum_select_fusion.1), channel_id=1, source_target_pairs={{0,4},{4,0},{8,12},{12,8},{1,5},{5,1},{9,13},{13,9},{2,6},{6,2},{1... | collective-permute-start | bytes 1572872 | tf_op jit(solution)/shard_map/ppermute | solution.py:62
  63.2 0.5 add_add_fusion.1
  63.9 6.7 %collective-permute-start.11 = (bf16[1024,256]{1,0:T(8,128)(2,1)S(1)}, bf16[1024,256]{1,0:T(8,128)(2,1)S(1)}, u32[]{:S(2)}, u32[]{:S(2)}) collective-permute-start(bf16[1024,256]{1,0:T(8,128)(2,1)S(1)} %maximum_select_fusion.2), channel_id=1, source_target_pairs={{0,4},{4,0},{8,12},{12,8},{1,5},{5,1},{9,13},{13,9},{2,6},{6,2},{1... | collective-permute-start | bytes 1572872 | tf_op jit(solution)/shard_map/ppermute | solution.py:62
  70.6 0.4 fusion.13
  71.0 0.5 fusion.3
  71.5 1.6 %collective-permute-start.14 = (f32[512,256]{1,0:T(8,128)S(1)}, f32[512,256]{1,0:T(8,128)S(1)}, u32[]{:S(2)}, u32[]{:S(2)}) collective-permute-start(f32[512,256]{1,0:T(8,128)S(1)} %fusion.3), channel_id=1, source_target_pairs={{0,2},{2,0},{1,3},{3,1},{4,6},{6,4},{5,7},{7,5},{8,10},{10,8},{9,1... | collective-permute-start | bytes 1572872 | tf_op jit(solution)/shard_map/ppermute | solution.py:128
  73.1 0.7 collective-permute-start.15
  74.0 0.4 fusion.21
  74.5 0.7 collective-permute-start.17
  75.2 4.5 %collective-permute-start.13 = (bf16[512,256]{1,0:T(8,128)(2,1)S(1)}, bf16[512,256]{1,0:T(8,128)(2,1)S(1)}, u32[]{:S(2)}, u32[]{:S(2)}) collective-permute-start(bf16[512,256]{1,0:T(8,128)(2,1)S(1)} %slice_select_fusion.2), channel_id=1, source_target_pairs={{0,4},{4,0},{8,12},{12,8},{1,5},{5,1},{9,13},{13,9},{2,6},{6,2},{1... | collective-permute-start | bytes 786440 | tf_op jit(solution)/shard_map/ppermute | solution.py:62
  79.8 0.2 fusion.91
  80.0 0.5 add_add_fusion
  80.5 0.2 convolution_add_fusion.8
  80.7 0.2 fusion.6
  81.3 5.2 %collective-permute-done.11 = bf16[1024,256]{1,0:T(8,128)(2,1)S(1)} collective-permute-done((bf16[1024,256]{1,0:T(8,128)(2,1)S(1)}, bf16[1024,256]{1,0:T(8,128)(2,1)S(1)}, u32[]{:S(2)}, u32[]{:S(2)}) %collective-permute-start.11) | collective-permute-done | bytes 524320 | tf_op jit(solution)/shard_map/ppermute | solution.py:62
  86.7 3.4 %collective-permute-start.16 = (bf16[1024,256]{1,0:T(8,128)(2,1)S(1)}, bf16[1024,256]{1,0:T(8,128)(2,1)S(1)}, u32[]{:S(2)}, u32[]{:S(2)}) collective-permute-start(bf16[1024,256]{1,0:T(8,128)(2,1)S(1)} %maximum_select_fusion.3), channel_id=1, source_target_pairs={{0,4},{4,0},{8,12},{12,8},{1,5},{5,1},{9,13},{13,9},{2,6},{6,2},{1... | collective-permute-start | bytes 1572872 | tf_op jit(solution)/shard_map/ppermute | solution.py:62
  90.0 0.7 collective-permute-start.19
  90.9 4.9 %collective-permute-start.21 = (s16[512,256]{1,0:T(8,128)(2,1)S(1)}, s16[512,256]{1,0:T(8,128)(2,1)S(1)}, u32[]{:S(2)}, u32[]{:S(2)}) collective-permute-start(s16[512,256]{1,0:T(8,128)(2,1)S(1)} %fusion.46), channel_id=1, source_target_pairs={{0,4},{12,8},{1,5},{13,9},{2,6},{14,10},{3,7},{15,11},{16,20},{28,... | collective-permute-start | bytes 786440 | tf_op jit(solution)/shard_map/ppermute | solution.py:133
  96.0 0.2 fusion.5
  96.3 0.3 fusion.49
  96.6 0.3 fusion.47
  96.9 0.5 fusion.7
  97.6 3.7 %collective-permute-start.18 = (bf16[1024,256]{1,0:T(8,128)(2,1)S(1)}, bf16[1024,256]{1,0:T(8,128)(2,1)S(1)}, u32[]{:S(2)}, u32[]{:S(2)}) collective-permute-start(bf16[1024,256]{1,0:T(8,128)(2,1)S(1)} %maximum_select_fusion.4), channel_id=1, source_target_pairs={{0,4},{4,0},{8,12},{12,8},{1,5},{5,1},{9,13},{13,9},{2,6},{6,2},{1... | collective-permute-start | bytes 1572872 | tf_op jit(solution)/shard_map/ppermute | solution.py:62
  101.3 2.0 %collective-permute-done.16 = bf16[1024,256]{1,0:T(8,128)(2,1)S(1)} collective-permute-done((bf16[1024,256]{1,0:T(8,128)(2,1)S(1)}, bf16[1024,256]{1,0:T(8,128)(2,1)S(1)}, u32[]{:S(2)}, u32[]{:S(2)}) %collective-permute-start.16) | collective-permute-done | bytes 524320 | tf_op jit(solution)/shard_map/ppermute | solution.py:62
  103.3 0.2 fusion.85
  103.5 0.2 fusion.4
  103.8 0.5 convolution_add_fusion.1
  104.2 1.3 collective-permute-start.20
  105.5 0.7 collective-permute-start.23
  106.2 9.3 %collective-permute-done.18 = bf16[1024,256]{1,0:T(8,128)(2,1)S(1)} collective-permute-done((bf16[1024,256]{1,0:T(8,128)(2,1)S(1)}, bf16[1024,256]{1,0:T(8,128)(2,1)S(1)}, u32[]{:S(2)}, u32[]{:S(2)}) %collective-permute-start.18) | collective-permute-done | bytes 524320 | tf_op jit(solution)/shard_map/ppermute | solution.py:62
  115.5 0.2 fusion.82
  115.8 0.2 convolution_add_fusion.5
  116.2 1.3 collective-permute-start.22
  117.5 0.4 convolution_add_fusion
  117.9 1.3 collective-permute-start.24
  119.2 5.5 %collective-permute-done.22 = f32[2,256]{1,0:T(2,128)S(1)} collective-permute-done((f32[2,256]{1,0:T(2,128)S(1)}, f32[2,256]{1,0:T(2,128)S(1)}, u32[]{:S(2)}, u32[]{:S(2)}) %collective-permute-start.22) | collective-permute-done | bytes 2080 | tf_op jit(solution)/shard_map/ppermute | solution.py:177
  124.8 0.4 fusion.9
  125.3 2.3 %collective-permute-done.24 = bf16[512,256]{1,0:T(8,128)(2,1)S(1)} collective-permute-done((bf16[512,256]{1,0:T(8,128)(2,1)S(1)}, bf16[512,256]{1,0:T(8,128)(2,1)S(1)}, u32[]{:S(2)}, u32[]{:S(2)}) %collective-permute-start.24) | collective-permute-done | bytes 262176 | tf_op jit(solution)/shard_map/ppermute | solution.py:62
  127.6 0.3 bitcast_reduce_fusion
  128.1 1.7 %collective-permute-start.25 = (f32[2,32]{1,0:T(2,128)S(1)}, f32[2,32]{1,0:T(2,128)S(1)}, u32[]{:S(2)}, u32[]{:S(2)}) collective-permute-start(f32[2,32]{1,0:T(2,128)S(1)} %reduce_sum.29), channel_id=1, source_target_pairs={{0,2},{2,0},{1,3},{3,1},{4,6},{6,4},{5,7},{7,5},{8,10},{10,8},{9,1... | collective-permute-start | bytes 776 | tf_op jit(solution)/shard_map/ppermute | solution.py:183
  129.7 1.9 %collective-permute-done.25 = f32[2,32]{1,0:T(2,128)S(1)} collective-permute-done((f32[2,32]{1,0:T(2,128)S(1)}, f32[2,32]{1,0:T(2,128)S(1)}, u32[]{:S(2)}, u32[]{:S(2)}) %collective-permute-start.25) | collective-permute-done | bytes 288 | tf_op jit(solution)/shard_map/ppermute | solution.py:183
  131.6 0.6 multiply_bitcast_fusion
  (53 shorter events, 2.7 us)
Async XLA Ops:
  0.0 28.4 %copy-start = (bf16[1,3584,256]{2,1,0:T(8,128)(2,1)S(1)}, bf16[1,3584,256]{2,1,0:T(8,128)(2,1)}, u32[]{:S(2)}) copy-start(bf16[1,3584,256]{2,1,0:T(8,128)(2,1)} %param.8) | copy-start | bytes 5505028
  0.0 16.0 %collective-permute-start = (bf16[1024,256]{1,0:T(8,128)(2,1)}, bf16[1024,256]{1,0:T(8,128)(2,1)S(1)}, u32[]{:S(2)}, u32[]{:S(2)}) collective-permute-start(bf16[1024,256]{1,0:T(8,128)(2,1)} %bitcast.124), channel_id=1, source_target_pairs={{0,4},{4,0},{8,12},{12,8},{1,5},{5,1},{9,13},{13,9},{2,6},{6,2},{1... | collective-permute-start | bytes 1572872 | tf_op jit(solution)/shard_map/ppermute | solution.py:62
  3.0 13.0 %collective-permute-start.1 = (bf16[1024,256]{1,0:T(8,128)(2,1)}, bf16[1024,256]{1,0:T(8,128)(2,1)S(1)}, u32[]{:S(2)}, u32[]{:S(2)}) collective-permute-start(bf16[1024,256]{1,0:T(8,128)(2,1)} %bitcast.125), channel_id=1, source_target_pairs={{4,8},{8,4},{5,9},{9,5},{6,10},{10,6},{7,11},{11,7},{20,24},{24,20... | collective-permute-start | bytes 1572872 | tf_op jit(solution)/shard_map/ppermute | solution.py:62
  5.6 22.8 %collective-permute-start.4 = (bf16[1024,256]{1,0:T(8,128)(2,1)}, bf16[1024,256]{1,0:T(8,128)(2,1)S(1)}, u32[]{:S(2)}, u32[]{:S(2)}) collective-permute-start(bf16[1024,256]{1,0:T(8,128)(2,1)} %slice_bitcast_fusion), channel_id=1, source_target_pairs={{0,4},{4,0},{8,12},{12,8},{1,5},{5,1},{9,13},{13,9},{2,6},{6,2},{1... | collective-permute-start | bytes 1572872 | tf_op jit(solution)/shard_map/ppermute | solution.py:62
  16.0 14.8 %collective-permute-start.3 = (bf16[1024,256]{1,0:T(8,128)(2,1)S(1)}, bf16[1024,256]{1,0:T(8,128)(2,1)S(1)}, u32[]{:S(2)}, u32[]{:S(2)}) collective-permute-start(bf16[1024,256]{1,0:T(8,128)(2,1)S(1)} %collective-permute-done), channel_id=1, source_target_pairs={{4,8},{8,4},{5,9},{9,5},{6,10},{10,6},{7,11},{11,7},{20,24},{24,20... | collective-permute-start | bytes 1572872 | tf_op jit(solution)/shard_map/ppermute | solution.py:62
  16.7 32.2 %copy-start.1 = (bf16[1,512,14336]{2,1,0:T(8,128)(2,1)S(1)}, bf16[1,512,14336]{2,1,0:T(8,128)(2,1)}, u32[]{:S(2)}) copy-start(bf16[1,512,14336]{2,1,0:T(8,128)(2,1)} %param.6) | copy-start | bytes 44040196
  17.9 22.5 %collective-permute-start.2 = (bf16[1024,256]{1,0:T(8,128)(2,1)S(1)}, bf16[1024,256]{1,0:T(8,128)(2,1)S(1)}, u32[]{:S(2)}, u32[]{:S(2)}) collective-permute-start(bf16[1024,256]{1,0:T(8,128)(2,1)S(1)} %slice_select_fusion.1), channel_id=1, source_target_pairs={{0,4},{4,0},{8,12},{12,8},{1,5},{5,1},{9,13},{13,9},{2,6},{6,2},{1... | collective-permute-start | bytes 1572872 | tf_op jit(solution)/shard_map/ppermute | solution.py:62
  28.4 13.1 %collective-permute-start.6 = (bf16[1024,256]{1,0:T(8,128)(2,1)S(1)}, bf16[1024,256]{1,0:T(8,128)(2,1)S(1)}, u32[]{:S(2)}, u32[]{:S(2)}) collective-permute-start(bf16[1024,256]{1,0:T(8,128)(2,1)S(1)} %slice.121), channel_id=1, source_target_pairs={{4,8},{8,4},{5,9},{9,5},{6,10},{10,6},{7,11},{11,7},{20,24},{24,20... | collective-permute-start | bytes 1572872 | tf_op jit(solution)/shard_map/ppermute | solution.py:62
  30.9 19.6 %collective-permute-start.8 = (bf16[1024,256]{1,0:T(8,128)(2,1)S(1)}, bf16[1024,256]{1,0:T(8,128)(2,1)S(1)}, u32[]{:S(2)}, u32[]{:S(2)}) collective-permute-start(bf16[1024,256]{1,0:T(8,128)(2,1)S(1)} %slice.122), channel_id=1, source_target_pairs={{4,8},{8,4},{5,9},{9,5},{6,10},{10,6},{7,11},{11,7},{20,24},{24,20... | collective-permute-start | bytes 1572872 | tf_op jit(solution)/shard_map/ppermute | solution.py:62
  31.7 21.1 %collective-permute-start.5 = (bf16[1024,256]{1,0:T(8,128)(2,1)S(1)}, bf16[1024,256]{1,0:T(8,128)(2,1)S(1)}, u32[]{:S(2)}, u32[]{:S(2)}) collective-permute-start(bf16[1024,256]{1,0:T(8,128)(2,1)S(1)} %slice_select_fusion), channel_id=1, source_target_pairs={{0,4},{4,0},{8,12},{12,8},{1,5},{5,1},{9,13},{13,9},{2,6},{6,2},{1... | collective-permute-start | bytes 1572872 | tf_op jit(solution)/shard_map/ppermute | solution.py:62
  41.7 21.9 %collective-permute-start.7 = (bf16[1024,256]{1,0:T(8,128)(2,1)S(1)}, bf16[1024,256]{1,0:T(8,128)(2,1)S(1)}, u32[]{:S(2)}, u32[]{:S(2)}) collective-permute-start(bf16[1024,256]{1,0:T(8,128)(2,1)S(1)} %maximum_select_fusion), channel_id=1, source_target_pairs={{0,4},{4,0},{8,12},{12,8},{1,5},{5,1},{9,13},{13,9},{2,6},{6,2},{1... | collective-permute-start | bytes 1572872 | tf_op jit(solution)/shard_map/ppermute | solution.py:62
  48.1 15.6 %collective-permute-start.10 = (bf16[1024,256]{1,0:T(8,128)(2,1)S(1)}, bf16[1024,256]{1,0:T(8,128)(2,1)S(1)}, u32[]{:S(2)}, u32[]{:S(2)}) collective-permute-start(bf16[1024,256]{1,0:T(8,128)(2,1)S(1)} %slice.135), channel_id=1, source_target_pairs={{4,8},{8,4},{5,9},{9,5},{6,10},{10,6},{7,11},{11,7},{20,24},{24,20... | collective-permute-start | bytes 1572872 | tf_op jit(solution)/shard_map/ppermute | solution.py:62
  50.5 23.9 %collective-permute-start.12 = (bf16[512,256]{1,0:T(8,128)(2,1)S(1)}, bf16[512,256]{1,0:T(8,128)(2,1)S(1)}, u32[]{:S(2)}, u32[]{:S(2)}) collective-permute-start(bf16[512,256]{1,0:T(8,128)(2,1)S(1)} %slice.137), channel_id=1, source_target_pairs={{4,8},{8,4},{5,9},{9,5},{6,10},{10,6},{7,11},{11,7},{20,24},{24,20... | collective-permute-start | bytes 786440 | tf_op jit(solution)/shard_map/ppermute | solution.py:62
  52.8 17.8 %copy-start.2 = (bf16[1,512,4096]{2,1,0:T(8,128)(2,1)S(1)}, bf16[1,512,4096]{2,1,0:T(8,128)(2,1)}, u32[]{:S(2)}) copy-start(bf16[1,512,4096]{2,1,0:T(8,128)(2,1)} %param.5) | copy-start | bytes 12582916
  53.0 22.2 %collective-permute-start.9 = (bf16[1024,256]{1,0:T(8,128)(2,1)S(1)}, bf16[1024,256]{1,0:T(8,128)(2,1)S(1)}, u32[]{:S(2)}, u32[]{:S(2)}) collective-permute-start(bf16[1024,256]{1,0:T(8,128)(2,1)S(1)} %maximum_select_fusion.1), channel_id=1, source_target_pairs={{0,4},{4,0},{8,12},{12,8},{1,5},{5,1},{9,13},{13,9},{2,6},{6,2},{1... | collective-permute-start | bytes 1572872 | tf_op jit(solution)/shard_map/ppermute | solution.py:62
  63.9 22.5 %collective-permute-start.11 = (bf16[1024,256]{1,0:T(8,128)(2,1)S(1)}, bf16[1024,256]{1,0:T(8,128)(2,1)S(1)}, u32[]{:S(2)}, u32[]{:S(2)}) collective-permute-start(bf16[1024,256]{1,0:T(8,128)(2,1)S(1)} %maximum_select_fusion.2), channel_id=1, source_target_pairs={{0,4},{4,0},{8,12},{12,8},{1,5},{5,1},{9,13},{13,9},{2,6},{6,2},{1... | collective-permute-start | bytes 1572872 | tf_op jit(solution)/shard_map/ppermute | solution.py:62
  71.5 9.6 %collective-permute-start.14 = (f32[512,256]{1,0:T(8,128)S(1)}, f32[512,256]{1,0:T(8,128)S(1)}, u32[]{:S(2)}, u32[]{:S(2)}) collective-permute-start(f32[512,256]{1,0:T(8,128)S(1)} %fusion.3), channel_id=1, source_target_pairs={{0,2},{2,0},{1,3},{3,1},{4,6},{6,4},{5,7},{7,5},{8,10},{10,8},{9,1... | collective-permute-start | bytes 1572872 | tf_op jit(solution)/shard_map/ppermute | solution.py:128
  73.1 13.4 %collective-permute-start.15 = (bf16[1024,256]{1,0:T(8,128)(2,1)S(1)}, bf16[1024,256]{1,0:T(8,128)(2,1)S(1)}, u32[]{:S(2)}, u32[]{:S(2)}) collective-permute-start(bf16[1024,256]{1,0:T(8,128)(2,1)S(1)} %collective-permute-done.4), channel_id=1, source_target_pairs={{4,8},{8,4},{5,9},{9,5},{6,10},{10,6},{7,11},{11,7},{20,24},{24,20... | collective-permute-start | bytes 1572872 | tf_op jit(solution)/shard_map/ppermute | solution.py:62
  74.5 23.0 %collective-permute-start.17 = (bf16[1024,256]{1,0:T(8,128)(2,1)S(1)}, bf16[1024,256]{1,0:T(8,128)(2,1)S(1)}, u32[]{:S(2)}, u32[]{:S(2)}) collective-permute-start(bf16[1024,256]{1,0:T(8,128)(2,1)S(1)} %collective-permute-done.2), channel_id=1, source_target_pairs={{4,8},{8,4},{5,9},{9,5},{6,10},{10,6},{7,11},{11,7},{20,24},{24,20... | collective-permute-start | bytes 1572872 | tf_op jit(solution)/shard_map/ppermute | solution.py:62
  75.2 21.0 %collective-permute-start.13 = (bf16[512,256]{1,0:T(8,128)(2,1)S(1)}, bf16[512,256]{1,0:T(8,128)(2,1)S(1)}, u32[]{:S(2)}, u32[]{:S(2)}) collective-permute-start(bf16[512,256]{1,0:T(8,128)(2,1)S(1)} %slice_select_fusion.2), channel_id=1, source_target_pairs={{0,4},{4,0},{8,12},{12,8},{1,5},{5,1},{9,13},{13,9},{2,6},{6,2},{1... | collective-permute-start | bytes 786440 | tf_op jit(solution)/shard_map/ppermute | solution.py:62
  86.7 16.6 %collective-permute-start.16 = (bf16[1024,256]{1,0:T(8,128)(2,1)S(1)}, bf16[1024,256]{1,0:T(8,128)(2,1)S(1)}, u32[]{:S(2)}, u32[]{:S(2)}) collective-permute-start(bf16[1024,256]{1,0:T(8,128)(2,1)S(1)} %maximum_select_fusion.3), channel_id=1, source_target_pairs={{0,4},{4,0},{8,12},{12,8},{1,5},{5,1},{9,13},{13,9},{2,6},{6,2},{1... | collective-permute-start | bytes 1572872 | tf_op jit(solution)/shard_map/ppermute | solution.py:62
  90.0 14.2 %collective-permute-start.19 = (bf16[1024,256]{1,0:T(8,128)(2,1)S(1)}, bf16[1024,256]{1,0:T(8,128)(2,1)S(1)}, u32[]{:S(2)}, u32[]{:S(2)}) collective-permute-start(bf16[1024,256]{1,0:T(8,128)(2,1)S(1)} %collective-permute-done.5), channel_id=1, source_target_pairs={{4,8},{8,4},{5,9},{9,5},{6,10},{10,6},{7,11},{11,7},{20,24},{24,20... | collective-permute-start | bytes 1572872 | tf_op jit(solution)/shard_map/ppermute | solution.py:62
  90.9 25.1 %collective-permute-start.21 = (s16[512,256]{1,0:T(8,128)(2,1)S(1)}, s16[512,256]{1,0:T(8,128)(2,1)S(1)}, u32[]{:S(2)}, u32[]{:S(2)}) collective-permute-start(s16[512,256]{1,0:T(8,128)(2,1)S(1)} %fusion.46), channel_id=1, source_target_pairs={{0,4},{12,8},{1,5},{13,9},{2,6},{14,10},{3,7},{15,11},{16,20},{28,... | collective-permute-start | bytes 786440 | tf_op jit(solution)/shard_map/ppermute | solution.py:133
  97.6 17.9 %collective-permute-start.18 = (bf16[1024,256]{1,0:T(8,128)(2,1)S(1)}, bf16[1024,256]{1,0:T(8,128)(2,1)S(1)}, u32[]{:S(2)}, u32[]{:S(2)}) collective-permute-start(bf16[1024,256]{1,0:T(8,128)(2,1)S(1)} %maximum_select_fusion.4), channel_id=1, source_target_pairs={{0,4},{4,0},{8,12},{12,8},{1,5},{5,1},{9,13},{13,9},{2,6},{6,2},{1... | collective-permute-start | bytes 1572872 | tf_op jit(solution)/shard_map/ppermute | solution.py:62
  104.2 20.5 %collective-permute-start.20 = (bf16[1024,256]{1,0:T(8,128)(2,1)S(1)}, bf16[1024,256]{1,0:T(8,128)(2,1)S(1)}, u32[]{:S(2)}, u32[]{:S(2)}) collective-permute-start(bf16[1024,256]{1,0:T(8,128)(2,1)S(1)} %collective-permute-done.19), channel_id=1, source_target_pairs={{4,0},{8,12},{5,1},{9,13},{6,2},{10,14},{7,3},{11,15},{20,16},{24,... | collective-permute-start | bytes 1572872 | tf_op jit(solution)/shard_map/ppermute | solution.py:62
  105.5 12.4 %collective-permute-start.23 = (bf16[512,256]{1,0:T(8,128)(2,1)S(1)}, bf16[512,256]{1,0:T(8,128)(2,1)S(1)}, u32[]{:S(2)}, u32[]{:S(2)}) collective-permute-start(bf16[512,256]{1,0:T(8,128)(2,1)S(1)} %collective-permute-done.13), channel_id=1, source_target_pairs={{4,8},{8,4},{5,9},{9,5},{6,10},{10,6},{7,11},{11,7},{20,24},{24,20... | collective-permute-start | bytes 786440 | tf_op jit(solution)/shard_map/ppermute | solution.py:62
  116.2 8.6 %collective-permute-start.22 = (f32[2,256]{1,0:T(2,128)S(1)}, f32[2,256]{1,0:T(2,128)S(1)}, u32[]{:S(2)}, u32[]{:S(2)}) collective-permute-start(f32[2,256]{1,0:T(2,128)S(1)} %bitcast_reduce_fusion.1), channel_id=1, source_target_pairs={{4,0},{8,12},{5,1},{9,13},{6,2},{10,14},{7,3},{11,15},{20,16},{24,... | collective-permute-start | bytes 6152 | tf_op jit(solution)/shard_map/ppermute | solution.py:177
  117.9 9.6 %collective-permute-start.24 = (bf16[512,256]{1,0:T(8,128)(2,1)S(1)}, bf16[512,256]{1,0:T(8,128)(2,1)S(1)}, u32[]{:S(2)}, u32[]{:S(2)}) collective-permute-start(bf16[512,256]{1,0:T(8,128)(2,1)S(1)} %collective-permute-done.23), channel_id=1, source_target_pairs={{4,0},{8,12},{5,1},{9,13},{6,2},{10,14},{7,3},{11,15},{20,16},{24,... | collective-permute-start | bytes 786440 | tf_op jit(solution)/shard_map/ppermute | solution.py:62
  128.1 3.6 %collective-permute-start.25 = (f32[2,32]{1,0:T(2,128)S(1)}, f32[2,32]{1,0:T(2,128)S(1)}, u32[]{:S(2)}, u32[]{:S(2)}) collective-permute-start(f32[2,32]{1,0:T(2,128)S(1)} %reduce_sum.29), channel_id=1, source_target_pairs={{0,2},{2,0},{1,3},{3,1},{4,6},{6,4},{5,7},{7,5},{8,10},{10,8},{9,1... | collective-permute-start | bytes 776 | tf_op jit(solution)/shard_map/ppermute | solution.py:183
